TPU v7x, 512 devices: a whole 4x4x16 slice. The times are simulated.
512 devices in a mesh: row: 16 (over z), col: 32 (over y, x, core).
Axes of the slice: x: 4, y: 4, z: 16, core: 2. Of those that a mesh axis runs over, the one named last changes fastest.
Arguments:
- kernel: float32 [8, 16, 128, 4, 32, 128], P(None, 'row', None, None, 'col'), may hold values from -6 to 6, as said below
Outputs:
- updated: float32 [8, 16, 128, 4, 32, 128], P(None, 'row', None, None, 'col')
Inputs may be any that keep to these rules, and one draw needn't show every extreme that they name: kernel is symmetric as a matrix: entry (i, j) equals entry (j, i) up to rounding.
All inputs are finite; a program needn't handle non-finite values.
Results may differ from a plain program's by a relative error of at most 0.0003.
Values sent between devices are 32-bit elements; how exact they have to be, the bound alone decides.
No kernel may reach another device: no remote copies, remote signals or barrier semaphores. Data moves between devices by JAX's collectives and lax.ppermute only.
A program may use at most 64 MiB of HBM per device.

v0:
```python
import jax
import jax.numpy as jnp
from jax import lax
from jax.sharding import PartitionSpec as P


def broadcast(value, axis, source):
    kept = jnp.where(lax.axis_index(axis) == source, value, 0).astype(value.dtype)
    return lax.psum(kept, axis)


def mult(left, right):
    return jnp.dot(left, right, precision=lax.Precision.HIGHEST, preferred_element_type=jnp.float32)


def factor_unit(square):
    count = square.shape[0]
    index_line = jnp.arange(count)

    def step(k, matrix):
        column = matrix[:, k] / matrix[k, k]
        below = index_line > k
        low_col = jnp.where(below, column, 0.0)
        up_row = jnp.where(below, matrix[k, :], 0.0)
        matrix = matrix - low_col[:, None] * up_row[None, :]
        return jnp.where(below[:, None] & (index_line == k)[None, :], low_col[:, None], matrix)

    matrix = lax.fori_loop(0, count, step, square)
    lower_factor = jnp.tril(matrix, -1) + jnp.eye(count, dtype=square.dtype)
    return (lower_factor, jnp.triu(matrix))


def block_factor(leading):
    sign_diag = jnp.where(jnp.diagonal(leading) >= 0, -1.0, 1.0).astype(leading.dtype)
    lower_factor, upper_factor = factor_unit(leading - jnp.diag(sign_diag))
    right_side = jax.scipy.linalg.solve_triangular(
        lower_factor, (upper_factor * sign_diag[None, :]).T, lower=True, unit_diagonal=True
    )
    return (sign_diag, upper_factor, -right_side.T)


def solve_pass(block, factor):
    return jax.scipy.linalg.solve_triangular(factor, block.T, lower=True).T


def reflect_rows(q_rows, block_ids, sign_diag, upper_factor, width):
    first_rows = jnp.repeat(block_ids == 1, width)
    offset_rows = jnp.tile(jnp.diag(sign_diag), (block_ids.shape[0], 1))
    shifted = q_rows - jnp.where(first_rows[:, None], offset_rows, 0.0)
    return jax.scipy.linalg.solve_triangular(upper_factor.T, shifted.T, lower=True).T


def body(kernel):
    row_blocks, _, block_width, col_blocks, _, _ = kernel.shape
    local_block = kernel.reshape(row_blocks * block_width, col_blocks * block_width)
    row_count = lax.axis_size("row")
    col_count = lax.axis_size("col")
    fold_count = col_count // row_count
    row_index = lax.axis_index("row")
    col_index = lax.axis_index("col")
    block_ids = jnp.arange(row_blocks, dtype=jnp.int32) * row_count + row_index
    panel_cols = broadcast(local_block[:, :block_width], "col", 0)
    keep_rows = jnp.repeat(block_ids != 0, block_width)
    panel_cols = jnp.where(keep_rows[:, None], panel_cols, 0.0)
    gram = mult(panel_cols.T, panel_cols)
    owner_row = col_index % row_count
    pick_slot = col_index // row_count

    def select_columns(held):
        grouped = held.reshape(col_blocks, fold_count, block_width, held.shape[1])
        chosen = lax.dynamic_index_in_dim(grouped, pick_slot, 1, keepdims=False)
        return chosen.reshape(col_blocks * block_width, held.shape[1])

    first_factor = jnp.linalg.cholesky(lax.psum(gram, "row"))
    orthonormal = solve_pass(panel_cols, first_factor)
    leading = broadcast(orthonormal[:block_width], "row", 1)
    sign_diag, upper_factor, coupling = block_factor(leading)
    vec_rows = reflect_rows(orthonormal, block_ids, sign_diag, upper_factor, block_width)
    vec_cols = select_columns(broadcast(vec_rows, "row", owner_row))
    projected = mult(lax.psum(mult(local_block, vec_cols), "col"), coupling)
    middle_term = lax.psum(mult(vec_rows.T, projected), "row")
    weight_rows = projected - 0.5 * mult(vec_rows, mult(coupling.T, middle_term))
    weight_cols = select_columns(broadcast(weight_rows, "row", owner_row))
    updated = local_block - mult(
        jnp.concatenate([vec_rows, weight_rows], 1), jnp.concatenate([weight_cols, vec_cols], 1).T
    )
    return updated.reshape(kernel.shape)


def solution(mesh):
    return jax.shard_map(
        body,
        mesh=mesh,
        in_specs=(P(None, "row", None, None, "col", None),),
        out_specs=P(None, "row", None, None, "col", None),
        check_vma=False,
    )
```

profile of v0, /device:TPU:1, one launch (start us, length us, event | category | flops | bytes accessed | tf_op | source)
XLA Modules:
  0.0 1197.0 jit_solution(10360617593802550612)
XLA Ops:
  6.5 1.8 copy.29
  8.3 0.9 slice_select_fusion
  9.4 140.6 %all-reduce.8.cloned.1.call-done = f32[1024,128]{1,0:T(8,128)} async-done(((f32[1024,128]{1,0:T(8,128)}), f32[1024,128]{1,0:T(8,128)}) %all-reduce.8.cloned.1.call-update) | async-done | bytes 524304 | tf_op jit(solution)/shard_map/psum | solution.py:9
  150.1 3.1 fusion.16
  153.3 122.3 %all-reduce.10.cloned.1.call-done = f32[128,128]{0,1:T(8,128)} async-done(((f32[128,128]{0,1:T(8,128)}), f32[128,128]{0,1:T(8,128)}) %all-reduce.10.cloned.1.call-update) | async-done | bytes 65552 | tf_op jit(solution)/shard_map/psum | solution.py:74
  275.6 0.9 copy.14
  276.5 0.9 fusion.27
  277.4 11.7 cholesky.21
  289.8 0.7 fusion.22
  290.4 9.8 custom-call.14
  300.3 1.7 convolution_bitcast_fusion.1
  302.8 129.1 %all-reduce.12.cloned.1.call-done = f32[128,128]{1,0:T(8,128)} async-done(((f32[128,128]{1,0:T(8,128)}), f32[128,128]{1,0:T(8,128)}) %all-reduce.12.cloned.1.call-update) | async-done | bytes 65552 | tf_op jit(solution)/shard_map/psum | solution.py:9
  431.9 1.9 gather_fusion
  433.9 0.9 fusion.35
  434.9 192.8 %while.15 = (s32[]{:T(128)}, f32[128,128]{0,1:T(8,128)S(1)}, s32[]{:T(128)}) while((s32[]{:T(128)}, f32[128,128]{0,1:T(8,128)S(1)}, s32[]{:T(128)}) %tuple.42), condition=%wide.region_6.8_spmd.clone.clone, body=%wide.region_5.7_spmd.clone.clone.sunk | while | flops 66434 | bytes 267849 | solution.py:28
  437.0 0.7 fusion.57
  628.0 9.8 custom-call.15
  638.9 0.9 broadcast_select_fusion.1
  639.9 134.2 %all-reduce.14.cloned.1.call-done = f32[4,2,128,128]{3,2,1,0:T(8,128)} async-done(((f32[4,2,128,128]{3,2,1,0:T(8,128)}), f32[4,2,128,128]{3,2,1,0:T(8,128)}) %all-reduce.14.cloned.1.call-update) | async-done | bytes 524304 | tf_op jit(solution)/shard_map/psum | solution.py:9
  774.1 1.0 constant_dynamic-slice_fusion.3
  775.1 3.1 convolution_bitcast_fusion
  778.4 9.8 custom-call.10
  788.5 130.3 %all-reduce.16.cloned.1.call-done = f32[1024,128]{0,1:T(8,128)} async-done(((f32[1024,128]{0,1:T(8,128)}), f32[1024,128]{0,1:T(8,128)}) %all-reduce.16.cloned.1.call-update) | async-done | bytes 524304 | tf_op jit(solution)/shard_map/psum | solution.py:80
  918.8 2.0 fusion.42
  920.8 1.3 fusion.43
  922.4 122.1 %all-reduce.18.cloned.1.call-done = f32[128,128]{1,0:T(8,128)} async-done(((f32[128,128]{1,0:T(8,128)}), f32[128,128]{1,0:T(8,128)}) %all-reduce.18.cloned.1.call-update) | async-done | bytes 65552 | tf_op jit(solution)/shard_map/psum | solution.py:81
  1044.5 1.1 fusion.44
  1045.6 2.0 broadcast_select_fusion
  1047.6 134.3 %all-reduce.20.cloned.1.call-done = f32[4,2,128,128]{3,2,1,0:T(8,128)} async-done(((f32[4,2,128,128]{3,2,1,0:T(8,128)}), f32[4,2,128,128]{3,2,1,0:T(8,128)}) %all-reduce.20.cloned.1.call-update) | async-done | bytes 524304 | tf_op jit(solution)/shard_map/psum | solution.py:9
  1181.9 1.0 constant_dynamic-slice_fusion.2
  1182.9 4.4 convolution_subtract_fusion
  1187.3 2.9 reshape.102
  (804 shorter events, 189.6 us)
Async XLA Ops:
  6.5 143.5 %all-reduce.8.cloned.1.call-start = ((), (), s32[]{:S(2)}) async-start(), calls=%async_computation | async-start | bytes 1048576 | tf_op jit(solution)/shard_map/psum | solution.py:9
  9.2 266.4 %all-reduce.10.cloned.1.call-start = ((), (), s32[]{:S(2)}) async-start(), calls=%async_computation.1 | async-start | bytes 131072 | tf_op jit(solution)/shard_map/psum | solution.py:74
  153.2 278.7 %all-reduce.12.cloned.1.call-start = ((), (), s32[]{:S(2)}) async-start(), calls=%async_computation.2 | async-start | bytes 131072 | tf_op jit(solution)/shard_map/psum | solution.py:9
  302.6 471.5 %all-reduce.14.cloned.1.call-start = ((), (), s32[]{:S(2)}) async-start(), calls=%async_computation.3 | async-start | bytes 1048576 | tf_op jit(solution)/shard_map/psum | solution.py:9
  638.0 137.0 %copy-start = (f32[8,1,128,4,1,128]{5,4,3,2,1,0:T(1,128)S(1)}, f32[8,1,128,4,1,128]{5,4,3,2,1,0:T(1,128)}, u32[]{:S(2)}) copy-start(f32[8,1,128,4,1,128]{5,4,3,2,1,0:T(1,128)} %param.5) | copy-start | bytes 6291460
  638.9 139.3 %copy-start.1 = (f32[128,1024]{0,1:T(8,128)}, f32[128,1024]{0,1:T(8,128)S(1)}, u32[]{:S(2)}) copy-start(f32[128,1024]{0,1:T(8,128)S(1)} %copy.19) | copy-start | bytes 1572868
  639.8 279.0 %all-reduce.16.cloned.1.call-start = ((), (), s32[]{:S(2)}) async-start(), calls=%async_computation.4 | async-start | bytes 1048576 | tf_op jit(solution)/shard_map/psum | solution.py:80
  778.2 266.3 %all-reduce.18.cloned.1.call-start = ((), (), s32[]{:S(2)}) async-start(), calls=%async_computation.5 | async-start | bytes 131072 | tf_op jit(solution)/shard_map/psum | solution.py:81
  922.1 259.8 %all-reduce.20.cloned.1.call-start = ((), (), s32[]{:S(2)}) async-start(), calls=%async_computation.6 | async-start | bytes 1048576 | tf_op jit(solution)/shard_map/psum | solution.py:9
Sparse Core Ops, SparseCore 0:
  10.5 139.4 all-reduce.7
  153.3 122.2 all-reduce.9
  302.7 129.1 all-reduce.11
  639.9 134.1 all-reduce.13
  778.4 140.3 all-reduce.15
  922.3 122.2 all-reduce.17
  1047.8 134.1 all-reduce.19
where the time goes:
time: 1210 us; the launch traced here: 1200 us
  waiting for transfers between devices  913 us (75%)
  other arithmetic  147 us (12%)
  local copies, waits for them, and re-layouts  96.6 us (8%)
  matrix products  19.6 us (2%)
  between operations  13.7 us (1%)
    psum x4, waiting for transfers between devices, broadcast(): return lax.psum(kept, axis)  538 us
    psum x1, waiting for transfers between devices, body(): projected = mult(lax.psum(mult(local_block, vec_cols), 'col'), coupling)  130 us
    psum x1, waiting for transfers between devices, body(): first_factor = jnp.linalg.cholesky(lax.psum(gram, 'row'))  122 us
    psum x1, waiting for transfers between devices, body(): middle_term = lax.psum(mult(vec_rows.T, projected), 'row')  122 us
    broadcast_in_dim x128, other arithmetic, step(): jnp.where(below[:, None] & (index_line == k)[None, :], low_col[:, None],...  83.7 us
    dynamic_slice x128, local copies, waits for them, and re-layouts, step(): column = matrix[:, k] / matrix[k, k]  75.3 us
  transfers between devices with their start and end apart: 7, of which 7 were waited for; matrix products, arithmetic and copies ran while one was open for 1% of the time, Pallas kernels for 0%

commit v1 on v0

v1 whole, which is shorter than its diff:
```python
import jax
import jax.numpy as jnp
from jax import lax
from jax.experimental import pallas as pl
from jax.experimental.pallas import tpu as pltpu
from jax.sharding import PartitionSpec as P

NB = 128
SUB = 8


def mult(left, right, left_dim=1, right_dim=0):
    return lax.dot_general(
        left,
        right,
        (((left_dim,), (right_dim,)), ((), ())),
        precision=lax.Precision.HIGHEST,
        preferred_element_type=jnp.float32,
    )


def lane(block, k):
    return jnp.broadcast_to(block[:, k : k + 1], (SUB, NB))


def row(block, s):
    return jnp.broadcast_to(block[s : s + 1, :], (SUB, NB))


def lane_ids():
    sub_id = lax.broadcasted_iota(jnp.int32, (SUB, NB), 0)
    lane_id = lax.broadcasted_iota(jnp.int32, (SUB, NB), 1)
    return sub_id, lane_id


def cholesky_kernel(gram_ref, lead_ref, inv_ref, sign_ref, shift_ref):
    count = NB // SUB
    sub_id, lane_id = lane_ids()
    eye = [jnp.where(lane_id == sub_id + SUB * i, 1.0, 0.0) for i in range(count)]
    left = [gram_ref[SUB * i : SUB * i + SUB, :] for i in range(count)]
    right = list(eye)
    for k in range(NB):
        b, s = divmod(k, SUB)
        pivot_left, pivot_right = row(left[b], s), row(right[b], s)
        scale = 1.0 / lane(pivot_left, k)
        pivot_left, pivot_right = pivot_left * scale, pivot_right * scale
        for i in range(b, count):
            factor = lane(left[i], k)
            if i == b:
                factor = jnp.where(sub_id > s, factor, 0.0)
            left[i] = left[i] - factor * pivot_left
            right[i] = right[i] - factor * pivot_right
    for i in range(count):
        diagonal = jnp.sum(left[i] * eye[i], axis=1, keepdims=True)
        inv_ref[SUB * i : SUB * i + SUB, :] = right[i] * lax.rsqrt(diagonal)
    inverse = inv_ref[...]
    lead = lead_ref[...]
    sign = jnp.where(jnp.sum(lead * inverse, axis=1, keepdims=True) >= 0, -1.0, 1.0)
    for i in range(count):
        sign_ref[SUB * i : SUB * i + SUB, :] = eye[i] * sign[SUB * i : SUB * i + SUB]
    shift_ref[...] = sign * mult(lead, inverse, 1, 1)


def invert_kernel(shift_ref, out_ref):
    count = NB // SUB
    sub_id, lane_id = lane_ids()
    held = [
        jnp.where(lane_id == sub_id + SUB * i, 1.0, 0.0) - shift_ref[SUB * i : SUB * i + SUB, :] for i in range(count)
    ]
    for k in range(NB):
        b, s = divmod(k, SUB)
        pivot = row(held[b], s)
        scale = 1.0 / lane(pivot, k)
        scaled = pivot * scale
        here = lane_id == k
        other = jnp.where(here, 1.0 + scale, scaled)
        own = jnp.where(here, scale, scaled)
        for i in range(count):
            new = held[i] - lane(held[i], k) * other
            if i == b:
                new = jnp.where(sub_id == s, own, new)
            held[i] = new
    for i in range(count):
        out_ref[SUB * i : SUB * i + SUB, :] = held[i]


SQUARE = jax.ShapeDtypeStruct((NB, NB), jnp.float32)


def cholesky_parts(gram, lead):
    return pl.pallas_call(
        cholesky_kernel,
        out_shape=(SQUARE, SQUARE, SQUARE),
        name="cholesky_parts",
        cost_estimate=pl.CostEstimate(flops=40_000_000, bytes_accessed=400_000, transcendentals=0),
    )(gram, lead)


def invert(shift):
    return pl.pallas_call(
        invert_kernel,
        out_shape=SQUARE,
        name="invert",
        cost_estimate=pl.CostEstimate(flops=40_000_000, bytes_accessed=400_000, transcendentals=0),
    )(shift)


def exchange(pieces, axis):
    return lax.all_to_all(pieces, axis, 0, 0)


def gather(piece, axis):
    count = lax.axis_size(axis)
    return exchange(jnp.broadcast_to(piece[None], (count,) + piece.shape), axis)


def body(kernel):
    row_blocks, _, _, col_blocks, _, _ = kernel.shape
    rows, cols = row_blocks * NB, col_blocks * NB
    row_count, col_count = lax.axis_size("row"), lax.axis_size("col")
    fold = col_count // row_count
    row_index, col_index = lax.axis_index("row"), lax.axis_index("col")
    local = kernel.reshape(rows, cols)
    by_block = kernel.reshape(row_blocks, NB, col_blocks, NB)

    own_panel = jnp.where(
        (row_index == 0) & (jnp.arange(row_blocks) == 0)[:, None, None], 0.0, by_block[:, :, 0, :]
    ).reshape(rows, NB)
    own_gram = mult(own_panel, own_panel, 0, 0)
    own_lead = jnp.where(row_index == 1, own_panel[:NB], 0.0)

    step = NB // col_count
    pair = jnp.concatenate([own_gram.reshape(col_count, step, NB), own_lead.reshape(col_count, step, NB)], 1)
    piece = exchange(pair, "col")[0]
    piece = jnp.sum(gather(piece, "row"), 0)
    whole = gather(piece, "col")
    gram = whole[:, :step].reshape(NB, NB)
    lead = whole[:, step:].reshape(NB, NB)

    share = exchange(own_panel.reshape(col_count, rows // col_count, NB), "col")[0]
    panel_rows = gather(share, "col").reshape(rows, NB)

    own_top = jnp.where(
        (col_index == 0) & (jnp.arange(col_blocks) == 0)[:, None, None], 0.0, by_block[0].transpose(1, 2, 0)
    ).reshape(cols, NB)
    col_share = exchange(own_top.reshape(row_count, cols // row_count, NB), "row")[0]
    panel_cols = gather(col_share, "row").reshape(cols, NB)

    inverse, sign, shift = cholesky_parts(gram, lead)
    sign_rows = jnp.where(row_index == 1, sign, 0.0)
    y_rows = mult(panel_rows, inverse, 1, 1)
    y_rows = jnp.concatenate([y_rows[:NB] - sign_rows, y_rows[NB:]], 0)
    partial = mult(local, y_rows, 0, 0)

    part = jnp.sum(exchange(partial.reshape(row_count, cols // row_count, NB), "row"), 0)
    z_cols = gather(part, "row").reshape(cols, NB)

    coupling = invert(shift).T
    y_cols = mult(panel_cols, inverse, 1, 1)
    y_cols = jnp.concatenate([y_cols[:NB] - jnp.where(col_index == 1, sign, 0.0), y_cols[NB:]], 0)
    v_cols = mult(y_cols, coupling, 1, 1)
    u_cols = mult(z_cols, coupling)

    middle = mult(y_cols, z_cols, 0, 0)
    thin = cols // col_count
    sent = jnp.concatenate([z_cols.reshape(col_count, thin, NB), middle.reshape(col_count, step, NB)], 1)
    got = exchange(sent, "col")
    middle_piece = jnp.sum(got[:, thin:], 0)
    by_fold = got[:, :thin].reshape(fold, row_count, thin, NB)
    mine = lax.dynamic_index_in_dim(by_fold, row_index, 1, keepdims=False).reshape(fold * thin, NB)
    last = gather(jnp.concatenate([mine, middle_piece], 0), "col")
    middle = last[:, fold * thin :].reshape(NB, NB)
    z_rows = last[:, : fold * thin].reshape(col_count, fold, thin, NB).transpose(1, 0, 2, 3)
    z_rows = z_rows.reshape(fold, col_blocks, NB, NB).transpose(1, 0, 2, 3).reshape(rows, NB)

    inner = mult(mult(coupling, middle, 0, 0), coupling)
    u_cols = u_cols - mult(y_cols, inner)
    updated = local - mult(jnp.concatenate([y_rows, z_rows], 1), jnp.concatenate([u_cols, v_cols], 1), 1, 1)
    return updated.reshape(kernel.shape)


def solution(mesh):
    return jax.shard_map(
        body,
        mesh=mesh,
        in_specs=(P(None, "row", None, None, "col", None),),
        out_specs=P(None, "row", None, None, "col", None),
        check_vma=False,
    )
```

time: 1210 us -> 255 us (0.21)
  waiting for transfers between devices: 913 us -> 76.9 us
  other arithmetic: 147 us -> 2.84 us
  local copies, waits for them, and re-layouts: 96.6 us -> 14.9 us
  starting transfers between devices: 0.65 us -> 66.5 us
  blocking collectives: 0 us -> 41.4 us
  Pallas kernels: 0 us -> 37.8 us
  between operations: 13.7 us -> 0.45 us
    psum x7 -> x0, waiting for transfers between devices: 913 us -> none  [the longest x4 538 us: broadcast(): return lax.psum(kept, axis)]
    broadcast_in_dim x128 -> x0, other arithmetic: 83.7 us -> none  [step(): jnp.where(below[:, None] & (index_line == k)[None, :], low_col[:, None],...]
    dynamic_slice x130 -> x1, local copies, waits for them, and re-layouts: 77.2 us -> 0.01 us  [body(): lax.dynamic_index_in_dim(by_fold, row_index, 1, keepdims=False)]
    all_to_all x0 -> x9, waiting for transfers between devices: none -> 76.9 us  [exchange(): return lax.all_to_all(pieces, axis, 0, 0)]
    all_to_all x0 -> x9, starting transfers between devices: none -> 66.5 us  [exchange(): return lax.all_to_all(pieces, axis, 0, 0)]
    another operation x9 -> x0, other arithmetic: 42.6 us -> none  [the longest x3 12.4 us: body(): first_factor = jnp.linalg.cholesky(lax.psum(gram, 'row'))]
    all_to_all x0 -> x2, blocking collectives: none -> 41.4 us  [exchange(): return lax.all_to_all(pieces, axis, 0, 0)]
    pallas_call x0 -> x2, Pallas kernels: none -> 37.8 us  [the longest x1 19 us: cholesky_parts(): pl.pallas_call(cholesky_kernel, out_shape=(SQUARE, SQUARE, SQUARE), name=...]
  transfers between devices with their start and end apart: 7 -> 9, of which waited for: 7 -> 7; matrix products, arithmetic and copies ran while one was open for 1% -> 3% of each run, Pallas kernels for 0% -> 15%
where the time goes in v1:
time: 255 us; the launch traced here: 254 us
  waiting for transfers between devices  76.9 us (30%)
  starting transfers between devices  66.5 us (26%)
  blocking collectives  41.4 us (16%)
  Pallas kernels  37.8 us (15%)
  local copies, waits for them, and re-layouts  14.9 us (6%)
  matrix products  12.9 us (5%)
  other arithmetic  2.84 us (1%)
    all_to_all x9, waiting for transfers between devices, exchange(): return lax.all_to_all(pieces, axis, 0, 0)  76.9 us
    all_to_all x9, starting transfers between devices, exchange(): return lax.all_to_all(pieces, axis, 0, 0)  66.5 us
    all_to_all x2, blocking collectives, exchange(): return lax.all_to_all(pieces, axis, 0, 0)  41.4 us
    pallas_call x1, Pallas kernels, cholesky_parts(): pl.pallas_call(cholesky_kernel, out_shape=(SQUARE, SQUARE, SQUARE), name=...  19 us
    pallas_call x1, Pallas kernels, invert(): pl.pallas_call(invert_kernel, out_shape=SQUARE, name='invert', cost_estim...  18.9 us
    dot_general x11, matrix products, mult(): lax.dot_general(left, right, (((left_dim,), (right_dim,)), ((), ())), pre...  12.9 us
  transfers between devices with their start and end apart: 9, of which 7 were waited for; matrix products, arithmetic and copies ran while one was open for 3% of the time, Pallas kernels for 15%

profile of v1, /device:TPU:1, one launch (start us, length us, event | category | flops | bytes accessed | tf_op | source)
XLA Modules:
  0.0 253.8 jit_solution(3495503505922320252)
XLA Ops:
  0.1 1.8 copy.73
  2.5 0.9 fusion.17
  3.6 17.2 %all_to_all.55 = f32[32,8,128]{2,1,0:T(8,128)S(1)} all-to-all(f32[32,8,128]{2,1,0:T(8,128)S(1)} %copy.48), channel_id=1, replica_groups=mesh['row'=16,'col'=32] {'col'}, dimensions={0} | all-to-all | bytes 262144 | tf_op jit(solution)/shard_map/all_to_all | solution.py:109
  21.5 13.7 %all-to-all-start.3 = ((f32[16,8,128]{2,1,0:T(8,128)}), f32[16,8,128]{2,1,0:T(8,128)S(1)}, u32[]{:S(2)}, u32[]{:S(2)}) async-start(f32[16,8,128]{2,1,0:T(8,128)} %broadcast_in_dim.109), calls=%async_computation.3 | async-start | bytes 131072 | tf_op jit(solution)/shard_map/all_to_all | solution.py:109
  35.3 11.4 %all-to-all-done.3 = f32[16,8,128]{2,1,0:T(8,128)S(1)} async-done(((f32[16,8,128]{2,1,0:T(8,128)}), f32[16,8,128]{2,1,0:T(8,128)S(1)}, u32[]{:S(2)}, u32[]{:S(2)}) %all-to-all-start.3) | async-done | bytes 65568 | tf_op jit(solution)/shard_map/all_to_all | solution.py:109
  47.4 5.6 %all-to-all-start.4 = ((f32[32,8,128]{2,1,0:T(8,128)}), f32[32,8,128]{2,1,0:T(8,128)S(1)}, u32[]{:S(2)}, u32[]{:S(2)}) async-start(f32[32,8,128]{2,1,0:T(8,128)} %broadcast_in_dim.110), calls=%async_computation.4 | async-start | bytes 262144 | tf_op jit(solution)/shard_map/all_to_all | solution.py:109
  53.9 6.8 %all-to-all-done.4 = f32[32,8,128]{2,1,0:T(8,128)S(1)} async-done(((f32[32,8,128]{2,1,0:T(8,128)}), f32[32,8,128]{2,1,0:T(8,128)S(1)}, u32[]{:S(2)}, u32[]{:S(2)}) %all-to-all-start.4) | async-done | bytes 131104 | tf_op jit(solution)/shard_map/all_to_all | solution.py:109
  60.8 3.9 %all-to-all-start = ((f32[32,32,128]{2,1,0:T(8,128)}), f32[32,32,128]{2,1,0:T(8,128)S(1)}, u32[]{:S(2)}, u32[]{:S(2)}) async-start(f32[32,32,128]{2,1,0:T(8,128)} %broadcast_select_fusion.1), calls=%async_computation | async-start | bytes 1048576 | tf_op jit(solution)/shard_map/all_to_all | solution.py:109
  65.7 10.7 %all-to-all-done = f32[32,32,128]{2,1,0:T(8,128)S(1)} async-done(((f32[32,32,128]{2,1,0:T(8,128)}), f32[32,32,128]{2,1,0:T(8,128)S(1)}, u32[]{:S(2)}, u32[]{:S(2)}) %all-to-all-start) | async-done | bytes 524320 | tf_op jit(solution)/shard_map/all_to_all | solution.py:109
  76.4 3.5 %all-to-all-start.7 = ((f32[16,32,128]{2,1,0:T(8,128)}), f32[16,32,128]{2,1,0:T(8,128)S(1)}, u32[]{:S(2)}, u32[]{:S(2)}) async-start(f32[16,32,128]{2,1,0:T(8,128)} %bitcast.19), calls=%async_computation.7 | async-start | bytes 524288 | tf_op jit(solution)/shard_map/all_to_all | solution.py:109
  79.9 14.2 %all-to-all-done.7 = f32[16,32,128]{2,1,0:T(8,128)S(1)} async-done(((f32[16,32,128]{2,1,0:T(8,128)}), f32[16,32,128]{2,1,0:T(8,128)S(1)}, u32[]{:S(2)}, u32[]{:S(2)}) %all-to-all-start.7) | async-done | bytes 262176 | tf_op jit(solution)/shard_map/all_to_all | solution.py:109
  95.0 8.5 %all-to-all-start.1 = ((f32[32,32,128]{2,1,0:T(8,128)}), f32[32,32,128]{2,1,0:T(8,128)S(1)}, u32[]{:S(2)}, u32[]{:S(2)}) async-start(f32[32,32,128]{2,1,0:T(8,128)} %broadcast_in_dim.98), calls=%async_computation.1 | async-start | bytes 1048576 | tf_op jit(solution)/shard_map/all_to_all | solution.py:109
  103.5 11.6 %all-to-all-done.1 = f32[32,32,128]{2,1,0:T(8,128)S(1)} async-done(((f32[32,32,128]{2,1,0:T(8,128)}), f32[32,32,128]{2,1,0:T(8,128)S(1)}, u32[]{:S(2)}, u32[]{:S(2)}) %all-to-all-start.1) | async-done | bytes 524320 | tf_op jit(solution)/shard_map/all_to_all | solution.py:109
  115.9 5.7 %all-to-all-start.8 = ((f32[16,32,128]{2,1,0:T(8,128)}), f32[16,32,128]{2,1,0:T(8,128)}, u32[]{:S(2)}, u32[]{:S(2)}) async-start(f32[16,32,128]{2,1,0:T(8,128)} %broadcast_in_dim.116), calls=%async_computation.8 | async-start | bytes 524288 | tf_op jit(solution)/shard_map/all_to_all | solution.py:109
  122.2 19.0 %cholesky_parts.1 = (f32[128,128]{1,0:T(8,128)}, f32[128,128]{1,0:T(8,128)}, f32[128,128]{1,0:T(8,128)}) custom-call(f32[128,128]{1,0:T(8,128)} %bitcast.96, f32[128,128]{1,0:T(8,128)} %bitcast.95), custom_call_target="tpu_custom_call" | custom-call | flops 40000000 | bytes 400000 | tf_op jit(solution)/shard_map/cholesky_parts/pallas_call | solution.py:91
  141.2 1.4 fusion.29
  142.7 1.3 fusion.30
  144.8 1.4 fusion.3
  146.3 24.2 %all_to_all.56 = f32[16,32,128]{2,1,0:T(8,128)S(1)} all-to-all(f32[16,32,128]{2,1,0:T(8,128)S(1)} %bitcast.90), channel_id=1, replica_groups=mesh['row'=16,'col'=32] {'row'}, dimensions={0} | all-to-all | bytes 524288 | tf_op jit(solution)/shard_map/all_to_all | solution.py:109
  171.2 11.1 %all-to-all-start.6 = ((f32[16,32,128]{2,1,0:T(8,128)}), f32[16,32,128]{2,1,0:T(8,128)S(1)}, u32[]{:S(2)}, u32[]{:S(2)}) async-start(f32[16,32,128]{2,1,0:T(8,128)} %broadcast_in_dim.112), calls=%async_computation.6 | async-start | bytes 524288 | tf_op jit(solution)/shard_map/all_to_all | solution.py:109
  182.4 0.9 slice.77
  183.6 11.9 %all-to-all-done.6 = f32[16,32,128]{2,1,0:T(8,128)S(1)} async-done(((f32[16,32,128]{2,1,0:T(8,128)}), f32[16,32,128]{2,1,0:T(8,128)S(1)}, u32[]{:S(2)}, u32[]{:S(2)}) %all-to-all-start.6) | async-done | bytes 262176 | tf_op jit(solution)/shard_map/all_to_all | solution.py:109
  196.7 9.9 %all-to-all-start.9 = ((f32[32,20,128]{2,1,0:T(8,128)}), f32[32,20,128]{2,1,0:T(8,128)S(1)}, u32[]{:S(2)}, u32[]{:S(2)}) async-start(f32[32,20,128]{2,1,0:T(8,128)} %pad_maximum_fusion), calls=%async_computation.9 | async-start | bytes 786432 | tf_op jit(solution)/shard_map/all_to_all | solution.py:109
  206.7 10.3 %all-to-all-done.9 = f32[32,20,128]{2,1,0:T(8,128)S(1)} async-done(((f32[32,20,128]{2,1,0:T(8,128)}), f32[32,20,128]{2,1,0:T(8,128)S(1)}, u32[]{:S(2)}, u32[]{:S(2)}) %all-to-all-start.9) | async-done | bytes 327712 | tf_op jit(solution)/shard_map/all_to_all | solution.py:109
  217.9 4.6 %all-to-all-start.10 = ((f32[32,36,128]{2,1,0:T(8,128)}), f32[32,36,128]{2,1,0:T(8,128)}, u32[]{:S(2)}, u32[]{:S(2)}) async-start(f32[32,36,128]{2,1,0:T(8,128)} %broadcast_in_dim.117), calls=%async_computation.10 | async-start | bytes 1310720 | tf_op jit(solution)/shard_map/all_to_all | solution.py:109
  222.5 18.9 %invert.1 = f32[128,128]{1,0:T(8,128)} custom-call(f32[128,128]{1,0:T(8,128)} %get-tuple-element.10.shift_ref), custom_call_target="tpu_custom_call" | custom-call | flops 40000000 | bytes 400000 | tf_op jit(solution)/shard_map/invert/pallas_call | solution.py:100
  241.4 1.3 fusion.21
  242.7 1.9 fusion.31
  244.6 1.1 slice.80
  245.9 0.9 slice.81
  247.7 3.2 %bitcast_subtract_fusion = f32[1024,512]{1,0:T(8,128)} fusion(f32[128,8,4,128]{3,2,1,0:T(4,128)S(1)} %bitcast.78, f32[1024,128]{1,0:T(8,128)S(1)} %bitcast.89, f32[896,128]{1,0:T(8,128)S(1)} %slice.74, f32[128,128]{1,0:T(8,128)S(1)} %copy-done.7, f32[512,128]{0,1:T(8,128)S(1)} %fusion.21, f32[512,128]{0,1:T(8,128)S(1)} %convolution_subtract_fusion), kind=kOutput, calls=%fused_computation | convolution fusion | flops 1611792384 | bytes 5767168 | tf_op jit(solution)/shard_map/dot_general | solution.py:13
  250.9 2.9 %reshape.98 = f32[8,1,128,4,1,128]{5,3,2,0,4,1:T(4,128)} reshape(f32[1024,512]{1,0:T(8,128)} %bitcast_subtract_fusion) | data formatting | bytes 4194304 | tf_op jit(solution)/shard_map/reshape | solution.py:179
  (68 shorter events, 11.4 us)
Async XLA Ops:
  3.4 61.3 %slice-start = ((f32[8,1,128,4,1,128]{5,4,3,2,1,0:T(1,128)}), f32[1,1,128,4,1,128]{5,4,3,2,1,0:T(1,128)S(1)}, s32[]{:S(2)}) async-start(f32[8,1,128,4,1,128]{5,4,3,2,1,0:T(1,128)} %param.1), calls=%async_computation.11 | async-start | bytes 524288 | tf_op jit(solution)/shard_map/slice | solution.py:144
  21.5 25.3 %all-to-all-start.3 = ((f32[16,8,128]{2,1,0:T(8,128)}), f32[16,8,128]{2,1,0:T(8,128)S(1)}, u32[]{:S(2)}, u32[]{:S(2)}) async-start(f32[16,8,128]{2,1,0:T(8,128)} %broadcast_in_dim.109), calls=%async_computation.3 | async-start | bytes 131072 | tf_op jit(solution)/shard_map/all_to_all | solution.py:109
  47.4 13.4 %all-to-all-start.4 = ((f32[32,8,128]{2,1,0:T(8,128)}), f32[32,8,128]{2,1,0:T(8,128)S(1)}, u32[]{:S(2)}, u32[]{:S(2)}) async-start(f32[32,8,128]{2,1,0:T(8,128)} %broadcast_in_dim.110), calls=%async_computation.4 | async-start | bytes 262144 | tf_op jit(solution)/shard_map/all_to_all | solution.py:109
  60.8 15.6 %all-to-all-start = ((f32[32,32,128]{2,1,0:T(8,128)}), f32[32,32,128]{2,1,0:T(8,128)S(1)}, u32[]{:S(2)}, u32[]{:S(2)}) async-start(f32[32,32,128]{2,1,0:T(8,128)} %broadcast_select_fusion.1), calls=%async_computation | async-start | bytes 1048576 | tf_op jit(solution)/shard_map/all_to_all | solution.py:109
  76.4 17.7 %all-to-all-start.7 = ((f32[16,32,128]{2,1,0:T(8,128)}), f32[16,32,128]{2,1,0:T(8,128)S(1)}, u32[]{:S(2)}, u32[]{:S(2)}) async-start(f32[16,32,128]{2,1,0:T(8,128)} %bitcast.19), calls=%async_computation.7 | async-start | bytes 524288 | tf_op jit(solution)/shard_map/all_to_all | solution.py:109
  95.0 20.1 %all-to-all-start.1 = ((f32[32,32,128]{2,1,0:T(8,128)}), f32[32,32,128]{2,1,0:T(8,128)S(1)}, u32[]{:S(2)}, u32[]{:S(2)}) async-start(f32[32,32,128]{2,1,0:T(8,128)} %broadcast_in_dim.98), calls=%async_computation.1 | async-start | bytes 1048576 | tf_op jit(solution)/shard_map/all_to_all | solution.py:109
  103.5 41.3 %copy-start = (f32[8,1,128,4,1,128]{5,4,3,2,1,0:T(1,128)S(1)}, f32[8,1,128,4,1,128]{5,4,3,2,1,0:T(1,128)}, u32[]{:S(2)}) copy-start(f32[8,1,128,4,1,128]{5,4,3,2,1,0:T(1,128)} %param.1) | copy-start | bytes 6291460
  115.9 26.8 %all-to-all-start.8 = ((f32[16,32,128]{2,1,0:T(8,128)}), f32[16,32,128]{2,1,0:T(8,128)}, u32[]{:S(2)}, u32[]{:S(2)}) async-start(f32[16,32,128]{2,1,0:T(8,128)} %broadcast_in_dim.116), calls=%async_computation.8 | async-start | bytes 524288 | tf_op jit(solution)/shard_map/all_to_all | solution.py:109
  141.2 2.9 %copy-start.8 = (f32[128,128]{1,0:T(8,128)S(1)}, f32[128,128]{1,0:T(8,128)}, u32[]{:S(2)}) copy-start(f32[128,128]{1,0:T(8,128)} %get-tuple-element.9) | copy-start | bytes 196612
  144.1 26.4 %copy-start.2 = (f32[512,128]{1,0:T(8,128)}, f32[512,128]{1,0:T(8,128)S(1)}, u32[]{:S(2)}) copy-start(f32[512,128]{1,0:T(8,128)S(1)} %fusion.30) | copy-start | bytes 786436
  144.1 0.7 copy-start.6
  144.1 39.2 %copy-start.4 = (f32[128,128]{1,0:T(8,128)}, f32[128,128]{1,0:T(8,128)S(1)}, u32[]{:S(2)}) copy-start(f32[128,128]{1,0:T(8,128)S(1)} %get-tuple-element.16) | copy-start | bytes 196612
  171.2 24.2 %all-to-all-start.6 = ((f32[16,32,128]{2,1,0:T(8,128)}), f32[16,32,128]{2,1,0:T(8,128)S(1)}, u32[]{:S(2)}, u32[]{:S(2)}) async-start(f32[16,32,128]{2,1,0:T(8,128)} %broadcast_in_dim.112), calls=%async_computation.6 | async-start | bytes 524288 | tf_op jit(solution)/shard_map/all_to_all | solution.py:109
  195.9 45.4 %copy-start.5 = (f32[128,128]{1,0:T(8,128)S(1)}, f32[128,128]{1,0:T(8,128)}, u32[]{:S(2)}) copy-start(f32[128,128]{1,0:T(8,128)} %copy-done.4) | copy-start | bytes 196612
  196.7 20.2 %all-to-all-start.9 = ((f32[32,20,128]{2,1,0:T(8,128)}), f32[32,20,128]{2,1,0:T(8,128)S(1)}, u32[]{:S(2)}, u32[]{:S(2)}) async-start(f32[32,20,128]{2,1,0:T(8,128)} %pad_maximum_fusion), calls=%async_computation.9 | async-start | bytes 786432 | tf_op jit(solution)/shard_map/all_to_all | solution.py:109
  217.9 26.8 %all-to-all-start.10 = ((f32[32,36,128]{2,1,0:T(8,128)}), f32[32,36,128]{2,1,0:T(8,128)}, u32[]{:S(2)}, u32[]{:S(2)}) async-start(f32[32,36,128]{2,1,0:T(8,128)} %broadcast_in_dim.117), calls=%async_computation.10 | async-start | bytes 1310720 | tf_op jit(solution)/shard_map/all_to_all | solution.py:109
  241.4 5.4 %copy-start.1 = (f32[128,128]{1,0:T(8,128)S(1)}, f32[128,128]{1,0:T(8,128)}, u32[]{:S(2)}) copy-start(f32[128,128]{1,0:T(8,128)} %invert.1) | copy-start | bytes 196612
  244.6 3.1 %copy-start.7 = (f32[128,128]{1,0:T(8,128)S(1)}, f32[128,128]{1,0:T(8,128)}, u32[]{:S(2)}) copy-start(f32[128,128]{1,0:T(8,128)} %copy-done.6) | copy-start | bytes 196612
  244.6 2.6 %copy-start.3 = (f32[512,128]{0,1:T(8,128)S(1)}, f32[512,128]{0,1:T(8,128)}, u32[]{:S(2)}) copy-start(f32[512,128]{0,1:T(8,128)} %fusion.31) | copy-start | bytes 786436

commit v2 on v1

v2 whole, which is shorter than its diff:
```python
import jax
import jax.numpy as jnp
from jax import lax
from jax.experimental import pallas as pl
from jax.experimental.pallas import tpu as pltpu
from jax.sharding import PartitionSpec as P

NB = 128
SUB = 8
VMEM = pl.BlockSpec(memory_space=pltpu.VMEM)
SMEM = pl.BlockSpec(memory_space=pltpu.SMEM)
PARAMS = pltpu.CompilerParams(vmem_limit_bytes=40 * 1024 * 1024)


def mult(left, right, left_dim=1, right_dim=0):
    return lax.dot_general(
        left,
        right,
        (((left_dim,), (right_dim,)), ((), ())),
        precision=lax.Precision.HIGHEST,
        preferred_element_type=jnp.float32,
    )


def shape(*dims):
    return jax.ShapeDtypeStruct(dims, jnp.float32)


def cost(flops, nbytes):
    return pl.CostEstimate(flops=flops, bytes_accessed=nbytes, transcendentals=0)


def lane(block, k):
    return jnp.broadcast_to(block[:, k : k + 1], (SUB, NB))


def row(block, s):
    return jnp.broadcast_to(block[s : s + 1, :], (SUB, NB))


def lane_ids():
    sub_id = lax.broadcasted_iota(jnp.int32, (SUB, NB), 0)
    lane_id = lax.broadcasted_iota(jnp.int32, (SUB, NB), 1)
    return sub_id, lane_id


def inverse_factor(left):
    count = NB // SUB
    sub_id, lane_id = lane_ids()
    eye = [jnp.where(lane_id == sub_id + SUB * i, 1.0, 0.0) for i in range(count)]
    right = list(eye)
    for k in range(0, NB, 2):
        b, s = divmod(k, SUB)
        one, two = row(left[b], s), row(left[b], s + 1)
        eone, etwo = row(right[b], s), row(right[b], s + 1)
        a11, a12, a22 = lane(one, k), lane(one, k + 1), lane(two, k + 1)
        scale = 1.0 / (a11 * a22 - a12 * a12)
        i11, i12, i22 = a22 * scale, a12 * scale, a11 * scale
        p1, p2 = i11 * one - i12 * two, i22 * two - i12 * one
        q1, q2 = i11 * eone - i12 * etwo, i22 * etwo - i12 * eone
        for i in range(b, count):
            c1, c2 = lane(left[i], k), lane(left[i], k + 1)
            if i == b:
                c1 = jnp.where(sub_id > s + 1, c1, 0.0)
                c2 = jnp.where(sub_id > s + 1, c2, 0.0)
            left[i] = left[i] - c1 * p1 - c2 * p2
            right[i] = right[i] - c1 * q1 - c2 * q2
    odd = (sub_id % 2) == 1
    out = []
    for i in range(count):
        diag = jnp.sum(left[i] * eye[i], axis=1, keepdims=True)
        below = jnp.sum(jnp.where(lane_id == sub_id + (SUB * i - 1), left[i], 0.0), axis=1, keepdims=True)
        diag, below = jnp.broadcast_to(diag, (SUB, NB)), jnp.broadcast_to(below, (SUB, NB))
        ratio = jnp.where(odd, below / pltpu.roll(diag, 1, 0), 0.0)
        rows = right[i] - ratio * pltpu.roll(right[i], 1, 0)
        out.append(rows * lax.rsqrt(diag - ratio * below))
    return out


def invert_kernel(shift_ref, out_ref):
    count = NB // SUB
    sub_id, lane_id = lane_ids()
    held = [
        jnp.where(lane_id == sub_id + SUB * i, 1.0, 0.0) - shift_ref[SUB * i : SUB * i + SUB, :] for i in range(count)
    ]
    for k in range(0, NB, 2):
        b, s = divmod(k, SUB)
        one, two = row(held[b], s), row(held[b], s + 1)
        a11, a12, a21, a22 = lane(one, k), lane(one, k + 1), lane(two, k), lane(two, k + 1)
        scale = 1.0 / (a11 * a22 - a12 * a21)
        i11, i12, i21, i22 = a22 * scale, -a12 * scale, -a21 * scale, a11 * scale
        h1, h2 = lane_id == k, lane_id == k + 1
        o1 = jnp.where(h1, 1.0, jnp.where(h2, 0.0, one))
        o2 = jnp.where(h1, 0.0, jnp.where(h2, 1.0, two))
        n1, n2 = i11 * o1 + i12 * o2, i21 * o1 + i22 * o2
        for i in range(count):
            c1, c2 = lane(held[i], k), lane(held[i], k + 1)
            new = jnp.where(h1 | h2, 0.0, held[i]) - c1 * n1 - c2 * n2
            if i == b:
                new = jnp.where(sub_id == s, n1, jnp.where(sub_id == s + 1, n2, new))
            held[i] = new
    for i in range(count):
        out_ref[SUB * i : SUB * i + SUB, :] = held[i]


def prepare_kernel(col_blocks, ids_ref, a_ref, send_ref, top_ref):
    rows = a_ref.shape[0] // col_blocks
    col_count, row_count = send_ref.shape[0], top_ref.shape[0]
    share, step = rows // col_count, NB // col_count
    panel = a_ref[pl.ds(0, rows, col_blocks), :]
    first = jnp.where(ids_ref[0] == 0, 0.0, panel[:NB])
    panel = jnp.concatenate([first, panel[NB:]], 0)
    gram = mult(panel, panel, 0, 0)
    lead = jnp.where(ids_ref[0] == 1, first, 0.0)
    send_ref[:, :share, :] = panel.reshape(col_count, share, NB)
    for c in range(col_count):
        send_ref[c, share : share + step, :] = gram[c * step : (c + 1) * step]
        send_ref[c, share + step : share + 2 * step, :] = lead[c * step : (c + 1) * step]
    thin = col_blocks * NB // row_count
    per = NB // thin
    for k in range(col_blocks):
        block = a_ref[pl.ds(k, NB, col_blocks), :].T
        if k == 0:
            block = jnp.where(ids_ref[1] == 0, 0.0, block)
        top_ref[k * per : (k + 1) * per] = block.reshape(per, thin, NB)


def factor_kernel(col_blocks, ids_ref, got_ref, a_ref, inv_ref, sign_ref, shift_ref, y_ref, part_ref, hold_ref, lead_ref):
    col_count = got_ref.shape[0]
    rows = a_ref.shape[0] // col_blocks
    share, step = rows // col_count, NB // col_count
    count = NB // SUB
    sub_id, lane_id = lane_ids()
    for c in range(col_count):
        hold_ref[c * step : (c + 1) * step, :] = got_ref[c, share : share + step, :]
        lead_ref[c * step : (c + 1) * step, :] = got_ref[c, share + step : share + 2 * step, :]
    out = inverse_factor([hold_ref[SUB * i : SUB * i + SUB, :] for i in range(count)])
    for i in range(count):
        inv_ref[SUB * i : SUB * i + SUB, :] = out[i]
    inverse = inv_ref[...]
    lead = lead_ref[...]
    signs = jnp.where(jnp.sum(lead * inverse, axis=1, keepdims=True) >= 0, -1.0, 1.0)
    shift_ref[...] = signs * mult(lead, inverse, 1, 1)
    for i in range(count):
        here = jnp.where(lane_id == sub_id + SUB * i, 1.0, 0.0)
        sign_ref[SUB * i : SUB * i + SUB, :] = here * signs[SUB * i : SUB * i + SUB]
    panel = got_ref[:, :share, :].reshape(rows, NB)
    y_ref[...] = mult(panel, inverse, 1, 1)

    @pl.when(ids_ref[0] == 1)
    def _():
        y_ref[:NB, :] = y_ref[:NB, :] - sign_ref[...]

    flipped = y_ref[...].T
    for k in range(col_blocks):
        part_ref[k * NB : (k + 1) * NB, :] = mult(flipped, a_ref[pl.ds(k, rows, col_blocks), :]).T


def middle_kernel(ids_ref, got_ref, inv_ref, sign_ref, y_ref, send_ref, hold_ref):
    row_count, both, _ = got_ref.shape
    thin = both // 2
    cols = row_count * thin
    col_count = send_ref.shape[0]
    step, share = NB // col_count, cols // col_count
    z = got_ref[:, :thin, :].reshape(cols, NB)
    y_ref[...] = mult(got_ref[:, thin:, :].reshape(cols, NB), inv_ref[...], 1, 1)

    @pl.when(ids_ref[1] == 1)
    def _():
        y_ref[:NB, :] = y_ref[:NB, :] - sign_ref[...]

    hold_ref[...] = mult(y_ref[...], z, 0, 0)
    send_ref[:, :share, :] = z.reshape(col_count, share, NB)
    for c in range(col_count):
        send_ref[c, share : share + step, :] = hold_ref[c * step : (c + 1) * step, :]
        if send_ref.shape[1] > share + step:
            send_ref[c, share + step :, :] = jnp.zeros((send_ref.shape[1] - share - step, NB), jnp.float32)


def columns_kernel(got_ref, y_ref, coupling_ref, u_ref, v_ref):
    row_count, both, _ = got_ref.shape
    z = got_ref[:, : both // 2, :].reshape(row_count * (both // 2), NB)
    v_ref[...] = mult(y_ref[...], coupling_ref[...])
    u_ref[...] = mult(z, coupling_ref[...], 1, 1)


def update_kernel(col_blocks, fold, got_ref, coupling_ref, u_ref, v_ref, y_col_ref, y_ref, a_ref, out_ref, right_ref, hold_ref):
    col_count = got_ref.shape[0]
    thin = col_blocks * NB // col_count
    step = NB // col_count
    per = NB // thin
    at = pl.program_id(0)

    @pl.when(at == 0)
    def _():
        for c in range(col_count):
            hold_ref[c * step : (c + 1) * step, :] = got_ref[c, fold * thin : fold * thin + step, :]
        coupling = coupling_ref[...]
        inner = mult(mult(coupling, hold_ref[...]), coupling, 1, 1)
        right_ref[:, :NB] = u_ref[...] - mult(y_col_ref[...], inner)
        right_ref[:, NB:] = v_ref[...]

    for f in range(fold):
        z = got_ref[pl.ds(at * per, per), f * thin : (f + 1) * thin, :].reshape(NB, NB)
        y = y_ref[f * NB : (f + 1) * NB, :]
        change = mult(jnp.concatenate([y, z], 1), right_ref[...], 1, 1)
        for k in range(col_blocks):
            here = pl.ds(f * NB * col_blocks + k, NB, col_blocks)
            out_ref[here, :] = a_ref[here, :] - change[:, k * NB : (k + 1) * NB]


def exchange(pieces, axis):
    return lax.all_to_all(pieces, axis, 0, 0)


def gather(piece, axis):
    count = lax.axis_size(axis)
    return exchange(jnp.broadcast_to(piece[None], (count,) + piece.shape), axis)


def body(kernel):
    row_blocks, _, _, col_blocks, _, _ = kernel.shape
    rows, cols = row_blocks * NB, col_blocks * NB
    row_count, col_count = lax.axis_size("row"), lax.axis_size("col")
    fold = col_count // row_count
    row_index, col_index = lax.axis_index("row"), lax.axis_index("col")
    ids = jnp.stack([row_index, col_index]).astype(jnp.int32)
    lines = kernel.reshape(rows * col_blocks, NB)
    share, step = rows // col_count, NB // col_count
    thin = cols // row_count
    slim = cols // col_count
    pad = pl.cdiv(step, SUB) * SUB

    send, top = pl.pallas_call(
        lambda *refs: prepare_kernel(col_blocks, *refs),
        out_shape=(shape(col_count, share + 2 * step, NB), shape(row_count, thin, NB)),
        in_specs=[SMEM, VMEM],
        out_specs=(VMEM, VMEM),
        compiler_params=PARAMS,
        name="prepare",
        cost_estimate=cost(2 * rows * NB * NB * 6, 3_000_000),
    )(ids, lines)
    got = exchange(send, "col")[0]
    panel_share, piece = got[:share], got[share:]
    got = exchange(jnp.concatenate([top, jnp.broadcast_to(piece[None], (row_count,) + piece.shape)], 1), "row")
    top_share = got[0, :thin]
    piece = jnp.sum(got[:, thin:], 0)
    got = gather(jnp.concatenate([panel_share, piece], 0), "col")

    inverse, sign, shift, y_rows, partial = pl.pallas_call(
        lambda *refs: factor_kernel(col_blocks, *refs),
        out_shape=(shape(NB, NB), shape(NB, NB), shape(NB, NB), shape(rows, NB), shape(cols, NB)),
        in_specs=[SMEM, VMEM, VMEM],
        out_specs=(VMEM,) * 5,
        scratch_shapes=[pltpu.VMEM((NB, NB), jnp.float32)] * 2,
        compiler_params=PARAMS,
        name="factor",
        cost_estimate=cost(2 * rows * cols * NB * 6, 4_000_000),
    )(ids, got, lines)

    got = exchange(partial.reshape(row_count, thin, NB), "row")
    coupling = pl.pallas_call(
        invert_kernel,
        out_shape=shape(NB, NB),
        in_specs=[VMEM],
        out_specs=VMEM,
        name="invert",
        cost_estimate=cost(4_000_000_000, 200_000),
    )(shift)
    got, coupling = lax.optimization_barrier((got, coupling))
    got = gather(jnp.concatenate([jnp.sum(got, 0), top_share], 0), "row")

    y_cols, send = pl.pallas_call(
        middle_kernel,
        out_shape=(shape(cols, NB), shape(col_count, slim + pad, NB)),
        in_specs=[SMEM, VMEM, VMEM, VMEM],
        out_specs=(VMEM, VMEM),
        scratch_shapes=[pltpu.VMEM((NB, NB), jnp.float32)],
        compiler_params=PARAMS,
        name="middle",
        cost_estimate=cost(4 * cols * NB * NB * 6, 2_000_000),
    )(ids, got, inverse, sign)
    back = exchange(send, "col")
    u_cols, v_cols = pl.pallas_call(
        columns_kernel,
        out_shape=(shape(cols, NB), shape(cols, NB)),
        in_specs=[VMEM] * 3,
        out_specs=(VMEM, VMEM),
        compiler_params=PARAMS,
        name="columns",
        cost_estimate=cost(4 * cols * NB * NB * 6, 2_000_000),
    )(got, y_cols, coupling)
    back, u_cols, v_cols = lax.optimization_barrier((back, u_cols, v_cols))
    by_fold = back[:, :slim].reshape(fold, row_count, slim, NB)
    mine = lax.dynamic_index_in_dim(by_fold, row_index, 1, keepdims=False).reshape(fold * slim, NB)
    last = gather(jnp.concatenate([mine, jnp.sum(back[:, slim:], 0)], 0), "col")

    whole = lambda *dims: pl.BlockSpec(dims, lambda i: (0,) * len(dims))
    updated = pl.pallas_call(
        lambda *refs: update_kernel(col_blocks, fold, *refs),
        grid=(row_blocks // fold,),
        out_shape=shape(rows * col_blocks, NB),
        in_specs=[
            whole(col_count, fold * slim + pad, NB),
            whole(NB, NB),
            whole(cols, NB),
            whole(cols, NB),
            whole(cols, NB),
            pl.BlockSpec((fold * NB, NB), lambda i: (i, 0)),
            pl.BlockSpec((fold * NB * col_blocks, NB), lambda i: (i, 0)),
        ],
        out_specs=pl.BlockSpec((fold * NB * col_blocks, NB), lambda i: (i, 0)),
        scratch_shapes=[pltpu.VMEM((cols, 2 * NB), jnp.float32), pltpu.VMEM((NB, NB), jnp.float32)],
        compiler_params=PARAMS,
        name="update",
        cost_estimate=cost(4 * rows * cols * NB * 6, 6_000_000),
    )(last, coupling, u_cols, v_cols, y_cols, y_rows, lines)
    return updated.reshape(kernel.shape)


def solution(mesh):
    return jax.shard_map(
        body,
        mesh=mesh,
        in_specs=(P(None, "row", None, None, "col", None),),
        out_specs=P(None, "row", None, None, "col", None),
        check_vma=False,
    )
```

time: 255 us -> 197 us (0.77)
  blocking collectives: 41.4 us -> 95.5 us
  waiting for transfers between devices: 76.9 us -> 25.4 us
  starting transfers between devices: 66.5 us -> 30.7 us
  matrix products: 12.9 us -> 0 us
  local copies, waits for them, and re-layouts: 14.9 us -> 8.3 us
  Pallas kernels: 37.8 us -> 34.9 us
    all_to_all x2 -> x4, blocking collectives: 41.4 us -> 95.5 us  [exchange(): return lax.all_to_all(pieces, axis, 0, 0)]
    all_to_all x9 -> x3, waiting for transfers between devices: 76.9 us -> 25.4 us  [exchange(): return lax.all_to_all(pieces, axis, 0, 0)]
    all_to_all x9 -> x3, starting transfers between devices: 66.5 us -> 30.7 us  [exchange(): return lax.all_to_all(pieces, axis, 0, 0)]
    dot_general x11 -> x0, matrix products: 12.9 us -> none  [mult(): lax.dot_general(left, right, (((left_dim,), (right_dim,)), ((), ())), pre...]
    broadcast_in_dim x9 -> x3, local copies, waits for them, and re-layouts: 4.49 us -> 0.13 us  [gather(): return exchange(jnp.broadcast_to(piece[None], (count,) + piece.shape), axis)]
    unnamed x20 -> x24, local copies, waits for them, and re-layouts: 2.67 us -> 6.45 us
    pallas_call x2 -> x6, Pallas kernels: 37.8 us -> 34.9 us  [the longest x1 14 us: body(): pl.pallas_call(lambda *refs: factor_kernel(col_blocks, *refs), out_shape=...]
    reshape x1 -> x0, local copies, waits for them, and re-layouts: 2.88 us -> none  [body(): return updated.reshape(kernel.shape)]
  transfers between devices with their start and end apart: 9 -> 3, of which waited for: 7 -> 3; matrix products, arithmetic and copies ran while one was open for 3% -> 0% of each run, Pallas kernels for 15% -> 6%
where the time goes in v2:
time: 197 us
  blocking collectives  95.5 us (48%)
  Pallas kernels  34.9 us (18%)
  starting transfers between devices  30.7 us (16%)
  waiting for transfers between devices  25.4 us (13%)
  local copies, waits for them, and re-layouts  8.3 us (4%)
    all_to_all x4, blocking collectives, exchange(): return lax.all_to_all(pieces, axis, 0, 0)  95.5 us
    all_to_all x3, starting transfers between devices, exchange(): return lax.all_to_all(pieces, axis, 0, 0)  30.7 us
    all_to_all x3, waiting for transfers between devices, exchange(): return lax.all_to_all(pieces, axis, 0, 0)  25.4 us
    pallas_call x1, Pallas kernels, body(): pl.pallas_call(lambda *refs: factor_kernel(col_blocks, *refs), out_shape=...  14 us
    pallas_call x1, Pallas kernels, body(): pl.pallas_call(invert_kernel, out_shape=shape(NB, NB), in_specs=[VMEM], o...  11.1 us
    unnamed x24, local copies, waits for them, and re-layouts  6.45 us
    pallas_call x1, Pallas kernels, body(): pl.pallas_call(lambda *refs: update_kernel(col_blocks, fold, *refs), grid...  6.41 us
  transfers between devices with their start and end apart: 3, of which 3 were waited for; matrix products, arithmetic and copies ran while one was open for 0% of the time, Pallas kernels for 6%

profile of v2, /device:TPU:1, one launch (start us, length us, event | category | flops | bytes accessed | tf_op | source)
XLA Modules:
  0.0 196.7 jit_solution(2663361917450120301)
XLA Ops:
  0.0 0.1 pad_add_fusion.refs_0_.ids_ref
  0.1 1.6 copy-done
  1.7 1.2 prepare.1
  2.9 0.0 copy-start.1
  2.9 22.7 %all_to_all.35 = f32[32,40,128]{2,1,0:T(8,128)S(1)} all-to-all(f32[32,40,128]{2,1,0:T(8,128)S(1)} %get-tuple-element.21), channel_id=1, replica_groups=mesh['row'=16,'col'=32] {'col'}, dimensions={0} | all-to-all | bytes 1310720 | tf_op jit(solution)/shard_map/all_to_all | solution.py:213
  25.6 0.7 pad_maximum_fusion
  26.3 13.7 %all-to-all-start.1 = ((f32[16,40,128]{2,1,0:T(8,128)}), f32[16,40,128]{2,1,0:T(8,128)S(1)}, u32[]{:S(2)}, u32[]{:S(2)}) async-start(f32[16,40,128]{2,1,0:T(8,128)} %pad_maximum_fusion), calls=%async_computation.1 | async-start | bytes 655360 | tf_op jit(solution)/shard_map/all_to_all | solution.py:213
  40.0 15.2 %all-to-all-done.1 = f32[16,40,128]{2,1,0:T(8,128)S(1)} async-done(((f32[16,40,128]{2,1,0:T(8,128)}), f32[16,40,128]{2,1,0:T(8,128)S(1)}, u32[]{:S(2)}, u32[]{:S(2)}) %all-to-all-start.1) | async-done | bytes 327712 | tf_op jit(solution)/shard_map/all_to_all | solution.py:213
  55.2 0.6 copy-done.11
  55.9 23.2 %all_to_all.36.refs_1_ = f32[32,40,128]{2,1,0:T(8,128)S(1)} all-to-all(f32[32,40,128]{2,1,0:T(8,128)S(1)} %broadcast_in_dim.12), channel_id=1, replica_groups=mesh['row'=16,'col'=32] {'col'}, dimensions={0} | all-to-all | bytes 1310720 | tf_op jit(solution)/shard_map/all_to_all | solution.py:213
  79.1 0.0 copy-done.1
  79.1 14.0 %factor.1 = (f32[128,128]{1,0:T(8,128)S(1)}, f32[128,128]{1,0:T(8,128)S(1)}, f32[128,128]{1,0:T(8,128)S(1)}, f32[1024,128]{1,0:T(8,128)S(1)}, f32[512,128]{1,0:T(8,128)}) custom-call(s32[2]{0:T(128)S(1)} %pad_add_fusion.refs_0_.ids_ref, f32[32,40,128]{2,1,0:T(8,128)S(1)} %all_to_all.36.refs_1_, f32[4096,128]{1,0:T(8,128)S(1)} %bitcast.16), custom_call_target="tpu_custom_call" | custom-call | flops 805306368 | bytes 4000000 | tf_op jit(solution)/shard_map/factor/pallas_call | solution.py:250
  93.1 0.6 copy-done.8
  93.7 0.6 copy-done.10
  94.3 5.6 %all-to-all-start.3 = ((f32[16,32,128]{2,1,0:T(8,128)}), f32[16,32,128]{2,1,0:T(8,128)S(1)}, u32[]{:S(2)}, u32[]{:S(2)}) async-start(f32[16,32,128]{2,1,0:T(8,128)} %bitcast.5), calls=%async_computation.3 | async-start | bytes 524288 | tf_op jit(solution)/shard_map/all_to_all | solution.py:213
  99.9 0.7 slice_bitcast_fusion
  100.6 11.1 %invert.1.coupling_ref.refs_1_ = f32[128,128]{1,0:T(8,128)} custom-call(f32[128,128]{1,0:T(8,128)} %copy-done.10), custom_call_target="tpu_custom_call" | custom-call | flops 4000000000 | bytes 200000 | tf_op jit(solution)/shard_map/invert/pallas_call | solution.py:262
  111.7 1.8 all-to-all-done.3
  113.6 33.1 %all_to_all.37.got_ref = f32[16,64,128]{2,1,0:T(8,128)S(1)} all-to-all(f32[16,64,128]{2,1,0:T(8,128)S(1)} %broadcast_in_dim.13), channel_id=1, replica_groups=mesh['row'=16,'col'=32] {'row'}, dimensions={0} | all-to-all | bytes 1048576 | tf_op jit(solution)/shard_map/all_to_all | solution.py:213
  146.7 0.8 copy-done.9
  147.5 1.7 middle.1
  149.3 0.0 copy-start.2
  149.3 0.7 copy-done.2
  150.0 11.4 %all-to-all-start.5 = ((f32[32,24,128]{2,1,0:T(8,128)}), f32[32,24,128]{2,1,0:T(8,128)}, u32[]{:S(2)}, u32[]{:S(2)}) async-start(f32[32,24,128]{2,1,0:T(8,128)} %copy-done.2), calls=%async_computation.5 | async-start | bytes 786432 | tf_op jit(solution)/shard_map/all_to_all | solution.py:213
  161.5 0.6 columns.1
  162.0 0.7 copy-done.4
  162.7 0.7 copy-done.6
  163.4 8.4 %all-to-all-done.5 = f32[32,24,128]{2,1,0:T(8,128)} async-done(((f32[32,24,128]{2,1,0:T(8,128)}), f32[32,24,128]{2,1,0:T(8,128)}, u32[]{:S(2)}, u32[]{:S(2)}) %all-to-all-start.5) | async-done | bytes 393248 | tf_op jit(solution)/shard_map/all_to_all | solution.py:213
  171.8 1.0 slice_reduce_fusion
  172.8 1.0 slice.30
  173.8 16.5 %all_to_all.38.refs_0_ = f32[32,40,128]{2,1,0:T(8,128)S(1)} all-to-all(f32[32,40,128]{2,1,0:T(8,128)S(1)} %broadcast_in_dim.14), channel_id=1, replica_groups=mesh['row'=16,'col'=32] {'col'}, dimensions={0} | all-to-all | bytes 1310720 | tf_op jit(solution)/shard_map/all_to_all | solution.py:213
  190.3 6.4 %update.1 = f32[4096,128]{1,0:T(8,128)} custom-call(f32[32,40,128]{2,1,0:T(8,128)S(1)} %all_to_all.38.refs_0_, f32[128,128]{1,0:T(8,128)S(1)} %copy-done.3, f32[512,128]{1,0:T(8,128)S(1)} %copy-done.5, f32[512,128]{1,0:T(8,128)S(1)} %copy-done.7, f32[512,128]{1,0:T(8,128)S(1)} %get-tuple-element.29.y_ref.refs_4_, f32[1024,128]{1,0:T(8,128)S(1)} %get-tuple-element.36.refs_5_, ...), custom_call_target="tpu_custom_call" | custom-call | flops 1610612736 | bytes 6000000 | tf_op jit(solution)/shard_map/update/pallas_call | solution.py:299
  (25 shorter events, 0.2 us)
Async XLA Ops:
  0.1 1.6 copy-start
  2.9 76.2 %copy-start.1 = (f32[8,1,128,4,1,128]{5,4,3,2,1,0:T(1,128)S(1)}, f32[8,1,128,4,1,128]{5,4,3,2,1,0:T(1,128)}, u32[]{:S(2)}) copy-start(f32[8,1,128,4,1,128]{5,4,3,2,1,0:T(1,128)} %param.1) | copy-start | bytes 6291460
  26.3 28.9 %all-to-all-start.1 = ((f32[16,40,128]{2,1,0:T(8,128)}), f32[16,40,128]{2,1,0:T(8,128)S(1)}, u32[]{:S(2)}, u32[]{:S(2)}) async-start(f32[16,40,128]{2,1,0:T(8,128)} %pad_maximum_fusion), calls=%async_computation.1 | async-start | bytes 655360 | tf_op jit(solution)/shard_map/all_to_all | solution.py:213
  55.2 0.7 copy-start.11
  93.1 0.6 copy-start.8
  93.7 0.6 copy-start.10
  94.3 19.2 %all-to-all-start.3 = ((f32[16,32,128]{2,1,0:T(8,128)}), f32[16,32,128]{2,1,0:T(8,128)S(1)}, u32[]{:S(2)}, u32[]{:S(2)}) async-start(f32[16,32,128]{2,1,0:T(8,128)} %bitcast.5), calls=%async_computation.3 | async-start | bytes 524288 | tf_op jit(solution)/shard_map/all_to_all | solution.py:213
  111.7 49.8 %copy-start.3 = (f32[128,128]{1,0:T(8,128)S(1)}, f32[128,128]{1,0:T(8,128)}, u32[]{:S(2)}) copy-start(f32[128,128]{1,0:T(8,128)} %invert.1.coupling_ref.refs_1_) | copy-start | bytes 196612
  146.7 0.8 copy-start.9
  149.3 0.7 copy-start.2
  150.0 21.8 %all-to-all-start.5 = ((f32[32,24,128]{2,1,0:T(8,128)}), f32[32,24,128]{2,1,0:T(8,128)}, u32[]{:S(2)}, u32[]{:S(2)}) async-start(f32[32,24,128]{2,1,0:T(8,128)} %copy-done.2), calls=%async_computation.5 | async-start | bytes 786432 | tf_op jit(solution)/shard_map/all_to_all | solution.py:213
  162.0 0.7 copy-start.4
  162.7 0.7 copy-start.6
  171.8 18.6 %copy-start.5 = (f32[512,128]{1,0:T(8,128)S(1)}, f32[512,128]{1,0:T(8,128)}, u32[]{:S(2)}) copy-start(f32[512,128]{1,0:T(8,128)} %copy-done.4) | copy-start | bytes 786436
  171.8 18.6 %copy-start.7 = (f32[512,128]{1,0:T(8,128)S(1)}, f32[512,128]{1,0:T(8,128)}, u32[]{:S(2)}) copy-start(f32[512,128]{1,0:T(8,128)} %copy-done.6) | copy-start | bytes 786436

commit v3 on v2

v3 whole, which is shorter than its diff:
```python
import jax
import jax.numpy as jnp
from jax import lax
from jax.experimental import pallas as pl
from jax.experimental.pallas import tpu as pltpu
from jax.sharding import PartitionSpec as P

NB = 128
SUB = 8
VMEM = pl.BlockSpec(memory_space=pltpu.VMEM)
SMEM = pl.BlockSpec(memory_space=pltpu.SMEM)
PARAMS = pltpu.CompilerParams(vmem_limit_bytes=40 * 1024 * 1024)


def mult(left, right, left_dim=1, right_dim=0):
    return lax.dot_general(
        left,
        right,
        (((left_dim,), (right_dim,)), ((), ())),
        precision=lax.Precision.HIGHEST,
        preferred_element_type=jnp.float32,
    )


def shape(*dims):
    return jax.ShapeDtypeStruct(dims, jnp.float32)


def cost(flops, nbytes):
    return pl.CostEstimate(flops=flops, bytes_accessed=nbytes, transcendentals=0)


def lane(block, k):
    return jnp.broadcast_to(block[:, k : k + 1], (SUB, NB))


def row(block, s):
    return jnp.broadcast_to(block[s : s + 1, :], (SUB, NB))


def lane_ids():
    sub_id = lax.broadcasted_iota(jnp.int32, (SUB, NB), 0)
    lane_id = lax.broadcasted_iota(jnp.int32, (SUB, NB), 1)
    return sub_id, lane_id


def inverse_factor(left):
    count = NB // SUB
    sub_id, lane_id = lane_ids()
    eye = [jnp.where(lane_id == sub_id + SUB * i, 1.0, 0.0) for i in range(count)]
    right = list(eye)
    for k in range(0, NB, 2):
        b, s = divmod(k, SUB)
        one, two = row(left[b], s), row(left[b], s + 1)
        eone, etwo = row(right[b], s), row(right[b], s + 1)
        a11, a12, a22 = lane(one, k), lane(one, k + 1), lane(two, k + 1)
        scale = 1.0 / (a11 * a22 - a12 * a12)
        i11, i12, i22 = a22 * scale, a12 * scale, a11 * scale
        p1, p2 = i11 * one - i12 * two, i22 * two - i12 * one
        q1, q2 = i11 * eone - i12 * etwo, i22 * etwo - i12 * eone
        for i in range(b, count):
            c1, c2 = lane(left[i], k), lane(left[i], k + 1)
            if i == b:
                c1 = jnp.where(sub_id > s + 1, c1, 0.0)
                c2 = jnp.where(sub_id > s + 1, c2, 0.0)
            left[i] = left[i] - c1 * p1 - c2 * p2
            right[i] = right[i] - c1 * q1 - c2 * q2
    odd = (sub_id % 2) == 1
    out = []
    for i in range(count):
        diag = jnp.sum(left[i] * eye[i], axis=1, keepdims=True)
        below = jnp.sum(jnp.where(lane_id == sub_id + (SUB * i - 1), left[i], 0.0), axis=1, keepdims=True)
        diag, below = jnp.broadcast_to(diag, (SUB, NB)), jnp.broadcast_to(below, (SUB, NB))
        ratio = jnp.where(odd, below / pltpu.roll(diag, 1, 0), 0.0)
        rows = right[i] - ratio * pltpu.roll(right[i], 1, 0)
        out.append(rows * lax.rsqrt(diag - ratio * below))
    return out


def invert_kernel(shift_ref, y_ref, out_ref, v_ref):
    count = NB // SUB
    sub_id, lane_id = lane_ids()
    held = [
        jnp.where(lane_id == sub_id + SUB * i, 1.0, 0.0) - shift_ref[SUB * i : SUB * i + SUB, :] for i in range(count)
    ]
    for k in range(0, NB, 2):
        b, s = divmod(k, SUB)
        one, two = row(held[b], s), row(held[b], s + 1)
        a11, a12, a21, a22 = lane(one, k), lane(one, k + 1), lane(two, k), lane(two, k + 1)
        scale = 1.0 / (a11 * a22 - a12 * a21)
        i11, i12, i21, i22 = a22 * scale, -a12 * scale, -a21 * scale, a11 * scale
        h1, h2 = lane_id == k, lane_id == k + 1
        o1 = jnp.where(h1, 1.0, jnp.where(h2, 0.0, one))
        o2 = jnp.where(h1, 0.0, jnp.where(h2, 1.0, two))
        n1, n2 = i11 * o1 + i12 * o2, i21 * o1 + i22 * o2
        for i in range(count):
            c1, c2 = lane(held[i], k), lane(held[i], k + 1)
            new = jnp.where(h1 | h2, 0.0, held[i]) - c1 * n1 - c2 * n2
            if i == b:
                new = jnp.where(sub_id == s, n1, jnp.where(sub_id == s + 1, n2, new))
            held[i] = new
    for i in range(count):
        out_ref[SUB * i : SUB * i + SUB, :] = held[i]
    v_ref[...] = mult(y_ref[...], out_ref[...])


def prepare_kernel(col_blocks, fold, slim, ids_ref, a_ref, send_ref):
    rows = a_ref.shape[0] // col_blocks
    col_count = send_ref.shape[0]
    share, step, per = fold * slim, NB // col_count, NB // slim
    panel = a_ref[pl.ds(0, rows, col_blocks), :]
    first = jnp.where(ids_ref[0] == 0, 0.0, panel[:NB])
    panel = jnp.concatenate([first, panel[NB:]], 0)
    gram = mult(panel, panel, 0, 0)
    lead = jnp.where(ids_ref[0] == 1, first, 0.0)
    for m in range(rows // NB):
        k, f = divmod(m, fold)
        send_ref[k * per : (k + 1) * per, f * slim : (f + 1) * slim, :] = panel[m * NB : (m + 1) * NB].reshape(per, slim, NB)
    for c in range(col_count):
        send_ref[c, share : share + step, :] = gram[c * step : (c + 1) * step]
        send_ref[c, share + step : share + 2 * step, :] = lead[c * step : (c + 1) * step]


def relay_kernel(fold, slim, ids_ref, got_ref, send_ref):
    row_count = got_ref.shape[0]
    share = fold * slim
    mine = got_ref[ids_ref[0], :share, :]
    piece = jnp.sum(got_ref[:, share:, :], 0)
    send_ref[:, :share, :] = jnp.broadcast_to(mine[None], (fold * row_count,) + mine.shape)
    send_ref[:, share + slim :, :] = jnp.broadcast_to(piece[None], (fold * row_count,) + piece.shape)
    for f in range(fold):
        send_ref[f * row_count : (f + 1) * row_count, share : share + slim, :] = got_ref[:, f * slim : (f + 1) * slim, :]


def factor_kernel(
    col_blocks, fold, slim, ids_ref, got_ref, a_ref, sign_shift_ref, y_ref, y_col_ref, send_ref, inv_ref, sign_ref, hold_ref, lead_ref
):
    col_count = got_ref.shape[0]
    rows, cols = a_ref.shape[0] // col_blocks, col_blocks * NB
    share, step, per = fold * slim, NB // col_count, NB // slim
    count = NB // SUB
    sub_id, lane_id = lane_ids()
    for c in range(col_count):
        hold_ref[c * step : (c + 1) * step, :] = got_ref[c, share + slim : share + slim + step, :]
        lead_ref[c * step : (c + 1) * step, :] = got_ref[c, share + slim + step : share + slim + 2 * step, :]
    out = inverse_factor([hold_ref[SUB * i : SUB * i + SUB, :] for i in range(count)])
    for i in range(count):
        inv_ref[SUB * i : SUB * i + SUB, :] = out[i]
    inverse = inv_ref[...]
    lead = lead_ref[...]
    signs = jnp.where(jnp.sum(lead * inverse, axis=1, keepdims=True) >= 0, -1.0, 1.0)
    sign_shift_ref[...] = signs * mult(lead, inverse, 1, 1)
    for i in range(count):
        here = jnp.where(lane_id == sub_id + SUB * i, 1.0, 0.0)
        sign_ref[SUB * i : SUB * i + SUB, :] = here * signs[SUB * i : SUB * i + SUB]
    y_col_ref[...] = mult(got_ref[:, share : share + slim, :].reshape(cols, NB), inverse, 1, 1)
    for m in range(rows // NB):
        k, f = divmod(m, fold)
        block = got_ref[k * per : (k + 1) * per, f * slim : (f + 1) * slim, :].reshape(NB, NB)
        y_ref[m * NB : (m + 1) * NB, :] = mult(block, inverse, 1, 1)

    @pl.when(ids_ref[0] == 1)
    def _():
        y_ref[:NB, :] = y_ref[:NB, :] - sign_ref[...]

    @pl.when(ids_ref[1] == 1)
    def _():
        y_col_ref[:NB, :] = y_col_ref[:NB, :] - sign_ref[...]

    part = jnp.zeros((rows, NB), jnp.float32)
    for k in range(col_blocks):
        part = part + mult(a_ref[pl.ds(k, rows, col_blocks), :], y_col_ref[k * NB : (k + 1) * NB, :])
    for m in range(rows // NB):
        k, f = divmod(m, fold)
        send_ref[k * per : (k + 1) * per, f * slim : (f + 1) * slim, :] = part[m * NB : (m + 1) * NB].reshape(per, slim, NB)
    hold_ref[...] = mult(y_ref[...], part, 0, 0)
    for c in range(col_count):
        send_ref[c, share : share + step, :] = hold_ref[c * step : (c + 1) * step, :]
        if send_ref.shape[1] > share + step:
            send_ref[c, share + step :, :] = jnp.zeros((send_ref.shape[1] - share - step, NB), jnp.float32)


def spread_kernel(got_ref, send_ref):
    total = jnp.sum(got_ref[...], 0)
    send_ref[...] = jnp.broadcast_to(total[None], send_ref.shape)


def update_kernel(col_blocks, fold, slim, got_ref, coupling_ref, v_ref, y_col_ref, y_ref, a_ref, out_ref, right_ref, hold_ref):
    col_count = got_ref.shape[0]
    share, step, per = fold * slim, NB // col_count, NB // slim
    at = pl.program_id(0)

    @pl.when(at == 0)
    def _():
        for c in range(col_count):
            hold_ref[c * step : (c + 1) * step, :] = got_ref[c, share + slim : share + slim + step, :]
        coupling = coupling_ref[...]
        inner = mult(mult(coupling, hold_ref[...]), coupling, 1, 1)
        z = got_ref[:, share : share + slim, :].reshape(col_blocks * NB, NB)
        right_ref[:, :NB] = mult(z, coupling, 1, 1) - mult(y_col_ref[...], inner)
        right_ref[:, NB:] = v_ref[...]

    for f in range(fold):
        z = got_ref[pl.ds(at * per, per), f * slim : (f + 1) * slim, :].reshape(NB, NB)
        y = y_ref[f * NB : (f + 1) * NB, :]
        change = mult(jnp.concatenate([y, z], 1), right_ref[...], 1, 1)
        for k in range(col_blocks):
            here = pl.ds(f * NB * col_blocks + k, NB, col_blocks)
            out_ref[here, :] = a_ref[here, :] - change[:, k * NB : (k + 1) * NB]


def exchange(pieces, axis):
    return lax.all_to_all(pieces, axis, 0, 0)


def body(kernel):
    row_blocks, _, _, col_blocks, _, _ = kernel.shape
    rows, cols = row_blocks * NB, col_blocks * NB
    row_count, col_count = lax.axis_size("row"), lax.axis_size("col")
    fold = col_count // row_count
    row_index, col_index = lax.axis_index("row"), lax.axis_index("col")
    ids = jnp.stack([row_index, col_index]).astype(jnp.int32)
    lines = kernel.reshape(rows * col_blocks, NB)
    slim, step = cols // col_count, NB // col_count
    share = fold * slim
    pad = 2 * step

    def relay(got):
        return pl.pallas_call(
            lambda *refs: relay_kernel(fold, slim, *refs),
            out_shape=shape(col_count, share + slim + pad, NB),
            in_specs=[SMEM, VMEM],
            out_specs=VMEM,
            compiler_params=PARAMS,
            name="relay",
            cost_estimate=cost(1_000_000, 1_000_000),
        )(ids, got)

    send = pl.pallas_call(
        lambda *refs: prepare_kernel(col_blocks, fold, slim, *refs),
        out_shape=shape(col_count, share + pad, NB),
        in_specs=[SMEM, VMEM],
        out_specs=VMEM,
        compiler_params=PARAMS,
        name="prepare",
        cost_estimate=cost(2 * rows * NB * NB * 6, 3_000_000),
    )(ids, lines)
    got = exchange(send, "col")[0]
    got = exchange(jnp.broadcast_to(got[None], (row_count,) + got.shape), "row")
    got = exchange(relay(got), "col")

    shift, y_rows, y_cols, send = pl.pallas_call(
        lambda *refs: factor_kernel(col_blocks, fold, slim, *refs),
        out_shape=(shape(NB, NB), shape(rows, NB), shape(cols, NB), shape(col_count, share + pad, NB)),
        in_specs=[SMEM, VMEM, VMEM],
        out_specs=(VMEM,) * 4,
        scratch_shapes=[pltpu.VMEM((NB, NB), jnp.float32)] * 4,
        compiler_params=PARAMS,
        name="factor",
        cost_estimate=cost(2 * rows * cols * NB * 6, 4_000_000),
    )(ids, got, lines)

    got = exchange(send, "col")
    send = pl.pallas_call(
        spread_kernel,
        out_shape=shape(row_count, share + pad, NB),
        in_specs=[VMEM],
        out_specs=VMEM,
        compiler_params=PARAMS,
        name="spread",
        cost_estimate=cost(1_000_000, 1_000_000),
    )(got)
    got = exchange(send, "row")
    coupling, v_cols = pl.pallas_call(
        invert_kernel,
        out_shape=(shape(NB, NB), shape(cols, NB)),
        in_specs=[VMEM, VMEM],
        out_specs=(VMEM, VMEM),
        compiler_params=PARAMS,
        name="invert",
        cost_estimate=cost(4_000_000_000, 1_000_000),
    )(shift, y_cols)
    got, coupling, v_cols = lax.optimization_barrier((got, coupling, v_cols))
    last = exchange(relay(got), "col")

    whole = lambda *dims: pl.BlockSpec(dims, lambda i: (0,) * len(dims))
    updated = pl.pallas_call(
        lambda *refs: update_kernel(col_blocks, fold, slim, *refs),
        grid=(row_blocks // fold,),
        out_shape=shape(rows * col_blocks, NB),
        in_specs=[
            whole(col_count, share + slim + pad, NB),
            whole(NB, NB),
            whole(cols, NB),
            whole(cols, NB),
            pl.BlockSpec((fold * NB, NB), lambda i: (i, 0)),
            pl.BlockSpec((fold * NB * col_blocks, NB), lambda i: (i, 0)),
        ],
        out_specs=pl.BlockSpec((fold * NB * col_blocks, NB), lambda i: (i, 0)),
        scratch_shapes=[pltpu.VMEM((cols, 2 * NB), jnp.float32), pltpu.VMEM((NB, NB), jnp.float32)],
        compiler_params=PARAMS,
        name="update",
        cost_estimate=cost(4 * rows * cols * NB * 6, 6_000_000),
    )(last, coupling, v_cols, y_cols, y_rows, lines)
    return updated.reshape(kernel.shape)


def solution(mesh):
    return jax.shard_map(
        body,
        mesh=mesh,
        in_specs=(P(None, "row", None, None, "col", None),),
        out_specs=P(None, "row", None, None, "col", None),
        check_vma=False,
    )
```

time: 197 us -> 167 us (0.85)
  starting transfers between devices: 30.7 us -> 5.61 us
  blocking collectives: 95.5 us -> 120 us
  waiting for transfers between devices: 25.4 us -> 3.62 us
  local copies, waits for them, and re-layouts: 8.3 us -> 2.46 us
    all_to_all x3 -> x1, starting transfers between devices: 30.7 us -> 5.61 us  [exchange(): return lax.all_to_all(pieces, axis, 0, 0)]
    all_to_all x4 -> x5, blocking collectives: 95.5 us -> 120 us  [exchange(): return lax.all_to_all(pieces, axis, 0, 0)]
    all_to_all x3 -> x1, waiting for transfers between devices: 25.4 us -> 3.62 us  [exchange(): return lax.all_to_all(pieces, axis, 0, 0)]
    unnamed x24 -> x8, local copies, waits for them, and re-layouts: 6.45 us -> 2.43 us
    pallas_call x6 -> x7, Pallas kernels: 34.9 us -> 35.1 us  [the longest x1 14.7 us: body(): pl.pallas_call(lambda *refs: factor_kernel(col_blocks, fold, slim, *refs)...]
  transfers between devices with their start and end apart: 3 -> 1, of which waited for: 3 -> 1; matrix products, arithmetic and copies ran while one was open for 0% -> 0% of each run, Pallas kernels for 6% -> 6%
where the time goes in v3:
time: 167 us
  blocking collectives  120 us (72%)
  Pallas kernels  35.1 us (21%)
  starting transfers between devices  5.61 us (3%)
  waiting for transfers between devices  3.62 us (2%)
  local copies, waits for them, and re-layouts  2.46 us (1%)
    all_to_all x5, blocking collectives, exchange(): return lax.all_to_all(pieces, axis, 0, 0)  120 us
    pallas_call x1, Pallas kernels, body(): pl.pallas_call(lambda *refs: factor_kernel(col_blocks, fold, slim, *refs)...  14.7 us
    pallas_call x1, Pallas kernels, body(): pl.pallas_call(invert_kernel, out_shape=(shape(NB, NB), shape(cols, NB)),...  10.7 us
    pallas_call x1, Pallas kernels, body(): pl.pallas_call(lambda *refs: update_kernel(col_blocks, fold, slim, *refs)...  6.5 us
    all_to_all x1, starting transfers between devices, exchange(): return lax.all_to_all(pieces, axis, 0, 0)  5.61 us
    all_to_all x1, waiting for transfers between devices, exchange(): return lax.all_to_all(pieces, axis, 0, 0)  3.62 us
  transfers between devices with their start and end apart: 1, of which 1 were waited for; matrix products, arithmetic and copies ran while one was open for 0% of the time, Pallas kernels for 6%

profile of v3, /device:TPU:1, one launch (start us, length us, event | category | flops | bytes accessed | tf_op | source)
XLA Modules:
  0.0 166.8 jit_solution(13889584058236480856)
XLA Ops:
  0.0 0.1 pad_add_fusion.refs_0_
  0.1 0.0 copy-start
  0.1 1.6 copy-done
  1.7 1.2 prepare.1
  2.9 22.5 %all_to_all.30 = f32[32,40,128]{2,1,0:T(8,128)S(1)} all-to-all(f32[32,40,128]{2,1,0:T(8,128)S(1)} %prepare.1), channel_id=1, replica_groups=mesh['row'=16,'col'=32] {'col'}, dimensions={0} | all-to-all | bytes 1310720 | tf_op jit(solution)/shard_map/all_to_all | solution.py:213
  25.4 0.0 copy-start.1
  25.4 28.8 %all_to_all.31.refs_1_ = f32[16,40,128]{2,1,0:T(8,128)S(1)} all-to-all(f32[16,40,128]{2,1,0:T(8,128)S(1)} %broadcast_in_dim.8), channel_id=1, replica_groups=mesh['row'=16,'col'=32] {'row'}, dimensions={0} | all-to-all | bytes 655360 | tf_op jit(solution)/shard_map/all_to_all | solution.py:213
  54.2 0.6 relay.2
  54.8 26.1 %all_to_all.32.refs_1_ = f32[32,56,128]{2,1,0:T(8,128)S(1)} all-to-all(f32[32,56,128]{2,1,0:T(8,128)S(1)} %relay.2), channel_id=1, replica_groups=mesh['row'=16,'col'=32] {'col'}, dimensions={0} | all-to-all | bytes 1835008 | tf_op jit(solution)/shard_map/all_to_all | solution.py:213
  80.9 0.0 copy-done.1
  80.9 14.7 %factor.1 = (f32[128,128]{1,0:T(8,128)S(1)}, f32[1024,128]{1,0:T(8,128)S(1)}, f32[512,128]{1,0:T(8,128)S(1)}, f32[32,40,128]{2,1,0:T(8,128)S(1)}) custom-call(s32[2]{0:T(128)S(1)} %pad_add_fusion.refs_0_, f32[32,56,128]{2,1,0:T(8,128)S(1)} %all_to_all.32.refs_1_, f32[4096,128]{1,0:T(8,128)S(1)} %bitcast.9), custom_call_target="tpu_custom_call" | custom-call | flops 805306368 | bytes 4000000 | tf_op jit(solution)/shard_map/factor/pallas_call | solution.py:252
  95.6 0.0 copy-start.2
  95.7 16.4 %all_to_all.33.got_ref = f32[32,40,128]{2,1,0:T(8,128)S(1)} all-to-all(f32[32,40,128]{2,1,0:T(8,128)S(1)} %get-tuple-element.14), channel_id=1, replica_groups=mesh['row'=16,'col'=32] {'col'}, dimensions={0} | all-to-all | bytes 1310720 | tf_op jit(solution)/shard_map/all_to_all | solution.py:213
  112.1 0.8 spread.1
  112.9 0.0 copy-done.2
  112.9 5.6 %all-to-all-start.4 = ((f32[16,40,128]{2,1,0:T(8,128)}), f32[16,40,128]{2,1,0:T(8,128)S(1)}, u32[]{:S(2)}, u32[]{:S(2)}) async-start(f32[16,40,128]{2,1,0:T(8,128)} %spread.1), calls=%async_computation.4 | async-start | bytes 655360 | tf_op jit(solution)/shard_map/all_to_all | solution.py:213
  118.5 0.0 copy-start.3
  118.5 0.8 copy-done.3
  119.3 10.7 %invert.1 = (f32[128,128]{1,0:T(8,128)S(1)}, f32[512,128]{1,0:T(8,128)S(1)}) custom-call(f32[128,128]{1,0:T(8,128)S(1)} %copy-done.3, f32[512,128]{1,0:T(8,128)S(1)} %get-tuple-element.16.y_ref.refs_3_), custom_call_target="tpu_custom_call" | custom-call | flops 4000000000 | bytes 1000000 | tf_op jit(solution)/shard_map/invert/pallas_call | solution.py:274
  130.0 3.6 %all-to-all-done.4.refs_1_ = f32[16,40,128]{2,1,0:T(8,128)S(1)} async-done(((f32[16,40,128]{2,1,0:T(8,128)}), f32[16,40,128]{2,1,0:T(8,128)S(1)}, u32[]{:S(2)}, u32[]{:S(2)}) %all-to-all-start.4) | async-done | bytes 327712 | tf_op jit(solution)/shard_map/all_to_all | solution.py:213
  133.7 0.6 relay.3
  134.3 26.1 %all_to_all.34.refs_0_ = f32[32,56,128]{2,1,0:T(8,128)S(1)} all-to-all(f32[32,56,128]{2,1,0:T(8,128)S(1)} %relay.3), channel_id=1, replica_groups=mesh['row'=16,'col'=32] {'col'}, dimensions={0} | all-to-all | bytes 1835008 | tf_op jit(solution)/shard_map/all_to_all | solution.py:213
  160.3 6.5 %update.1 = f32[4096,128]{1,0:T(8,128)} custom-call(f32[32,56,128]{2,1,0:T(8,128)S(1)} %all_to_all.34.refs_0_, f32[128,128]{1,0:T(8,128)S(1)} %get-tuple-element.20.refs_1_, f32[512,128]{1,0:T(8,128)S(1)} %get-tuple-element.21.refs_2_, f32[512,128]{1,0:T(8,128)S(1)} %get-tuple-element.16.y_ref.refs_3_, f32[1024,128]{1,0:T(8,128)S(1)} %get-tuple-element.22.refs_4_, ...), custom_call_target="tpu_custom_call" | custom-call | flops 1610612736 | bytes 6000000 | tf_op jit(solution)/shard_map/update/pallas_call | solution.py:287
  (2 shorter events, 0.0 us)
Async XLA Ops:
  0.1 1.6 copy-start
  25.4 55.5 %copy-start.1 = (f32[8,1,128,4,1,128]{5,4,3,2,1,0:T(1,128)S(1)}, f32[8,1,128,4,1,128]{5,4,3,2,1,0:T(1,128)}, u32[]{:S(2)}) copy-start(f32[8,1,128,4,1,128]{5,4,3,2,1,0:T(1,128)} %param.1) | copy-start | bytes 6291460
  95.6 17.2 %copy-start.2 = (f32[128,128]{1,0:T(8,128)}, f32[128,128]{1,0:T(8,128)S(1)}, u32[]{:S(2)}) copy-start(f32[128,128]{1,0:T(8,128)S(1)} %get-tuple-element.15.shift_ref) | copy-start | bytes 196612
  112.9 20.8 %all-to-all-start.4 = ((f32[16,40,128]{2,1,0:T(8,128)}), f32[16,40,128]{2,1,0:T(8,128)S(1)}, u32[]{:S(2)}, u32[]{:S(2)}) async-start(f32[16,40,128]{2,1,0:T(8,128)} %spread.1), calls=%async_computation.4 | async-start | bytes 655360 | tf_op jit(solution)/shard_map/all_to_all | solution.py:213
  118.5 0.8 copy-start.3

commit v4 on v3

--- a/solution.py
+++ b/solution.py
@@ -109,7 +109,7 @@
     col_count = send_ref.shape[0]
     share, step, per = fold * slim, NB // col_count, NB // slim
     panel = a_ref[pl.ds(0, rows, col_blocks), :]
-    first = jnp.where(ids_ref[0] == 0, 0.0, panel[:NB])
+    first = jnp.where((ids_ref[0] == 0) & (ids_ref[1] == 0), 0.0, panel[:NB])
     panel = jnp.concatenate([first, panel[NB:]], 0)
     gram = mult(panel, panel, 0, 0)
     lead = jnp.where(ids_ref[0] == 1, first, 0.0)
@@ -132,11 +132,28 @@
         send_ref[f * row_count : (f + 1) * row_count, share : share + slim, :] = got_ref[:, f * slim : (f + 1) * slim, :]
 
 
-def factor_kernel(
-    col_blocks, fold, slim, ids_ref, got_ref, a_ref, sign_shift_ref, y_ref, y_col_ref, send_ref, inv_ref, sign_ref, hold_ref, lead_ref
-):
+def product_kernel(col_blocks, fold, slim, ids_ref, got_ref, a_ref, send_ref, panel_ref, hold_ref):
     col_count = got_ref.shape[0]
     rows, cols = a_ref.shape[0] // col_blocks, col_blocks * NB
+    share, step, per = fold * slim, NB // col_count, NB // slim
+    panel_cols = got_ref[:, share : share + slim, :].reshape(cols, NB)
+    part = jnp.zeros((rows, NB), jnp.float32)
+    for k in range(col_blocks):
+        part = part + mult(a_ref[pl.ds(k, rows, col_blocks), :], panel_cols[k * NB : (k + 1) * NB])
+    for m in range(rows // NB):
+        k, f = divmod(m, fold)
+        panel_ref[m * NB : (m + 1) * NB, :] = got_ref[k * per : (k + 1) * per, f * slim : (f + 1) * slim, :].reshape(NB, NB)
+        send_ref[k * per : (k + 1) * per, f * slim : (f + 1) * slim, :] = part[m * NB : (m + 1) * NB].reshape(per, slim, NB)
+    hold_ref[...] = mult(panel_ref[...], part, 0, 0)
+    lead = jnp.where(ids_ref[0] == 1, part[:NB], 0.0)
+    for c in range(col_count):
+        send_ref[c, share : share + step, :] = hold_ref[c * step : (c + 1) * step, :]
+        send_ref[c, share + step : share + 2 * step, :] = lead[c * step : (c + 1) * step]
+
+
+def factor_kernel(col_blocks, fold, slim, ids_ref, got_ref, inv_ref, sign_ref, shift_ref, y_ref, y_col_ref, hold_ref, lead_ref):
+    col_count = got_ref.shape[0]
+    rows, cols = y_ref.shape[0], col_blocks * NB
     share, step, per = fold * slim, NB // col_count, NB // slim
     count = NB // SUB
     sub_id, lane_id = lane_ids()
@@ -149,7 +166,7 @@
     inverse = inv_ref[...]
     lead = lead_ref[...]
     signs = jnp.where(jnp.sum(lead * inverse, axis=1, keepdims=True) >= 0, -1.0, 1.0)
-    sign_shift_ref[...] = signs * mult(lead, inverse, 1, 1)
+    shift_ref[...] = signs * mult(lead, inverse, 1, 1)
     for i in range(count):
         here = jnp.where(lane_id == sub_id + SUB * i, 1.0, 0.0)
         sign_ref[SUB * i : SUB * i + SUB, :] = here * signs[SUB * i : SUB * i + SUB]
@@ -167,46 +184,61 @@
     def _():
         y_col_ref[:NB, :] = y_col_ref[:NB, :] - sign_ref[...]
 
-    part = jnp.zeros((rows, NB), jnp.float32)
-    for k in range(col_blocks):
-        part = part + mult(a_ref[pl.ds(k, rows, col_blocks), :], y_col_ref[k * NB : (k + 1) * NB, :])
-    for m in range(rows // NB):
-        k, f = divmod(m, fold)
-        send_ref[k * per : (k + 1) * per, f * slim : (f + 1) * slim, :] = part[m * NB : (m + 1) * NB].reshape(per, slim, NB)
-    hold_ref[...] = mult(y_ref[...], part, 0, 0)
-    for c in range(col_count):
-        send_ref[c, share : share + step, :] = hold_ref[c * step : (c + 1) * step, :]
-        if send_ref.shape[1] > share + step:
-            send_ref[c, share + step :, :] = jnp.zeros((send_ref.shape[1] - share - step, NB), jnp.float32)
-
-
-def spread_kernel(got_ref, send_ref):
+
+def spread_kernel(share, step, ids_ref, got_ref, own_ref, inv_ref, sign_ref, send_ref):
     total = jnp.sum(got_ref[...], 0)
-    send_ref[...] = jnp.broadcast_to(total[None], send_ref.shape)
-
-
-def update_kernel(col_blocks, fold, slim, got_ref, coupling_ref, v_ref, y_col_ref, y_ref, a_ref, out_ref, right_ref, hold_ref):
+    own = own_ref[...]
+    line = jnp.sum(sign_ref[...], axis=0, keepdims=True)
+    turned = mult(total, inv_ref[...], 1, 1)
+    rows = turned[:share] - own[:share] * line
+    lead = jnp.where(ids_ref[0] == 1, turned[share + step :] - 0.5 * own[share + step :] * line, 0.0)
+    out = jnp.concatenate([rows, total[share : share + step], lead], 0)
+    send_ref[...] = jnp.broadcast_to(out[None], send_ref.shape)
+
+
+def halves(value):
+    high = value.astype(jnp.bfloat16)
+    return high, (value - high.astype(jnp.float32)).astype(jnp.bfloat16)
+
+
+def mult_half(left, right):
+    return lax.dot_general(left, right, (((1,), (1,)), ((), ())), preferred_element_type=jnp.float32)
+
+
+def update_kernel(
+    col_blocks, fold, slim, got_ref, inv_ref, sign_ref, coupling_ref, v_ref, y_ref, a_ref, out_ref, high_ref, low_ref, hold_ref, lead_ref, new_ref, sems
+):
     col_count = got_ref.shape[0]
     share, step, per = fold * slim, NB // col_count, NB // slim
-    at = pl.program_id(0)
-
-    @pl.when(at == 0)
-    def _():
-        for c in range(col_count):
-            hold_ref[c * step : (c + 1) * step, :] = got_ref[c, share + slim : share + slim + step, :]
-        coupling = coupling_ref[...]
-        inner = mult(mult(coupling, hold_ref[...]), coupling, 1, 1)
-        z = got_ref[:, share : share + slim, :].reshape(col_blocks * NB, NB)
-        right_ref[:, :NB] = mult(z, coupling, 1, 1) - mult(y_col_ref[...], inner)
-        right_ref[:, NB:] = v_ref[...]
-
-    for f in range(fold):
-        z = got_ref[pl.ds(at * per, per), f * slim : (f + 1) * slim, :].reshape(NB, NB)
-        y = y_ref[f * NB : (f + 1) * NB, :]
-        change = mult(jnp.concatenate([y, z], 1), right_ref[...], 1, 1)
-        for k in range(col_blocks):
-            here = pl.ds(f * NB * col_blocks + k, NB, col_blocks)
-            out_ref[here, :] = a_ref[here, :] - change[:, k * NB : (k + 1) * NB]
+    cols = col_blocks * NB
+    for c in range(col_count):
+        hold_ref[c * step : (c + 1) * step, :] = got_ref[c, share + slim : share + slim + step, :]
+        lead_ref[c * step : (c + 1) * step, :] = got_ref[c, share + slim + step : share + slim + 2 * step, :]
+    inverse, v = inv_ref[...], v_ref[...]
+    cross = jnp.sum(sign_ref[...], axis=1, keepdims=True) * lead_ref[...]
+    middle = mult(mult(inverse, hold_ref[...]), inverse, 1, 1) - cross - cross.T
+    z_cols = got_ref[:, share : share + slim, :].reshape(cols, NB)
+    u = mult(z_cols - mult(v, middle), coupling_ref[...], 1, 1)
+    for at, part in enumerate((u, v)):
+        high, low = halves(part)
+        high_ref[:, at * NB : (at + 1) * NB] = high
+        low_ref[:, at * NB : (at + 1) * NB] = low
+    right_high, right_low = high_ref[...], low_ref[...]
+    copies = []
+    for m in range(y_ref.shape[0] // NB):
+        k, f = divmod(m, fold)
+        z = got_ref[k * per : (k + 1) * per, f * slim : (f + 1) * slim, :].reshape(NB, NB)
+        high, low = halves(jnp.concatenate([y_ref[m * NB : (m + 1) * NB, :], z], 1))
+        change = mult_half(low, right_high) + mult_half(high, right_low) + mult_half(high, right_high)
+        for n in range(col_blocks):
+            here = pl.ds(m * NB * col_blocks + n, NB, col_blocks)
+            new_ref[here, :] = a_ref[here, :] - change[:, n * NB : (n + 1) * NB]
+        there = pl.ds(m * NB * col_blocks, NB * col_blocks)
+        copy = pltpu.make_async_copy(new_ref.at[there, :], out_ref.at[there, :], sems.at[m])
+        copy.start()
+        copies.append(copy)
+    for copy in copies:
+        copy.wait()
 
 
 def exchange(pieces, axis):
@@ -245,31 +277,42 @@
         name="prepare",
         cost_estimate=cost(2 * rows * NB * NB * 6, 3_000_000),
     )(ids, lines)
-    got = exchange(send, "col")[0]
-    got = exchange(jnp.broadcast_to(got[None], (row_count,) + got.shape), "row")
-    got = exchange(relay(got), "col")
-
-    shift, y_rows, y_cols, send = pl.pallas_call(
-        lambda *refs: factor_kernel(col_blocks, fold, slim, *refs),
-        out_shape=(shape(NB, NB), shape(rows, NB), shape(cols, NB), shape(col_count, share + pad, NB)),
+    got = exchange(send, "col")
+    own = got[1]
+    got = jnp.broadcast_to(got[0][None], (row_count,) + got.shape[1:])
+    got = exchange(relay(exchange(got, "row")), "col")
+
+    send = pl.pallas_call(
+        lambda *refs: product_kernel(col_blocks, fold, slim, *refs),
+        out_shape=shape(col_count, share + pad, NB),
         in_specs=[SMEM, VMEM, VMEM],
-        out_specs=(VMEM,) * 4,
-        scratch_shapes=[pltpu.VMEM((NB, NB), jnp.float32)] * 4,
-        compiler_params=PARAMS,
-        name="factor",
+        out_specs=VMEM,
+        scratch_shapes=[pltpu.VMEM((rows, NB), jnp.float32), pltpu.VMEM((NB, NB), jnp.float32)],
+        compiler_params=PARAMS,
+        name="product",
         cost_estimate=cost(2 * rows * cols * NB * 6, 4_000_000),
     )(ids, got, lines)
-
-    got = exchange(send, "col")
+    summed = exchange(send, "col")
+    inverse, sign, shift, y_rows, y_cols = pl.pallas_call(
+        lambda *refs: factor_kernel(col_blocks, fold, slim, *refs),
+        out_shape=(shape(NB, NB), shape(NB, NB), shape(NB, NB), shape(rows, NB), shape(cols, NB)),
+        in_specs=[SMEM, VMEM],
+        out_specs=(VMEM,) * 5,
+        scratch_shapes=[pltpu.VMEM((NB, NB), jnp.float32)] * 2,
+        compiler_params=PARAMS,
+        name="factor",
+        cost_estimate=cost(4_000_000_000, 2_000_000),
+    )(ids, got)
+
     send = pl.pallas_call(
-        spread_kernel,
+        lambda *refs: spread_kernel(share, step, *refs),
         out_shape=shape(row_count, share + pad, NB),
-        in_specs=[VMEM],
+        in_specs=[SMEM] + [VMEM] * 4,
         out_specs=VMEM,
         compiler_params=PARAMS,
         name="spread",
-        cost_estimate=cost(1_000_000, 1_000_000),
-    )(got)
+        cost_estimate=cost(10_000_000, 1_000_000),
+    )(ids, summed, own, inverse, sign)
     got = exchange(send, "row")
     coupling, v_cols = pl.pallas_call(
         invert_kernel,
@@ -283,25 +326,23 @@
     got, coupling, v_cols = lax.optimization_barrier((got, coupling, v_cols))
     last = exchange(relay(got), "col")
 
-    whole = lambda *dims: pl.BlockSpec(dims, lambda i: (0,) * len(dims))
     updated = pl.pallas_call(
         lambda *refs: update_kernel(col_blocks, fold, slim, *refs),
-        grid=(row_blocks // fold,),
         out_shape=shape(rows * col_blocks, NB),
-        in_specs=[
-            whole(col_count, share + slim + pad, NB),
-            whole(NB, NB),
-            whole(cols, NB),
-            whole(cols, NB),
-            pl.BlockSpec((fold * NB, NB), lambda i: (i, 0)),
-            pl.BlockSpec((fold * NB * col_blocks, NB), lambda i: (i, 0)),
+        in_specs=[VMEM] * 7,
+        out_specs=pl.BlockSpec(memory_space=pl.ANY),
+        scratch_shapes=[
+            pltpu.VMEM((cols, 2 * NB), jnp.bfloat16),
+            pltpu.VMEM((cols, 2 * NB), jnp.bfloat16),
+            pltpu.VMEM((NB, NB), jnp.float32),
+            pltpu.VMEM((NB, NB), jnp.float32),
+            pltpu.VMEM((rows * col_blocks, NB), jnp.float32),
+            pltpu.SemaphoreType.DMA((row_blocks,)),
         ],
-        out_specs=pl.BlockSpec((fold * NB * col_blocks, NB), lambda i: (i, 0)),
-        scratch_shapes=[pltpu.VMEM((cols, 2 * NB), jnp.float32), pltpu.VMEM((NB, NB), jnp.float32)],
         compiler_params=PARAMS,
         name="update",
         cost_estimate=cost(4 * rows * cols * NB * 6, 6_000_000),
-    )(last, coupling, v_cols, y_cols, y_rows, lines)
+    )(last, inverse, sign, coupling, v_cols, y_rows, lines)
     return updated.reshape(kernel.shape)
 
 

time: 167 us -> 165 us (0.988)
  blocking collectives: 120 us -> 107 us
  local copies, waits for them, and re-layouts: 2.46 us -> 9.82 us
  starting transfers between devices: 5.61 us -> 10.2 us
    all_to_all x5 -> x4, blocking collectives: 120 us -> 107 us  [exchange(): return lax.all_to_all(pieces, axis, 0, 0)]
    unnamed x8 -> x28, local copies, waits for them, and re-layouts: 2.43 us -> 9.19 us
    pallas_call x1 -> x2, Pallas kernels: 0.78 us -> 5.72 us  [the longest x1 3.65 us: body(): pl.pallas_call(lambda *refs: product_kernel(col_blocks, fold, slim, *refs...]
    all_to_all x1 -> x2, starting transfers between devices: 5.61 us -> 10.2 us  [exchange(): return lax.all_to_all(pieces, axis, 0, 0)]
    pallas_call x1, Pallas kernels: 14.7 us -> 11.5 us  [body(): pl.pallas_call(lambda *refs: factor_kernel(col_blocks, fold, slim, *refs)...]
    pallas_call x1, Pallas kernels: 6.5 us -> 4.53 us  [body(): pl.pallas_call(lambda *refs: update_kernel(col_blocks, fold, slim, *refs)...]
    all_to_all x1 -> x2, waiting for transfers between devices: 3.62 us -> 2.68 us  [exchange(): return lax.all_to_all(pieces, axis, 0, 0)]
  transfers between devices with their start and end apart: 1 -> 2, of which waited for: 1 -> 1; matrix products, arithmetic and copies ran while one was open for 0% -> 0% of each run, Pallas kernels for 6% -> 13%
where the time goes in v4:
time: 165 us
  blocking collectives  107 us (65%)
  Pallas kernels  34.8 us (21%)
  starting transfers between devices  10.2 us (6%)
  local copies, waits for them, and re-layouts  9.82 us (6%)
  waiting for transfers between devices  2.68 us (2%)
    all_to_all x4, blocking collectives, exchange(): return lax.all_to_all(pieces, axis, 0, 0)  107 us
    pallas_call x1, Pallas kernels, body(): pl.pallas_call(lambda *refs: factor_kernel(col_blocks, fold, slim, *refs)...  11.5 us
    pallas_call x1, Pallas kernels, body(): pl.pallas_call(invert_kernel, out_shape=(shape(NB, NB), shape(cols, NB)),...  10.7 us
    all_to_all x2, starting transfers between devices, exchange(): return lax.all_to_all(pieces, axis, 0, 0)  10.2 us
    unnamed x28, local copies, waits for them, and re-layouts  9.19 us
    pallas_call x1, Pallas kernels, body(): pl.pallas_call(lambda *refs: update_kernel(col_blocks, fold, slim, *refs)...  4.53 us
    pallas_call x1, Pallas kernels, body(): pl.pallas_call(lambda *refs: product_kernel(col_blocks, fold, slim, *refs...  3.65 us
  transfers between devices with their start and end apart: 2, of which 1 were waited for; matrix products, arithmetic and copies ran while one was open for 0% of the time, Pallas kernels for 13%

profile of v4, /device:TPU:1, one launch (start us, length us, event | category | flops | bytes accessed | tf_op | source)
XLA Modules:
  0.0 164.6 jit_solution(7461730064360225915)
XLA Ops:
  0.0 0.1 pad_add_fusion.refs_0_
  0.1 1.6 copy-done
  1.7 1.2 prepare.1
  2.9 22.5 %all_to_all.30 = f32[32,40,128]{2,1,0:T(8,128)S(1)} all-to-all(f32[32,40,128]{2,1,0:T(8,128)S(1)} %prepare.1), channel_id=1, replica_groups=mesh['row'=16,'col'=32] {'col'}, dimensions={0} | all-to-all | bytes 1310720 | tf_op jit(solution)/shard_map/all_to_all | solution.py:245
  25.4 0.6 slice_bitcast_fusion
  26.0 28.6 %all_to_all.31.refs_1_ = f32[16,40,128]{2,1,0:T(8,128)S(1)} all-to-all(f32[16,40,128]{2,1,0:T(8,128)S(1)} %broadcast_in_dim.8), channel_id=1, replica_groups=mesh['row'=16,'col'=32] {'row'}, dimensions={0} | all-to-all | bytes 655360 | tf_op jit(solution)/shard_map/all_to_all | solution.py:245
  54.7 0.6 relay.2
  55.3 26.1 %all_to_all.32.refs_1_ = f32[32,56,128]{2,1,0:T(8,128)S(1)} all-to-all(f32[32,56,128]{2,1,0:T(8,128)S(1)} %relay.2), channel_id=1, replica_groups=mesh['row'=16,'col'=32] {'col'}, dimensions={0} | all-to-all | bytes 1835008 | tf_op jit(solution)/shard_map/all_to_all | solution.py:245
  81.4 0.0 copy-done.1
  81.4 3.7 %product.1 = f32[32,40,128]{2,1,0:T(8,128)S(1)} custom-call(s32[2]{0:T(128)S(1)} %pad_add_fusion.refs_0_, f32[32,56,128]{2,1,0:T(8,128)S(1)} %all_to_all.32.refs_1_, f32[4096,128]{1,0:T(8,128)S(1)} %bitcast.11), custom_call_target="tpu_custom_call" | custom-call | flops 805306368 | bytes 4000000 | tf_op jit(solution)/shard_map/product/pallas_call | solution.py:285
  85.0 0.0 copy-start.2
  85.0 0.8 copy-done.2
  85.9 4.6 %all-to-all-start.3 = ((f32[32,40,128]{2,1,0:T(8,128)}), f32[32,40,128]{2,1,0:T(8,128)}, u32[]{:S(2)}, u32[]{:S(2)}) async-start(f32[32,40,128]{2,1,0:T(8,128)} %copy-done.2), calls=%async_computation.3 | async-start | bytes 1310720 | tf_op jit(solution)/shard_map/all_to_all | solution.py:245
  90.5 11.5 %factor.1 = (f32[128,128]{1,0:T(8,128)S(1)}, f32[128,128]{1,0:T(8,128)S(1)}, f32[128,128]{1,0:T(8,128)S(1)}, f32[1024,128]{1,0:T(8,128)S(1)}, f32[512,128]{1,0:T(8,128)S(1)}) custom-call(s32[2]{0:T(128)S(1)} %pad_add_fusion.refs_0_, f32[32,56,128]{2,1,0:T(8,128)S(1)} %all_to_all.32.refs_1_), custom_call_target="tpu_custom_call" | custom-call | flops 4000000000 | bytes 2000000 | tf_op jit(solution)/shard_map/factor/pallas_call | solution.py:296
  101.9 0.0 copy-start.3
  102.0 0.6 copy-done.3
  102.6 0.6 copy-done.6
  103.2 0.7 copy-done.10
  103.9 0.6 copy-done.12
  104.5 0.0 all-to-all-done.3.refs_1_
  104.5 0.8 copy-done.4
  105.4 0.8 copy-done.7
  106.2 0.7 copy-done.9
  106.9 2.1 %spread.1 = f32[16,40,128]{2,1,0:T(8,128)} custom-call(s32[2]{0:T(128)S(1)} %pad_add_fusion.refs_0_, f32[32,40,128]{2,1,0:T(8,128)} %all-to-all-done.3.refs_1_, f32[40,128]{1,0:T(8,128)S(1)} %copy-done.9, f32[128,128]{1,0:T(8,128)S(1)} %copy-done.4, f32[128,128]{1,0:T(8,128)S(1)} %copy-done.7), custom_call_target="tpu_custom_call" | custom-call | flops 10000000 | bytes 1000000 | tf_op jit(solution)/shard_map/spread/pallas_call | solution.py:307
  109.0 5.6 %all-to-all-start.4 = ((f32[16,40,128]{2,1,0:T(8,128)}), f32[16,40,128]{2,1,0:T(8,128)S(1)}, u32[]{:S(2)}, u32[]{:S(2)}) async-start(f32[16,40,128]{2,1,0:T(8,128)} %spread.1), calls=%async_computation.4 | async-start | bytes 655360 | tf_op jit(solution)/shard_map/all_to_all | solution.py:245
  114.6 0.9 copy-done.11
  115.6 0.8 copy-done.13
  116.4 10.7 %invert.1 = (f32[128,128]{1,0:T(8,128)S(1)}, f32[512,128]{1,0:T(8,128)S(1)}) custom-call(f32[128,128]{1,0:T(8,128)S(1)} %copy-done.13, f32[512,128]{1,0:T(8,128)S(1)} %copy-done.11), custom_call_target="tpu_custom_call" | custom-call | flops 4000000000 | bytes 1000000 | tf_op jit(solution)/shard_map/invert/pallas_call | solution.py:317
  127.1 2.7 %all-to-all-done.4.refs_1_ = f32[16,40,128]{2,1,0:T(8,128)S(1)} async-done(((f32[16,40,128]{2,1,0:T(8,128)}), f32[16,40,128]{2,1,0:T(8,128)S(1)}, u32[]{:S(2)}, u32[]{:S(2)}) %all-to-all-start.4) | async-done | bytes 327712 | tf_op jit(solution)/shard_map/all_to_all | solution.py:245
  129.8 0.6 relay.3
  130.4 29.5 %all_to_all.33.refs_0_ = f32[32,56,128]{2,1,0:T(8,128)S(1)} all-to-all(f32[32,56,128]{2,1,0:T(8,128)S(1)} %relay.3), channel_id=1, replica_groups=mesh['row'=16,'col'=32] {'col'}, dimensions={0} | all-to-all | bytes 1835008 | tf_op jit(solution)/shard_map/all_to_all | solution.py:245
  159.9 4.5 %update.1 = f32[4096,128]{1,0:T(8,128)} custom-call(f32[32,56,128]{2,1,0:T(8,128)S(1)} %all_to_all.33.refs_0_, f32[128,128]{1,0:T(8,128)S(1)} %copy-done.5, f32[128,128]{1,0:T(8,128)S(1)} %copy-done.8, f32[128,128]{1,0:T(8,128)S(1)} %get-tuple-element.22.refs_3_, f32[512,128]{1,0:T(8,128)S(1)} %get-tuple-element.23.refs_4_, ...), custom_call_target="tpu_custom_call" | custom-call | flops 1610612736 | bytes 6000000 | tf_op jit(solution)/shard_map/update/pallas_call | solution.py:329
  (15 shorter events, 0.0 us)
Async XLA Ops:
  0.1 1.6 copy-start
  25.4 56.0 %copy-start.1 = (f32[8,1,128,4,1,128]{5,4,3,2,1,0:T(1,128)S(1)}, f32[8,1,128,4,1,128]{5,4,3,2,1,0:T(1,128)}, u32[]{:S(2)}) copy-start(f32[8,1,128,4,1,128]{5,4,3,2,1,0:T(1,128)} %param.1) | copy-start | bytes 6291460
  85.0 0.8 copy-start.2
  85.9 18.7 %all-to-all-start.3 = ((f32[32,40,128]{2,1,0:T(8,128)}), f32[32,40,128]{2,1,0:T(8,128)}, u32[]{:S(2)}, u32[]{:S(2)}) async-start(f32[32,40,128]{2,1,0:T(8,128)} %copy-done.2), calls=%async_computation.3 | async-start | bytes 1310720 | tf_op jit(solution)/shard_map/all_to_all | solution.py:245
  101.9 0.6 copy-start.3
  102.6 0.6 copy-start.6
  103.2 0.7 copy-start.10
  103.9 0.6 copy-start.12
  104.5 0.8 copy-start.4
  105.4 0.8 copy-start.7
  106.2 0.7 copy-start.9
  109.0 20.8 %all-to-all-start.4 = ((f32[16,40,128]{2,1,0:T(8,128)}), f32[16,40,128]{2,1,0:T(8,128)S(1)}, u32[]{:S(2)}, u32[]{:S(2)}) async-start(f32[16,40,128]{2,1,0:T(8,128)} %spread.1), calls=%async_computation.4 | async-start | bytes 655360 | tf_op jit(solution)/shard_map/all_to_all | solution.py:245
  114.6 1.0 copy-start.11
  115.6 0.8 copy-start.13
  127.1 32.8 %copy-start.5 = (f32[128,128]{1,0:T(8,128)S(1)}, f32[128,128]{1,0:T(8,128)}, u32[]{:S(2)}) copy-start(f32[128,128]{1,0:T(8,128)} %copy-done.3) | copy-start | bytes 196612
  127.1 32.8 %copy-start.8 = (f32[128,128]{1,0:T(8,128)S(1)}, f32[128,128]{1,0:T(8,128)}, u32[]{:S(2)}) copy-start(f32[128,128]{1,0:T(8,128)} %copy-done.6) | copy-start | bytes 196612

commit v5 on v4

--- a/solution.py
+++ b/solution.py
@@ -9,6 +9,7 @@
 SUB = 8
 VMEM = pl.BlockSpec(memory_space=pltpu.VMEM)
 SMEM = pl.BlockSpec(memory_space=pltpu.SMEM)
+HBM = pl.BlockSpec(memory_space=pltpu.HBM)
 PARAMS = pltpu.CompilerParams(vmem_limit_bytes=40 * 1024 * 1024)
 
 
@@ -49,22 +50,38 @@
     sub_id, lane_id = lane_ids()
     eye = [jnp.where(lane_id == sub_id + SUB * i, 1.0, 0.0) for i in range(count)]
     right = list(eye)
-    for k in range(0, NB, 2):
+    for k in range(0, NB, 4):
         b, s = divmod(k, SUB)
-        one, two = row(left[b], s), row(left[b], s + 1)
-        eone, etwo = row(right[b], s), row(right[b], s + 1)
-        a11, a12, a22 = lane(one, k), lane(one, k + 1), lane(two, k + 1)
-        scale = 1.0 / (a11 * a22 - a12 * a12)
-        i11, i12, i22 = a22 * scale, a12 * scale, a11 * scale
-        p1, p2 = i11 * one - i12 * two, i22 * two - i12 * one
-        q1, q2 = i11 * eone - i12 * etwo, i22 * etwo - i12 * eone
+        r = [row(left[b], s + j) for j in range(4)]
+        e = [row(right[b], s + j) for j in range(4)]
+        a = [[lane(r[i], k + j) if j >= i else None for j in range(4)] for i in range(4)]
+        scale = 1.0 / (a[0][0] * a[1][1] - a[0][1] * a[0][1])
+        i00, i01, i11 = a[1][1] * scale, -a[0][1] * scale, a[0][0] * scale
+        t = [(i00 * a[0][j] + i01 * a[1][j], i01 * a[0][j] + i11 * a[1][j]) for j in (2, 3)]
+        s22 = a[2][2] - t[0][0] * a[0][2] - t[0][1] * a[1][2]
+        s23 = a[2][3] - t[0][0] * a[0][3] - t[0][1] * a[1][3]
+        s33 = a[3][3] - t[1][0] * a[0][3] - t[1][1] * a[1][3]
+        scale = 1.0 / (s22 * s33 - s23 * s23)
+        j22, j23, j33 = s33 * scale, -s23 * scale, s22 * scale
+
+        def rank(x):
+            x2 = x[2] - t[0][0] * x[0] - t[0][1] * x[1]
+            x3 = x[3] - t[1][0] * x[0] - t[1][1] * x[1]
+            q2, q3 = j22 * x2 + j23 * x3, j23 * x2 + j33 * x3
+            u0 = i00 * x[0] + i01 * x[1] - t[0][0] * q2 - t[1][0] * q3
+            u1 = i01 * x[0] + i11 * x[1] - t[0][1] * q2 - t[1][1] * q3
+            return x2, x3, (u0, u1, q2, q3)
+
+        l2, l3, lu = rank(r)
+        e2, e3, eu = rank(e)
         for i in range(b, count):
-            c1, c2 = lane(left[i], k), lane(left[i], k + 1)
+            c = [lane(left[i], k + j) for j in range(4)]
             if i == b:
-                c1 = jnp.where(sub_id > s + 1, c1, 0.0)
-                c2 = jnp.where(sub_id > s + 1, c2, 0.0)
-            left[i] = left[i] - c1 * p1 - c2 * p2
-            right[i] = right[i] - c1 * q1 - c2 * q2
+                c = [jnp.where(sub_id > s + 3, x, 0.0) for x in c]
+            left[i] = left[i] - (c[0] * lu[0] + c[1] * lu[1]) - (c[2] * lu[2] + c[3] * lu[3])
+            right[i] = right[i] - (c[0] * eu[0] + c[1] * eu[1]) - (c[2] * eu[2] + c[3] * eu[3])
+        left[b] = jnp.where(sub_id == s + 2, l2, jnp.where(sub_id == s + 3, l3, left[b]))
+        right[b] = jnp.where(sub_id == s + 2, e2, jnp.where(sub_id == s + 3, e3, right[b]))
     odd = (sub_id % 2) == 1
     out = []
     for i in range(count):
@@ -77,11 +94,23 @@
     return out
 
 
-def invert_kernel(shift_ref, y_ref, out_ref, v_ref):
+def fetch(copies):
+    for copy in copies:
+        copy.start()
+    for copy in copies:
+        copy.wait()
+
+
+def invert_kernel(rows, cols, ids_ref, state_hbm, panel_hbm, pack_ref, state_ref, panel_ref, sems):
+    get_state = pltpu.make_async_copy(state_hbm, state_ref, sems.at[0])
+    get_panel = pltpu.make_async_copy(panel_hbm, panel_ref, sems.at[1])
+    get_state.start()
+    get_panel.start()
+    get_state.wait()
     count = NB // SUB
     sub_id, lane_id = lane_ids()
     held = [
-        jnp.where(lane_id == sub_id + SUB * i, 1.0, 0.0) - shift_ref[SUB * i : SUB * i + SUB, :] for i in range(count)
+        jnp.where(lane_id == sub_id + SUB * i, 1.0, 0.0) - state_ref[2 * NB + SUB * i : 2 * NB + SUB * i + SUB, :] for i in range(count)
     ]
     for k in range(0, NB, 2):
         b, s = divmod(k, SUB)
@@ -100,8 +129,15 @@
                 new = jnp.where(sub_id == s, n1, jnp.where(sub_id == s + 1, n2, new))
             held[i] = new
     for i in range(count):
-        out_ref[SUB * i : SUB * i + SUB, :] = held[i]
-    v_ref[...] = mult(y_ref[...], out_ref[...])
+        pack_ref[SUB * i : SUB * i + SUB, :] = held[i]
+    pack_ref[NB : 3 * NB, :] = state_ref[: 2 * NB, :]
+    get_panel.wait()
+    inverse, sign = state_ref[:NB, :], state_ref[NB : 2 * NB, :]
+    y = mult(panel_ref[...], inverse, 1, 1)
+    y_cols = jnp.concatenate([y[rows : rows + NB] - jnp.where(ids_ref[1] == 1, sign, 0.0), y[rows + NB :]], 0)
+    pack_ref[3 * NB : 3 * NB + cols, :] = mult(y_cols, pack_ref[:NB, :])
+    pack_ref[3 * NB + cols : 4 * NB + cols, :] = y[:NB] - jnp.where(ids_ref[0] == 1, sign, 0.0)
+    pack_ref[4 * NB + cols :, :] = y[NB:rows]
 
 
 def prepare_kernel(col_blocks, fold, slim, ids_ref, a_ref, send_ref):
@@ -132,64 +168,67 @@
         send_ref[f * row_count : (f + 1) * row_count, share : share + slim, :] = got_ref[:, f * slim : (f + 1) * slim, :]
 
 
-def product_kernel(col_blocks, fold, slim, ids_ref, got_ref, a_ref, send_ref, panel_ref, hold_ref):
+def product_kernel(col_blocks, fold, slim, ids_ref, got_ref, a_ref, send_hbm, panel_hbm, send_ref, panel_ref, hold_ref, sems):
     col_count = got_ref.shape[0]
     rows, cols = a_ref.shape[0] // col_blocks, col_blocks * NB
     share, step, per = fold * slim, NB // col_count, NB // slim
-    panel_cols = got_ref[:, share : share + slim, :].reshape(cols, NB)
-    part = jnp.zeros((rows, NB), jnp.float32)
-    for k in range(col_blocks):
-        part = part + mult(a_ref[pl.ds(k, rows, col_blocks), :], panel_cols[k * NB : (k + 1) * NB])
+    panel_ref[rows:, :] = got_ref[:, share : share + slim, :].reshape(cols, NB)
     for m in range(rows // NB):
         k, f = divmod(m, fold)
         panel_ref[m * NB : (m + 1) * NB, :] = got_ref[k * per : (k + 1) * per, f * slim : (f + 1) * slim, :].reshape(NB, NB)
+    put_panel = pltpu.make_async_copy(panel_ref, panel_hbm, sems.at[0])
+    put_panel.start()
+    part = jnp.zeros((rows, NB), jnp.float32)
+    for k in range(col_blocks):
+        part = part + mult(a_ref[pl.ds(k, rows, col_blocks), :], panel_ref[rows + k * NB : rows + (k + 1) * NB, :])
+    for m in range(rows // NB):
+        k, f = divmod(m, fold)
         send_ref[k * per : (k + 1) * per, f * slim : (f + 1) * slim, :] = part[m * NB : (m + 1) * NB].reshape(per, slim, NB)
-    hold_ref[...] = mult(panel_ref[...], part, 0, 0)
+    put_share = pltpu.make_async_copy(send_ref.at[:, :share, :], send_hbm.at[:, :share, :], sems.at[1])
+    put_share.start()
+    hold_ref[...] = mult(panel_ref[:rows, :], part, 0, 0)
     lead = jnp.where(ids_ref[0] == 1, part[:NB], 0.0)
     for c in range(col_count):
         send_ref[c, share : share + step, :] = hold_ref[c * step : (c + 1) * step, :]
         send_ref[c, share + step : share + 2 * step, :] = lead[c * step : (c + 1) * step]
-
-
-def factor_kernel(col_blocks, fold, slim, ids_ref, got_ref, inv_ref, sign_ref, shift_ref, y_ref, y_col_ref, hold_ref, lead_ref):
-    col_count = got_ref.shape[0]
-    rows, cols = y_ref.shape[0], col_blocks * NB
-    share, step, per = fold * slim, NB // col_count, NB // slim
+    put_piece = pltpu.make_async_copy(send_ref.at[:, share:, :], send_hbm.at[:, share:, :], sems.at[2])
+    put_piece.start()
+    put_panel.wait()
+    put_share.wait()
+    put_piece.wait()
+
+
+def factor_kernel(share, step, got_ref, state_hbm, state_ref, hold_ref, lead_ref, sem):
     count = NB // SUB
     sub_id, lane_id = lane_ids()
-    for c in range(col_count):
-        hold_ref[c * step : (c + 1) * step, :] = got_ref[c, share + slim : share + slim + step, :]
-        lead_ref[c * step : (c + 1) * step, :] = got_ref[c, share + slim + step : share + slim + 2 * step, :]
+    for c in range(got_ref.shape[0]):
+        hold_ref[c * step : (c + 1) * step, :] = got_ref[c, share : share + step, :]
+        lead_ref[c * step : (c + 1) * step, :] = got_ref[c, share + step : share + 2 * step, :]
     out = inverse_factor([hold_ref[SUB * i : SUB * i + SUB, :] for i in range(count)])
     for i in range(count):
-        inv_ref[SUB * i : SUB * i + SUB, :] = out[i]
-    inverse = inv_ref[...]
+        state_ref[SUB * i : SUB * i + SUB, :] = out[i]
+    inverse = state_ref[:NB, :]
     lead = lead_ref[...]
     signs = jnp.where(jnp.sum(lead * inverse, axis=1, keepdims=True) >= 0, -1.0, 1.0)
-    shift_ref[...] = signs * mult(lead, inverse, 1, 1)
+    state_ref[2 * NB :, :] = signs * mult(lead, inverse, 1, 1)
     for i in range(count):
         here = jnp.where(lane_id == sub_id + SUB * i, 1.0, 0.0)
-        sign_ref[SUB * i : SUB * i + SUB, :] = here * signs[SUB * i : SUB * i + SUB]
-    y_col_ref[...] = mult(got_ref[:, share : share + slim, :].reshape(cols, NB), inverse, 1, 1)
-    for m in range(rows // NB):
-        k, f = divmod(m, fold)
-        block = got_ref[k * per : (k + 1) * per, f * slim : (f + 1) * slim, :].reshape(NB, NB)
-        y_ref[m * NB : (m + 1) * NB, :] = mult(block, inverse, 1, 1)
-
-    @pl.when(ids_ref[0] == 1)
-    def _():
-        y_ref[:NB, :] = y_ref[:NB, :] - sign_ref[...]
-
-    @pl.when(ids_ref[1] == 1)
-    def _():
-        y_col_ref[:NB, :] = y_col_ref[:NB, :] - sign_ref[...]
-
-
-def spread_kernel(share, step, ids_ref, got_ref, own_ref, inv_ref, sign_ref, send_ref):
+        state_ref[NB + SUB * i : NB + SUB * i + SUB, :] = here * signs[SUB * i : SUB * i + SUB]
+    fetch([pltpu.make_async_copy(state_ref, state_hbm, sem)])
+
+
+def spread_kernel(share, step, ids_ref, got_hbm, own_hbm, state_hbm, send_ref, got_ref, own_ref, state_ref, sems):
+    fetch(
+        [
+            pltpu.make_async_copy(got_hbm, got_ref, sems.at[0]),
+            pltpu.make_async_copy(own_hbm, own_ref, sems.at[1]),
+            pltpu.make_async_copy(state_hbm.at[: 2 * NB, :], state_ref, sems.at[2]),
+        ]
+    )
     total = jnp.sum(got_ref[...], 0)
     own = own_ref[...]
-    line = jnp.sum(sign_ref[...], axis=0, keepdims=True)
-    turned = mult(total, inv_ref[...], 1, 1)
+    line = jnp.sum(state_ref[NB:, :], axis=0, keepdims=True)
+    turned = mult(total, state_ref[:NB, :], 1, 1)
     rows = turned[:share] - own[:share] * line
     lead = jnp.where(ids_ref[0] == 1, turned[share + step :] - 0.5 * own[share + step :] * line, 0.0)
     out = jnp.concatenate([rows, total[share : share + step], lead], 0)
@@ -206,7 +245,7 @@
 
 
 def update_kernel(
-    col_blocks, fold, slim, got_ref, inv_ref, sign_ref, coupling_ref, v_ref, y_ref, a_ref, out_ref, high_ref, low_ref, hold_ref, lead_ref, new_ref, sems
+    col_blocks, fold, slim, got_ref, pack_ref, a_ref, out_ref, high_ref, low_ref, hold_ref, lead_ref, new_ref, sems
 ):
     col_count = got_ref.shape[0]
     share, step, per = fold * slim, NB // col_count, NB // slim
@@ -214,18 +253,19 @@
     for c in range(col_count):
         hold_ref[c * step : (c + 1) * step, :] = got_ref[c, share + slim : share + slim + step, :]
         lead_ref[c * step : (c + 1) * step, :] = got_ref[c, share + slim + step : share + slim + 2 * step, :]
-    inverse, v = inv_ref[...], v_ref[...]
-    cross = jnp.sum(sign_ref[...], axis=1, keepdims=True) * lead_ref[...]
+    coupling, inverse, v = pack_ref[:NB, :], pack_ref[NB : 2 * NB, :], pack_ref[3 * NB : 3 * NB + cols, :]
+    y_ref = pack_ref.at[3 * NB + cols :, :]
+    cross = jnp.sum(pack_ref[2 * NB : 3 * NB, :], axis=1, keepdims=True) * lead_ref[...]
     middle = mult(mult(inverse, hold_ref[...]), inverse, 1, 1) - cross - cross.T
     z_cols = got_ref[:, share : share + slim, :].reshape(cols, NB)
-    u = mult(z_cols - mult(v, middle), coupling_ref[...], 1, 1)
+    u = mult(z_cols - mult(v, middle), coupling, 1, 1)
     for at, part in enumerate((u, v)):
         high, low = halves(part)
         high_ref[:, at * NB : (at + 1) * NB] = high
         low_ref[:, at * NB : (at + 1) * NB] = low
     right_high, right_low = high_ref[...], low_ref[...]
     copies = []
-    for m in range(y_ref.shape[0] // NB):
+    for m in range(a_ref.shape[0] // cols):
         k, f = divmod(m, fold)
         z = got_ref[k * per : (k + 1) * per, f * slim : (f + 1) * slim, :].reshape(NB, NB)
         high, low = halves(jnp.concatenate([y_ref[m * NB : (m + 1) * NB, :], z], 1))
@@ -282,54 +322,72 @@
     got = jnp.broadcast_to(got[0][None], (row_count,) + got.shape[1:])
     got = exchange(relay(exchange(got, "row")), "col")
 
-    send = pl.pallas_call(
+    send, panel = pl.pallas_call(
         lambda *refs: product_kernel(col_blocks, fold, slim, *refs),
-        out_shape=shape(col_count, share + pad, NB),
+        out_shape=(shape(col_count, share + pad, NB), shape(rows + cols, NB)),
         in_specs=[SMEM, VMEM, VMEM],
-        out_specs=VMEM,
-        scratch_shapes=[pltpu.VMEM((rows, NB), jnp.float32), pltpu.VMEM((NB, NB), jnp.float32)],
+        out_specs=(HBM, HBM),
+        scratch_shapes=[
+            pltpu.VMEM((col_count, share + pad, NB), jnp.float32),
+            pltpu.VMEM((rows + cols, NB), jnp.float32),
+            pltpu.VMEM((NB, NB), jnp.float32),
+            pltpu.SemaphoreType.DMA((3,)),
+        ],
         compiler_params=PARAMS,
         name="product",
         cost_estimate=cost(2 * rows * cols * NB * 6, 4_000_000),
     )(ids, got, lines)
     summed = exchange(send, "col")
-    inverse, sign, shift, y_rows, y_cols = pl.pallas_call(
-        lambda *refs: factor_kernel(col_blocks, fold, slim, *refs),
-        out_shape=(shape(NB, NB), shape(NB, NB), shape(NB, NB), shape(rows, NB), shape(cols, NB)),
-        in_specs=[SMEM, VMEM],
-        out_specs=(VMEM,) * 5,
-        scratch_shapes=[pltpu.VMEM((NB, NB), jnp.float32)] * 2,
+    state = pl.pallas_call(
+        lambda *refs: factor_kernel(share + slim, step, *refs),
+        out_shape=shape(3 * NB, NB),
+        in_specs=[VMEM],
+        out_specs=HBM,
+        scratch_shapes=[pltpu.VMEM((3 * NB, NB), jnp.float32)]
+        + [pltpu.VMEM((NB, NB), jnp.float32)] * 2
+        + [pltpu.SemaphoreType.DMA],
         compiler_params=PARAMS,
         name="factor",
         cost_estimate=cost(4_000_000_000, 2_000_000),
-    )(ids, got)
+    )(got)
 
     send = pl.pallas_call(
         lambda *refs: spread_kernel(share, step, *refs),
         out_shape=shape(row_count, share + pad, NB),
-        in_specs=[SMEM] + [VMEM] * 4,
+        in_specs=[SMEM, HBM, HBM, HBM],
         out_specs=VMEM,
+        scratch_shapes=[
+            pltpu.VMEM((col_count, share + pad, NB), jnp.float32),
+            pltpu.VMEM((share + pad, NB), jnp.float32),
+            pltpu.VMEM((2 * NB, NB), jnp.float32),
+            pltpu.SemaphoreType.DMA((3,)),
+        ],
         compiler_params=PARAMS,
         name="spread",
         cost_estimate=cost(10_000_000, 1_000_000),
-    )(ids, summed, own, inverse, sign)
+    )(ids, summed, own, state)
     got = exchange(send, "row")
-    coupling, v_cols = pl.pallas_call(
-        invert_kernel,
-        out_shape=(shape(NB, NB), shape(cols, NB)),
-        in_specs=[VMEM, VMEM],
-        out_specs=(VMEM, VMEM),
+    pack = pl.pallas_call(
+        lambda *refs: invert_kernel(rows, cols, *refs),
+        out_shape=shape(3 * NB + cols + rows, NB),
+        in_specs=[SMEM, HBM, HBM],
+        out_specs=VMEM,
+        scratch_shapes=[
+            pltpu.VMEM((3 * NB, NB), jnp.float32),
+            pltpu.VMEM((rows + cols, NB), jnp.float32),
+            pltpu.SemaphoreType.DMA((2,)),
+        ],
         compiler_params=PARAMS,
         name="invert",
         cost_estimate=cost(4_000_000_000, 1_000_000),
-    )(shift, y_cols)
-    got, coupling, v_cols = lax.optimization_barrier((got, coupling, v_cols))
+    )(ids, state, panel)
+    got, pack = lax.optimization_barrier((got, pack))
     last = exchange(relay(got), "col")
 
     updated = pl.pallas_call(
         lambda *refs: update_kernel(col_blocks, fold, slim, *refs),
         out_shape=shape(rows * col_blocks, NB),
-        in_specs=[VMEM] * 7,
+        in_specs=[VMEM] * 3,
         out_specs=pl.BlockSpec(memory_space=pl.ANY),
         scratch_shapes=[
             pltpu.VMEM((cols, 2 * NB), jnp.bfloat16),
@@ -342,7 +400,7 @@
         compiler_params=PARAMS,
         name="update",
         cost_estimate=cost(4 * rows * cols * NB * 6, 6_000_000),
-    )(last, inverse, sign, coupling, v_cols, y_rows, lines)
+    )(last, pack, lines)
     return updated.reshape(kernel.shape)
 
 

time: 165 us -> 160 us (0.970)
  waiting for transfers between devices: 2.68 us -> 7.85 us
  local copies, waits for them, and re-layouts: 9.82 us -> 5.41 us
  blocking collectives: 107 us -> 103 us
  Pallas kernels: 34.8 us -> 31.8 us
    all_to_all x2, waiting for transfers between devices: 2.68 us -> 7.85 us  [exchange(): return lax.all_to_all(pieces, axis, 0, 0)]
    pallas_call x2, Pallas kernels: 22.2 us -> 18.3 us  [the longest x1 11.9 us: body(): pl.pallas_call(lambda *refs: invert_kernel(rows, cols, *refs), out_shape=...]
    unnamed x28 -> x14, local copies, waits for them, and re-layouts: 9.19 us -> 5.38 us
    all_to_all x4, blocking collectives: 107 us -> 103 us  [exchange(): return lax.all_to_all(pieces, axis, 0, 0)]
  transfers between devices with their start and end apart: 2 -> 2, of which waited for: 1 -> 2; matrix products, arithmetic and copies ran while one was open for 0% -> 0% of each run, Pallas kernels for 13% -> 12%
where the time goes in v5:
time: 160 us; the launch traced here: 159 us
  blocking collectives  103 us (64%)
  Pallas kernels  31.8 us (20%)
  starting transfers between devices  10.2 us (6%)
  waiting for transfers between devices  7.85 us (5%)
  local copies, waits for them, and re-layouts  5.41 us (3%)
    all_to_all x4, blocking collectives, exchange(): return lax.all_to_all(pieces, axis, 0, 0)  103 us
    pallas_call x1, Pallas kernels, body(): pl.pallas_call(lambda *refs: invert_kernel(rows, cols, *refs), out_shape=...  11.9 us
    all_to_all x2, starting transfers between devices, exchange(): return lax.all_to_all(pieces, axis, 0, 0)  10.2 us
    all_to_all x2, waiting for transfers between devices, exchange(): return lax.all_to_all(pieces, axis, 0, 0)  7.85 us
    pallas_call x1, Pallas kernels, body(): pl.pallas_call(lambda *refs: factor_kernel(share + slim, step, *refs), ou...  6.4 us
    unnamed x14, local copies, waits for them, and re-layouts  5.38 us
    pallas_call x1, Pallas kernels, body(): pl.pallas_call(lambda *refs: update_kernel(col_blocks, fold, slim, *refs)...  4.52 us
    pallas_call x1, Pallas kernels, body(): pl.pallas_call(lambda *refs: product_kernel(col_blocks, fold, slim, *refs...  3.96 us
  transfers between devices with their start and end apart: 2, of which 2 were waited for; matrix products, arithmetic and copies ran while one was open for 0% of the time, Pallas kernels for 12%

profile of v5, /device:TPU:1, one launch (start us, length us, event | category | flops | bytes accessed | tf_op | source)
XLA Modules:
  0.0 159.0 jit_solution(13820579938485272122)
XLA Ops:
  0.0 0.1 pad_add_fusion.refs_0_
  0.1 0.0 copy-start
  0.1 1.6 copy-done
  1.7 1.2 prepare.1
  2.9 22.5 %all_to_all.30 = f32[32,40,128]{2,1,0:T(8,128)S(1)} all-to-all(f32[32,40,128]{2,1,0:T(8,128)S(1)} %prepare.1), channel_id=1, replica_groups=mesh['row'=16,'col'=32] {'col'}, dimensions={0} | all-to-all | bytes 1310720 | tf_op jit(solution)/shard_map/all_to_all | solution.py:285
  25.4 0.0 copy-start.1
  25.4 28.8 %all_to_all.31.refs_1_ = f32[16,40,128]{2,1,0:T(8,128)S(1)} all-to-all(f32[16,40,128]{2,1,0:T(8,128)S(1)} %broadcast_in_dim.8), channel_id=1, replica_groups=mesh['row'=16,'col'=32] {'row'}, dimensions={0} | all-to-all | bytes 655360 | tf_op jit(solution)/shard_map/all_to_all | solution.py:285
  54.2 0.6 relay.2
  54.8 26.1 %all_to_all.32.refs_1_.refs_0_ = f32[32,56,128]{2,1,0:T(8,128)S(1)} all-to-all(f32[32,56,128]{2,1,0:T(8,128)S(1)} %relay.2), channel_id=1, replica_groups=mesh['row'=16,'col'=32] {'col'}, dimensions={0} | all-to-all | bytes 1835008 | tf_op jit(solution)/shard_map/all_to_all | solution.py:285
  80.9 0.0 copy-done.1
  80.9 4.0 %product.1 = (f32[32,40,128]{2,1,0:T(8,128)S(1)}, f32[1536,128]{1,0:T(8,128)S(1)}) custom-call(s32[2]{0:T(128)S(1)} %pad_add_fusion.refs_0_, f32[32,56,128]{2,1,0:T(8,128)S(1)} %all_to_all.32.refs_1_.refs_0_, f32[4096,128]{1,0:T(8,128)S(1)} %bitcast.11), custom_call_target="tpu_custom_call" | custom-call | flops 805306368 | bytes 4000000 | tf_op jit(solution)/shard_map/product/pallas_call | solution.py:325
  84.9 0.0 copy-start.2
  84.9 0.9 copy-done.2
  85.7 0.0 copy-start.5
  85.7 0.9 copy-done.5
  86.6 4.6 %all-to-all-start.3 = ((f32[32,40,128]{2,1,0:T(8,128)}), f32[32,40,128]{2,1,0:T(8,128)}, u32[]{:S(2)}, u32[]{:S(2)}) async-start(f32[32,40,128]{2,1,0:T(8,128)} %copy-done.2), calls=%async_computation.3 | async-start | bytes 1310720 | tf_op jit(solution)/shard_map/all_to_all | solution.py:285
  91.2 6.4 %factor.1.refs_3_.refs_1_ = f32[384,128]{1,0:T(8,128)S(1)} custom-call(f32[32,56,128]{2,1,0:T(8,128)S(1)} %all_to_all.32.refs_1_.refs_0_), custom_call_target="tpu_custom_call" | custom-call | flops 4000000000 | bytes 2000000 | tf_op jit(solution)/shard_map/factor/pallas_call | solution.py:341
  97.6 0.0 copy-start.3
  97.6 6.7 %all-to-all-done.3.refs_1_ = f32[32,40,128]{2,1,0:T(8,128)} async-done(((f32[32,40,128]{2,1,0:T(8,128)}), f32[32,40,128]{2,1,0:T(8,128)}, u32[]{:S(2)}, u32[]{:S(2)}) %all-to-all-start.3) | async-done | bytes 655392 | tf_op jit(solution)/shard_map/all_to_all | solution.py:285
  104.3 2.6 %spread.1 = f32[16,40,128]{2,1,0:T(8,128)} custom-call(s32[2]{0:T(128)S(1)} %pad_add_fusion.refs_0_, f32[32,40,128]{2,1,0:T(8,128)} %all-to-all-done.3.refs_1_, f32[40,128]{1,0:T(8,128)S(1)} %get-tuple-element.13.refs_2_, f32[384,128]{1,0:T(8,128)S(1)} %factor.1.refs_3_.refs_1_), custom_call_target="tpu_custom_call" | custom-call | flops 10000000 | bytes 1000000 | tf_op jit(solution)/shard_map/spread/pallas_call | solution.py:354
  106.9 0.0 copy-done.3
  106.9 5.6 %all-to-all-start.4 = ((f32[16,40,128]{2,1,0:T(8,128)}), f32[16,40,128]{2,1,0:T(8,128)S(1)}, u32[]{:S(2)}, u32[]{:S(2)}) async-start(f32[16,40,128]{2,1,0:T(8,128)} %spread.1), calls=%async_computation.4 | async-start | bytes 655360 | tf_op jit(solution)/shard_map/all_to_all | solution.py:285
  112.6 0.0 copy-start.4
  112.6 0.9 copy-done.4
  113.5 0.0 copy-start.6
  113.5 1.1 copy-done.6
  114.6 11.9 %invert.1.refs_1_ = f32[1920,128]{1,0:T(8,128)S(1)} custom-call(s32[2]{0:T(128)S(1)} %pad_add_fusion.refs_0_, f32[384,128]{1,0:T(8,128)S(1)} %copy-done.4, f32[1536,128]{1,0:T(8,128)S(1)} %copy-done.6), custom_call_target="tpu_custom_call" | custom-call | flops 4000000000 | bytes 1000000 | tf_op jit(solution)/shard_map/invert/pallas_call | solution.py:370
  126.5 1.2 all-to-all-done.4.refs_1_
  127.7 0.6 relay.3
  128.3 26.0 %all_to_all.33.refs_0_ = f32[32,56,128]{2,1,0:T(8,128)S(1)} all-to-all(f32[32,56,128]{2,1,0:T(8,128)S(1)} %relay.3), channel_id=1, replica_groups=mesh['row'=16,'col'=32] {'col'}, dimensions={0} | all-to-all | bytes 1835008 | tf_op jit(solution)/shard_map/all_to_all | solution.py:285
  154.4 4.5 %update.1 = f32[4096,128]{1,0:T(8,128)} custom-call(f32[32,56,128]{2,1,0:T(8,128)S(1)} %all_to_all.33.refs_0_, f32[1920,128]{1,0:T(8,128)S(1)} %invert.1.refs_1_, f32[4096,128]{1,0:T(8,128)S(1)} %bitcast.12), custom_call_target="tpu_custom_call" | custom-call | flops 1610612736 | bytes 6000000 | tf_op jit(solution)/shard_map/update/pallas_call | solution.py:387
  (2 shorter events, 0.0 us)
Async XLA Ops:
  0.1 1.6 %copy-start = (f32[8,1,128,4,1,128]{5,4,3,2,1,0:T(1,128)S(1)}, f32[8,1,128,4,1,128]{5,4,3,2,1,0:T(1,128)}, u32[]{:S(2)}) copy-start(f32[8,1,128,4,1,128]{5,4,3,2,1,0:T(1,128)} %param.1) | copy-start | bytes 6291460
  25.4 55.5 %copy-start.1 = (f32[8,1,128,4,1,128]{5,4,3,2,1,0:T(1,128)S(1)}, f32[8,1,128,4,1,128]{5,4,3,2,1,0:T(1,128)}, u32[]{:S(2)}) copy-start(f32[8,1,128,4,1,128]{5,4,3,2,1,0:T(1,128)} %param.1) | copy-start | bytes 6291460
  84.9 0.9 copy-start.2
  85.7 0.9 copy-start.5
  86.6 17.7 %all-to-all-start.3 = ((f32[32,40,128]{2,1,0:T(8,128)}), f32[32,40,128]{2,1,0:T(8,128)}, u32[]{:S(2)}, u32[]{:S(2)}) async-start(f32[32,40,128]{2,1,0:T(8,128)} %copy-done.2), calls=%async_computation.3 | async-start | bytes 1310720 | tf_op jit(solution)/shard_map/all_to_all | solution.py:285
  97.6 9.3 %copy-start.3 = (f32[384,128]{1,0:T(8,128)}, f32[384,128]{1,0:T(8,128)S(1)}, u32[]{:S(2)}) copy-start(f32[384,128]{1,0:T(8,128)S(1)} %factor.1.refs_3_.refs_1_) | copy-start | bytes 589828
  106.9 20.8 %all-to-all-start.4 = ((f32[16,40,128]{2,1,0:T(8,128)}), f32[16,40,128]{2,1,0:T(8,128)S(1)}, u32[]{:S(2)}, u32[]{:S(2)}) async-start(f32[16,40,128]{2,1,0:T(8,128)} %spread.1), calls=%async_computation.4 | async-start | bytes 655360 | tf_op jit(solution)/shard_map/all_to_all | solution.py:285
  112.6 0.9 copy-start.4
  113.5 1.1 copy-start.6

commit v6 on v5

--- a/solution.py
+++ b/solution.py
@@ -140,7 +140,7 @@
     pack_ref[4 * NB + cols :, :] = y[NB:rows]
 
 
-def prepare_kernel(col_blocks, fold, slim, ids_ref, a_ref, send_ref):
+def prepare_kernel(col_blocks, fold, slim, ids_ref, a_ref, send_ref, top_ref):
     rows = a_ref.shape[0] // col_blocks
     col_count = send_ref.shape[0]
     share, step, per = fold * slim, NB // col_count, NB // slim
@@ -155,6 +155,18 @@
     for c in range(col_count):
         send_ref[c, share : share + step, :] = gram[c * step : (c + 1) * step]
         send_ref[c, share + step : share + 2 * step, :] = lead[c * step : (c + 1) * step]
+    for k in range(col_blocks):
+        block = a_ref[pl.ds(k, NB, col_blocks), :].T
+        if k == 0:
+            block = jnp.where(ids_ref[1] == 0, 0.0, block)
+        top_ref[k * NB : (k + 1) * NB, :] = block
+
+
+def join_kernel(share_ref, got_ref, send_ref):
+    mine = share_ref[...]
+    piece = jnp.sum(got_ref[...], 0)
+    send_ref[:, : mine.shape[0], :] = jnp.broadcast_to(mine[None], (send_ref.shape[0],) + mine.shape)
+    send_ref[:, mine.shape[0] :, :] = jnp.broadcast_to(piece[None], (send_ref.shape[0],) + piece.shape)
 
 
 def relay_kernel(fold, slim, ids_ref, got_ref, send_ref):
@@ -168,11 +180,11 @@
         send_ref[f * row_count : (f + 1) * row_count, share : share + slim, :] = got_ref[:, f * slim : (f + 1) * slim, :]
 
 
-def product_kernel(col_blocks, fold, slim, ids_ref, got_ref, a_ref, send_hbm, panel_hbm, send_ref, panel_ref, hold_ref, sems):
+def product_kernel(col_blocks, fold, slim, ids_ref, got_ref, top_ref, a_ref, send_hbm, panel_hbm, send_ref, panel_ref, hold_ref, sems):
     col_count = got_ref.shape[0]
     rows, cols = a_ref.shape[0] // col_blocks, col_blocks * NB
     share, step, per = fold * slim, NB // col_count, NB // slim
-    panel_ref[rows:, :] = got_ref[:, share : share + slim, :].reshape(cols, NB)
+    panel_ref[rows:, :] = top_ref[...]
     for m in range(rows // NB):
         k, f = divmod(m, fold)
         panel_ref[m * NB : (m + 1) * NB, :] = got_ref[k * per : (k + 1) * per, f * slim : (f + 1) * slim, :].reshape(NB, NB)
@@ -297,6 +309,9 @@
     share = fold * slim
     pad = 2 * step
 
+    def hbm(*dims):
+        return pltpu.HBM(dims, jnp.float32)
+
     def relay(got):
         return pl.pallas_call(
             lambda *refs: relay_kernel(fold, slim, *refs),
@@ -308,24 +323,39 @@
             cost_estimate=cost(1_000_000, 1_000_000),
         )(ids, got)
 
-    send = pl.pallas_call(
+    send, top = pl.pallas_call(
         lambda *refs: prepare_kernel(col_blocks, fold, slim, *refs),
-        out_shape=shape(col_count, share + pad, NB),
+        out_shape=(shape(col_count, share + pad, NB), shape(cols, NB)),
         in_specs=[SMEM, VMEM],
-        out_specs=VMEM,
+        out_specs=(VMEM, VMEM),
         compiler_params=PARAMS,
         name="prepare",
         cost_estimate=cost(2 * rows * NB * NB * 6, 3_000_000),
     )(ids, lines)
     got = exchange(send, "col")
-    own = got[1]
-    got = jnp.broadcast_to(got[0][None], (row_count,) + got.shape[1:])
-    got = exchange(relay(exchange(got, "row")), "col")
+    own, mine, piece = got[1], got[0, :share], got[0, share:]
+    distance = row_count // 2
+    while distance:
+        pairs = [(at, at + distance) for at in range(0, row_count, 2 * distance)]
+        moved = lax.ppermute(top, "row", pairs)
+        top = jnp.where(row_index % (2 * distance) == distance, moved, top)
+        distance //= 2
+    pieces = exchange(jnp.broadcast_to(piece[None], (row_count,) + piece.shape), "row")
+    send = pl.pallas_call(
+        join_kernel,
+        out_shape=shape(col_count, share + pad, NB),
+        in_specs=[VMEM, VMEM],
+        out_specs=VMEM,
+        compiler_params=PARAMS,
+        name="join",
+        cost_estimate=cost(1_000_000, 1_000_000),
+    )(mine, pieces)
+    got = exchange(send, "col")
 
     send, panel = pl.pallas_call(
         lambda *refs: product_kernel(col_blocks, fold, slim, *refs),
-        out_shape=(shape(col_count, share + pad, NB), shape(rows + cols, NB)),
-        in_specs=[SMEM, VMEM, VMEM],
+        out_shape=(hbm(col_count, share + pad, NB), hbm(rows + cols, NB)),
+        in_specs=[SMEM, VMEM, VMEM, VMEM],
         out_specs=(HBM, HBM),
         scratch_shapes=[
             pltpu.VMEM((col_count, share + pad, NB), jnp.float32),
@@ -336,11 +366,11 @@
         compiler_params=PARAMS,
         name="product",
         cost_estimate=cost(2 * rows * cols * NB * 6, 4_000_000),
-    )(ids, got, lines)
+    )(ids, got, top, lines)
     summed = exchange(send, "col")
     state = pl.pallas_call(
-        lambda *refs: factor_kernel(share + slim, step, *refs),
-        out_shape=shape(3 * NB, NB),
+        lambda *refs: factor_kernel(share, step, *refs),
+        out_shape=hbm(3 * NB, NB),
         in_specs=[VMEM],
         out_specs=HBM,
         scratch_shapes=[pltpu.VMEM((3 * NB, NB), jnp.float32)]

time: 160 us -> 157 us (0.981)
  blocking collectives: 103 us -> 25.1 us
  starting transfers between devices: 10.2 us -> 52.7 us
  waiting for transfers between devices: 7.85 us -> 38.8 us
    all_to_all x4 -> x1, blocking collectives: 103 us -> 25.1 us  [exchange(): return lax.all_to_all(pieces, axis, 0, 0)]
    ppermute x0 -> x4, starting transfers between devices: none -> 21.5 us  [body(): moved = lax.ppermute(top, 'row', pairs)]
    all_to_all x2 -> x5, starting transfers between devices: 10.2 us -> 31.2 us  [exchange(): return lax.all_to_all(pieces, axis, 0, 0)]
    all_to_all x2 -> x5, waiting for transfers between devices: 7.85 us -> 27.6 us  [exchange(): return lax.all_to_all(pieces, axis, 0, 0)]
    ppermute x0 -> x4, waiting for transfers between devices: none -> 11.2 us  [body(): moved = lax.ppermute(top, 'row', pairs)]
    pallas_call x1 -> x2, Pallas kernels: 6.4 us -> 7.72 us  [the longest x1 6.83 us: body(): pl.pallas_call(lambda *refs: factor_kernel(share, step, *refs), out_shape...]
    unnamed x14 -> x12, local copies, waits for them, and re-layouts: 5.38 us -> 4.58 us
  transfers between devices with their start and end apart: 2 -> 9, of which waited for: 2 -> 7; matrix products, arithmetic and copies ran while one was open for 0% -> 1% of each run, Pallas kernels for 12% -> 13%
where the time goes in v6:
time: 157 us; the launch traced here: 156 us
  starting transfers between devices  52.7 us (34%)
  waiting for transfers between devices  38.8 us (25%)
  Pallas kernels  33.1 us (21%)
  blocking collectives  25.1 us (16%)
  local copies, waits for them, and re-layouts  6 us (4%)
    all_to_all x5, starting transfers between devices, exchange(): return lax.all_to_all(pieces, axis, 0, 0)  31.2 us
    all_to_all x5, waiting for transfers between devices, exchange(): return lax.all_to_all(pieces, axis, 0, 0)  27.6 us
    all_to_all x1, blocking collectives, exchange(): return lax.all_to_all(pieces, axis, 0, 0)  25.1 us
    ppermute x4, starting transfers between devices, body(): moved = lax.ppermute(top, 'row', pairs)  21.5 us
    pallas_call x1, Pallas kernels, body(): pl.pallas_call(lambda *refs: invert_kernel(rows, cols, *refs), out_shape=...  11.9 us
    ppermute x4, waiting for transfers between devices, body(): moved = lax.ppermute(top, 'row', pairs)  11.2 us
    pallas_call x1, Pallas kernels, body(): pl.pallas_call(lambda *refs: factor_kernel(share, step, *refs), out_shape...  6.83 us
    unnamed x12, local copies, waits for them, and re-layouts  4.58 us
  transfers between devices with their start and end apart: 9, of which 7 were waited for; matrix products, arithmetic and copies ran while one was open for 1% of the time, Pallas kernels for 13%

profile of v6, /device:TPU:1, one launch (start us, length us, event | category | flops | bytes accessed | tf_op | source)
XLA Modules:
  0.0 156.4 jit_solution(9156535192275911496)
XLA Ops:
  0.0 0.1 pad_add_fusion.refs_0_
  0.1 1.6 %copy-done = f32[8,1,128,4,1,128]{5,4,3,2,1,0:T(1,128)S(1)} copy-done((f32[8,1,128,4,1,128]{5,4,3,2,1,0:T(1,128)S(1)}, f32[8,1,128,4,1,128]{5,4,3,2,1,0:T(1,128)}, u32[]{:S(2)}) %copy-start) | copy-done | bytes 2097176
  1.7 2.0 %prepare.1 = (f32[32,40,128]{2,1,0:T(8,128)}, f32[512,128]{1,0:T(8,128)S(1)}) custom-call(s32[2]{0:T(128)S(1)} %pad_add_fusion.refs_0_, f32[4096,128]{1,0:T(8,128)S(1)} %bitcast.12), custom_call_target="tpu_custom_call" | custom-call | flops 201326592 | bytes 3000000 | tf_op jit(solution)/shard_map/prepare/pallas_call | solution.py:326
  3.7 16.3 %collective-permute-start = (f32[512,128]{1,0:T(8,128)S(1)}, f32[512,128]{1,0:T(8,128)S(1)}, u32[]{:S(2)}, u32[]{:S(2)}) collective-permute-start(f32[512,128]{1,0:T(8,128)S(1)} %get-tuple-element.12), channel_id=1, source_target_pairs={{0,256},{1,257},{2,258},{3,259},{4,260},{5,261},{6,262},{7,263},{8... | collective-permute-start | bytes 786440 | tf_op jit(solution)/shard_map/ppermute | solution.py:340
  20.0 8.0 %all-to-all-start = ((f32[32,40,128]{2,1,0:T(8,128)}), f32[32,40,128]{2,1,0:T(8,128)S(1)}, u32[]{:S(2)}, u32[]{:S(2)}) async-start(f32[32,40,128]{2,1,0:T(8,128)} %get-tuple-element.11), calls=%async_computation | async-start | bytes 1310720 | tf_op jit(solution)/shard_map/all_to_all | solution.py:297
  28.1 1.3 collective-permute-start.1
  29.4 5.7 %collective-permute-done.1 = f32[512,128]{1,0:T(8,128)S(1)} collective-permute-done((f32[512,128]{1,0:T(8,128)S(1)}, f32[512,128]{1,0:T(8,128)S(1)}, u32[]{:S(2)}, u32[]{:S(2)}) %collective-permute-start.1) | collective-permute-done | bytes 262176 | tf_op jit(solution)/shard_map/ppermute | solution.py:340
  35.2 1.4 collective-permute-start.2
  36.6 4.3 %all-to-all-done = f32[32,40,128]{2,1,0:T(8,128)S(1)} async-done(((f32[32,40,128]{2,1,0:T(8,128)}), f32[32,40,128]{2,1,0:T(8,128)S(1)}, u32[]{:S(2)}, u32[]{:S(2)}) %all-to-all-start) | async-done | bytes 655392 | tf_op jit(solution)/shard_map/all_to_all | solution.py:297
  40.9 0.7 broadcast_in_dim.8
  41.6 4.5 %all-to-all-start.1 = ((f32[16,8,128]{2,1,0:T(8,128)}), f32[16,8,128]{2,1,0:T(8,128)S(1)}, u32[]{:S(2)}, u32[]{:S(2)}) async-start(f32[16,8,128]{2,1,0:T(8,128)} %broadcast_in_dim.8), calls=%async_computation.1 | async-start | bytes 131072 | tf_op jit(solution)/shard_map/all_to_all | solution.py:297
  46.1 11.5 %all-to-all-done.1.got_ref = f32[16,8,128]{2,1,0:T(8,128)S(1)} async-done(((f32[16,8,128]{2,1,0:T(8,128)}), f32[16,8,128]{2,1,0:T(8,128)S(1)}, u32[]{:S(2)}, u32[]{:S(2)}) %all-to-all-start.1) | async-done | bytes 65568 | tf_op jit(solution)/shard_map/all_to_all | solution.py:297
  57.7 0.9 join.1
  58.5 10.9 %all-to-all-start.2 = ((f32[32,40,128]{2,1,0:T(8,128)}), f32[32,40,128]{2,1,0:T(8,128)S(1)}, u32[]{:S(2)}, u32[]{:S(2)}) async-start(f32[32,40,128]{2,1,0:T(8,128)} %join.1), calls=%async_computation.2 | async-start | bytes 1310720 | tf_op jit(solution)/shard_map/all_to_all | solution.py:297
  69.5 2.5 %collective-permute-start.3 = (f32[512,128]{1,0:T(8,128)S(1)}, f32[512,128]{1,0:T(8,128)S(1)}, u32[]{:S(2)}, u32[]{:S(2)}) collective-permute-start(f32[512,128]{1,0:T(8,128)S(1)} %broadcast_select_fusion.2), channel_id=1, source_target_pairs={{0,32},{64,96},{128,160},{192,224},{256,288},{320,352},{384,416},{... | collective-permute-start | bytes 786440 | tf_op jit(solution)/shard_map/ppermute | solution.py:340
  72.0 5.4 %collective-permute-done.3 = f32[512,128]{1,0:T(8,128)S(1)} collective-permute-done((f32[512,128]{1,0:T(8,128)S(1)}, f32[512,128]{1,0:T(8,128)S(1)}, u32[]{:S(2)}, u32[]{:S(2)}) %collective-permute-start.3) | collective-permute-done | bytes 262176 | tf_op jit(solution)/shard_map/ppermute | solution.py:340
  77.5 4.9 %all-to-all-done.2.refs_1_.refs_0_ = f32[32,40,128]{2,1,0:T(8,128)S(1)} async-done(((f32[32,40,128]{2,1,0:T(8,128)}), f32[32,40,128]{2,1,0:T(8,128)S(1)}, u32[]{:S(2)}, u32[]{:S(2)}) %all-to-all-start.2) | async-done | bytes 655392 | tf_op jit(solution)/shard_map/all_to_all | solution.py:297
  82.3 4.4 %product.1 = (f32[32,40,128]{2,1,0:T(8,128)}, f32[1536,128]{1,0:T(8,128)}) custom-call(s32[2]{0:T(128)S(1)} %pad_add_fusion.refs_0_, f32[32,40,128]{2,1,0:T(8,128)S(1)} %all-to-all-done.2.refs_1_.refs_0_, f32[512,128]{1,0:T(8,128)S(1)} %broadcast_select_fusion.3.refs_2_, f32[4096,128]{1,0:T(8,128)S(1)} %bitcast.13), custom_call_target="tpu_custom_call" | custom-call | flops 805306368 | bytes 4000000 | tf_op jit(solution)/shard_map/product/pallas_call | solution.py:355
  86.7 4.1 %all-to-all-start.3 = ((f32[32,40,128]{2,1,0:T(8,128)}), f32[32,40,128]{2,1,0:T(8,128)S(1)}, u32[]{:S(2)}, u32[]{:S(2)}) async-start(f32[32,40,128]{2,1,0:T(8,128)} %get-tuple-element.13), calls=%async_computation.3 | async-start | bytes 1310720 | tf_op jit(solution)/shard_map/all_to_all | solution.py:297
  90.9 0.7 slice_bitcast_fusion.refs_2_
  91.6 6.8 %factor.1.refs_3_.refs_1_ = f32[384,128]{1,0:T(8,128)} custom-call(f32[32,40,128]{2,1,0:T(8,128)S(1)} %all-to-all-done.2.refs_1_.refs_0_), custom_call_target="tpu_custom_call" | custom-call | flops 4000000000 | bytes 2000000 | tf_op jit(solution)/shard_map/factor/pallas_call | solution.py:371
  98.4 5.4 %all-to-all-done.3.refs_1_ = f32[32,40,128]{2,1,0:T(8,128)S(1)} async-done(((f32[32,40,128]{2,1,0:T(8,128)}), f32[32,40,128]{2,1,0:T(8,128)S(1)}, u32[]{:S(2)}, u32[]{:S(2)}) %all-to-all-start.3) | async-done | bytes 655392 | tf_op jit(solution)/shard_map/all_to_all | solution.py:297
  103.9 0.9 copy-done.2
  104.8 1.9 %spread.1 = f32[16,40,128]{2,1,0:T(8,128)} custom-call(s32[2]{0:T(128)S(1)} %pad_add_fusion.refs_0_, f32[32,40,128]{2,1,0:T(8,128)S(1)} %all-to-all-done.3.refs_1_, f32[40,128]{1,0:T(8,128)S(1)} %slice_bitcast_fusion.refs_2_, f32[384,128]{1,0:T(8,128)S(1)} %copy-done.2), custom_call_target="tpu_custom_call" | custom-call | flops 10000000 | bytes 1000000 | tf_op jit(solution)/shard_map/spread/pallas_call | solution.py:384
  106.8 3.7 %all-to-all-start.4 = ((f32[16,40,128]{2,1,0:T(8,128)}), f32[16,40,128]{2,1,0:T(8,128)S(1)}, u32[]{:S(2)}, u32[]{:S(2)}) async-start(f32[16,40,128]{2,1,0:T(8,128)} %spread.1), calls=%async_computation.4 | async-start | bytes 655360 | tf_op jit(solution)/shard_map/all_to_all | solution.py:297
  110.5 0.9 copy-done.3
  111.4 1.1 copy-done.4
  112.6 11.9 %invert.1.refs_1_ = f32[1920,128]{1,0:T(8,128)S(1)} custom-call(s32[2]{0:T(128)S(1)} %pad_add_fusion.refs_0_, f32[384,128]{1,0:T(8,128)S(1)} %copy-done.3, f32[1536,128]{1,0:T(8,128)S(1)} %copy-done.4), custom_call_target="tpu_custom_call" | custom-call | flops 4000000000 | bytes 1000000 | tf_op jit(solution)/shard_map/invert/pallas_call | solution.py:400
  124.5 1.5 all-to-all-done.4.refs_1_
  125.9 0.6 relay.1
  126.6 25.1 %all_to_all.30.refs_0_ = f32[32,56,128]{2,1,0:T(8,128)S(1)} all-to-all(f32[32,56,128]{2,1,0:T(8,128)S(1)} %relay.1), channel_id=1, replica_groups=mesh['row'=16,'col'=32] {'col'}, dimensions={0} | all-to-all | bytes 1835008 | tf_op jit(solution)/shard_map/all_to_all | solution.py:297
  151.7 4.5 %update.1 = f32[4096,128]{1,0:T(8,128)} custom-call(f32[32,56,128]{2,1,0:T(8,128)S(1)} %all_to_all.30.refs_0_, f32[1920,128]{1,0:T(8,128)S(1)} %invert.1.refs_1_, f32[4096,128]{1,0:T(8,128)S(1)} %bitcast.14), custom_call_target="tpu_custom_call" | custom-call | flops 1610612736 | bytes 6000000 | tf_op jit(solution)/shard_map/update/pallas_call | solution.py:417
  (16 shorter events, 0.1 us)
Async XLA Ops:
  0.1 1.6 %copy-start = (f32[8,1,128,4,1,128]{5,4,3,2,1,0:T(1,128)S(1)}, f32[8,1,128,4,1,128]{5,4,3,2,1,0:T(1,128)}, u32[]{:S(2)}) copy-start(f32[8,1,128,4,1,128]{5,4,3,2,1,0:T(1,128)} %param.1) | copy-start | bytes 6291460
  3.7 24.4 %collective-permute-start = (f32[512,128]{1,0:T(8,128)S(1)}, f32[512,128]{1,0:T(8,128)S(1)}, u32[]{:S(2)}, u32[]{:S(2)}) collective-permute-start(f32[512,128]{1,0:T(8,128)S(1)} %get-tuple-element.12), channel_id=1, source_target_pairs={{0,256},{1,257},{2,258},{3,259},{4,260},{5,261},{6,262},{7,263},{8... | collective-permute-start | bytes 786440 | tf_op jit(solution)/shard_map/ppermute | solution.py:340
  20.0 21.0 %all-to-all-start = ((f32[32,40,128]{2,1,0:T(8,128)}), f32[32,40,128]{2,1,0:T(8,128)S(1)}, u32[]{:S(2)}, u32[]{:S(2)}) async-start(f32[32,40,128]{2,1,0:T(8,128)} %get-tuple-element.11), calls=%async_computation | async-start | bytes 1310720 | tf_op jit(solution)/shard_map/all_to_all | solution.py:297
  28.1 7.1 %collective-permute-start.1 = (f32[512,128]{1,0:T(8,128)S(1)}, f32[512,128]{1,0:T(8,128)S(1)}, u32[]{:S(2)}, u32[]{:S(2)}) collective-permute-start(f32[512,128]{1,0:T(8,128)S(1)} %broadcast_select_fusion), channel_id=1, source_target_pairs={{0,128},{256,384},{1,129},{257,385},{2,130},{258,386},{3,131},{259... | collective-permute-start | bytes 786440 | tf_op jit(solution)/shard_map/ppermute | solution.py:340
  35.2 47.2 %copy-start.1 = (f32[8,1,128,4,1,128]{5,4,3,2,1,0:T(1,128)S(1)}, f32[8,1,128,4,1,128]{5,4,3,2,1,0:T(1,128)}, u32[]{:S(2)}) copy-start(f32[8,1,128,4,1,128]{5,4,3,2,1,0:T(1,128)} %param.1) | copy-start | bytes 6291460
  35.2 34.2 %collective-permute-start.2 = (f32[512,128]{1,0:T(8,128)S(1)}, f32[512,128]{1,0:T(8,128)S(1)}, u32[]{:S(2)}, u32[]{:S(2)}) collective-permute-start(f32[512,128]{1,0:T(8,128)S(1)} %broadcast_select_fusion.1), channel_id=1, source_target_pairs={{0,64},{128,192},{256,320},{384,448},{1,65},{129,193},{257,321},{3... | collective-permute-start | bytes 786440 | tf_op jit(solution)/shard_map/ppermute | solution.py:340
  40.9 17.6 %copy-start.5 = (f32[32,40,128]{2,1,0:T(8,128)}, f32[32,40,128]{2,1,0:T(8,128)S(1)}, u32[]{:S(2)}) copy-start(f32[32,40,128]{2,1,0:T(8,128)S(1)} %all-to-all-done) | copy-start | bytes 1966084
  41.6 16.0 %all-to-all-start.1 = ((f32[16,8,128]{2,1,0:T(8,128)}), f32[16,8,128]{2,1,0:T(8,128)S(1)}, u32[]{:S(2)}, u32[]{:S(2)}) async-start(f32[16,8,128]{2,1,0:T(8,128)} %broadcast_in_dim.8), calls=%async_computation.1 | async-start | bytes 131072 | tf_op jit(solution)/shard_map/all_to_all | solution.py:297
  58.5 23.8 %all-to-all-start.2 = ((f32[32,40,128]{2,1,0:T(8,128)}), f32[32,40,128]{2,1,0:T(8,128)S(1)}, u32[]{:S(2)}, u32[]{:S(2)}) async-start(f32[32,40,128]{2,1,0:T(8,128)} %join.1), calls=%async_computation.2 | async-start | bytes 1310720 | tf_op jit(solution)/shard_map/all_to_all | solution.py:297
  69.5 7.9 %collective-permute-start.3 = (f32[512,128]{1,0:T(8,128)S(1)}, f32[512,128]{1,0:T(8,128)S(1)}, u32[]{:S(2)}, u32[]{:S(2)}) collective-permute-start(f32[512,128]{1,0:T(8,128)S(1)} %broadcast_select_fusion.2), channel_id=1, source_target_pairs={{0,32},{64,96},{128,160},{192,224},{256,288},{320,352},{384,416},{... | collective-permute-start | bytes 786440 | tf_op jit(solution)/shard_map/ppermute | solution.py:340
  86.7 17.1 %all-to-all-start.3 = ((f32[32,40,128]{2,1,0:T(8,128)}), f32[32,40,128]{2,1,0:T(8,128)S(1)}, u32[]{:S(2)}, u32[]{:S(2)}) async-start(f32[32,40,128]{2,1,0:T(8,128)} %get-tuple-element.13), calls=%async_computation.3 | async-start | bytes 1310720 | tf_op jit(solution)/shard_map/all_to_all | solution.py:297
  103.9 0.9 copy-start.2
  106.8 19.2 %all-to-all-start.4 = ((f32[16,40,128]{2,1,0:T(8,128)}), f32[16,40,128]{2,1,0:T(8,128)S(1)}, u32[]{:S(2)}, u32[]{:S(2)}) async-start(f32[16,40,128]{2,1,0:T(8,128)} %spread.1), calls=%async_computation.4 | async-start | bytes 655360 | tf_op jit(solution)/shard_map/all_to_all | solution.py:297
  110.5 0.9 copy-start.3
  111.4 1.1 copy-start.4

commit v7 on v6

--- a/solution.py
+++ b/solution.py
@@ -92,13 +92,6 @@
         rows = right[i] - ratio * pltpu.roll(right[i], 1, 0)
         out.append(rows * lax.rsqrt(diag - ratio * below))
     return out
-
-
-def fetch(copies):
-    for copy in copies:
-        copy.start()
-    for copy in copies:
-        copy.wait()
 
 
 def invert_kernel(rows, cols, ids_ref, state_hbm, panel_hbm, pack_ref, state_ref, panel_ref, sems):
@@ -140,7 +133,7 @@
     pack_ref[4 * NB + cols :, :] = y[NB:rows]
 
 
-def prepare_kernel(col_blocks, fold, slim, ids_ref, a_ref, send_ref, top_ref):
+def prepare_kernel(col_blocks, fold, slim, ids_ref, a_ref, send_ref):
     rows = a_ref.shape[0] // col_blocks
     col_count = send_ref.shape[0]
     share, step, per = fold * slim, NB // col_count, NB // slim
@@ -155,6 +148,9 @@
     for c in range(col_count):
         send_ref[c, share : share + step, :] = gram[c * step : (c + 1) * step]
         send_ref[c, share + step : share + 2 * step, :] = lead[c * step : (c + 1) * step]
+
+
+def top_kernel(col_blocks, ids_ref, a_ref, top_ref):
     for k in range(col_blocks):
         block = a_ref[pl.ds(k, NB, col_blocks), :].T
         if k == 0:
@@ -226,18 +222,16 @@
     for i in range(count):
         here = jnp.where(lane_id == sub_id + SUB * i, 1.0, 0.0)
         state_ref[NB + SUB * i : NB + SUB * i + SUB, :] = here * signs[SUB * i : SUB * i + SUB]
-    fetch([pltpu.make_async_copy(state_ref, state_hbm, sem)])
-
-
-def spread_kernel(share, step, ids_ref, got_hbm, own_hbm, state_hbm, send_ref, got_ref, own_ref, state_ref, sems):
-    fetch(
-        [
-            pltpu.make_async_copy(got_hbm, got_ref, sems.at[0]),
-            pltpu.make_async_copy(own_hbm, own_ref, sems.at[1]),
-            pltpu.make_async_copy(state_hbm.at[: 2 * NB, :], state_ref, sems.at[2]),
-        ]
-    )
+    put_state = pltpu.make_async_copy(state_ref, state_hbm, sem)
+    put_state.start()
+    put_state.wait()
+
+
+def spread_kernel(share, step, ids_ref, got_ref, own_ref, state_hbm, send_ref, state_ref, sem):
+    get_state = pltpu.make_async_copy(state_hbm.at[: 2 * NB, :], state_ref, sem)
+    get_state.start()
     total = jnp.sum(got_ref[...], 0)
+    get_state.wait()
     own = own_ref[...]
     line = jnp.sum(state_ref[NB:, :], axis=0, keepdims=True)
     turned = mult(total, state_ref[:NB, :], 1, 1)
@@ -277,16 +271,16 @@
         low_ref[:, at * NB : (at + 1) * NB] = low
     right_high, right_low = high_ref[...], low_ref[...]
     copies = []
-    for m in range(a_ref.shape[0] // cols):
-        k, f = divmod(m, fold)
-        z = got_ref[k * per : (k + 1) * per, f * slim : (f + 1) * slim, :].reshape(NB, NB)
-        high, low = halves(jnp.concatenate([y_ref[m * NB : (m + 1) * NB, :], z], 1))
+    for k in range(a_ref.shape[0] // (fold * cols)):
+        z = [got_ref[k * per : (k + 1) * per, f * slim : (f + 1) * slim, :].reshape(NB, NB) for f in range(fold)]
+        y = y_ref[k * fold * NB : (k + 1) * fold * NB, :]
+        high, low = halves(jnp.concatenate([y, jnp.concatenate(z, 0)], 1))
         change = mult_half(low, right_high) + mult_half(high, right_low) + mult_half(high, right_high)
         for n in range(col_blocks):
-            here = pl.ds(m * NB * col_blocks + n, NB, col_blocks)
+            here = pl.ds(k * fold * cols + n, fold * NB, col_blocks)
             new_ref[here, :] = a_ref[here, :] - change[:, n * NB : (n + 1) * NB]
-        there = pl.ds(m * NB * col_blocks, NB * col_blocks)
-        copy = pltpu.make_async_copy(new_ref.at[there, :], out_ref.at[there, :], sems.at[m])
+        there = pl.ds(k * fold * cols, fold * cols)
+        copy = pltpu.make_async_copy(new_ref.at[there, :], out_ref.at[there, :], sems.at[k])
         copy.start()
         copies.append(copy)
     for copy in copies:
@@ -323,24 +317,40 @@
             cost_estimate=cost(1_000_000, 1_000_000),
         )(ids, got)
 
-    send, top = pl.pallas_call(
+    send = pl.pallas_call(
         lambda *refs: prepare_kernel(col_blocks, fold, slim, *refs),
-        out_shape=(shape(col_count, share + pad, NB), shape(cols, NB)),
+        out_shape=shape(col_count, share + pad, NB),
         in_specs=[SMEM, VMEM],
-        out_specs=(VMEM, VMEM),
+        out_specs=VMEM,
         compiler_params=PARAMS,
         name="prepare",
         cost_estimate=cost(2 * rows * NB * NB * 6, 3_000_000),
     )(ids, lines)
-    got = exchange(send, "col")
+    top = pl.pallas_call(
+        lambda *refs: top_kernel(col_blocks, *refs),
+        out_shape=shape(cols, NB),
+        in_specs=[SMEM, VMEM],
+        out_specs=VMEM,
+        compiler_params=PARAMS,
+        name="top",
+        cost_estimate=cost(1_000_000, 1_000_000),
+    )(ids, lines)
+    got, top = lax.optimization_barrier((exchange(send, "col"), top))
     own, mine, piece = got[1], got[0, :share], got[0, share:]
-    distance = row_count // 2
-    while distance:
-        pairs = [(at, at + distance) for at in range(0, row_count, 2 * distance)]
-        moved = lax.ppermute(top, "row", pairs)
-        top = jnp.where(row_index % (2 * distance) == distance, moved, top)
-        distance //= 2
     pieces = exchange(jnp.broadcast_to(piece[None], (row_count,) + piece.shape), "row")
+    stride = max(row_count // 4, 1)
+
+    def fan(block, leap, rest):
+        sent = []
+        for hop in range(1, min(4, row_count // leap)):
+            pairs = [(at, at + hop * leap) for at in range(0, row_count, 4 * leap)]
+            sent.append(lax.ppermute(block, "row", pairs))
+        rest, *sent = lax.optimization_barrier((rest, *sent))
+        for hop, part in enumerate(sent, 1):
+            block = jnp.where(row_index % (4 * leap) == hop * leap, part, block)
+        return block, rest
+
+    top, pieces = fan(top, stride, pieces)
     send = pl.pallas_call(
         join_kernel,
         out_shape=shape(col_count, share + pad, NB),
@@ -351,6 +361,8 @@
         cost_estimate=cost(1_000_000, 1_000_000),
     )(mine, pieces)
     got = exchange(send, "col")
+    if stride > 1:
+        top, got = fan(top, 1, got)
 
     send, panel = pl.pallas_call(
         lambda *refs: product_kernel(col_blocks, fold, slim, *refs),
@@ -381,17 +393,15 @@
         cost_estimate=cost(4_000_000_000, 2_000_000),
     )(got)
 
+    state = pltpu.with_memory_space_constraint(state, pltpu.HBM)
+    panel = pltpu.with_memory_space_constraint(panel, pltpu.HBM)
+
     send = pl.pallas_call(
         lambda *refs: spread_kernel(share, step, *refs),
         out_shape=shape(row_count, share + pad, NB),
-        in_specs=[SMEM, HBM, HBM, HBM],
+        in_specs=[SMEM, VMEM, VMEM, HBM],
         out_specs=VMEM,
-        scratch_shapes=[
-            pltpu.VMEM((col_count, share + pad, NB), jnp.float32),
-            pltpu.VMEM((share + pad, NB), jnp.float32),
-            pltpu.VMEM((2 * NB, NB), jnp.float32),
-            pltpu.SemaphoreType.DMA((3,)),
-        ],
+        scratch_shapes=[pltpu.VMEM((2 * NB, NB), jnp.float32), pltpu.SemaphoreType.DMA],
         compiler_params=PARAMS,
         name="spread",
         cost_estimate=cost(10_000_000, 1_000_000),
@@ -425,7 +435,7 @@
             pltpu.VMEM((NB, NB), jnp.float32),
             pltpu.VMEM((NB, NB), jnp.float32),
             pltpu.VMEM((rows * col_blocks, NB), jnp.float32),
-            pltpu.SemaphoreType.DMA((row_blocks,)),
+            pltpu.SemaphoreType.DMA((row_blocks // fold,)),
         ],
         compiler_params=PARAMS,
         name="update",

time: 157 us -> 169 us (1.076)
  starting transfers between devices: 52.7 us -> 59.1 us
  waiting for transfers between devices: 38.8 us -> 44.3 us
  local copies, waits for them, and re-layouts: 6 us -> 3.69 us
    all_to_all x5, starting transfers between devices: 31.2 us -> 37.1 us  [exchange(): return lax.all_to_all(pieces, axis, 0, 0)]
    all_to_all x5, waiting for transfers between devices: 27.6 us -> 30.9 us  [exchange(): return lax.all_to_all(pieces, axis, 0, 0)]
    unnamed x12 -> x10, local copies, waits for them, and re-layouts: 4.58 us -> 1.61 us
    ppermute x4 -> x6, waiting for transfers between devices: 11.2 us -> 13.3 us  [fan(): sent.append(lax.ppermute(block, 'row', pairs))]
    ppermute x4 -> x6, starting transfers between devices: 21.5 us -> 22 us  [fan(): sent.append(lax.ppermute(block, 'row', pairs))]
  transfers between devices with their start and end apart: 9 -> 11, of which waited for: 7 -> 7; matrix products, arithmetic and copies ran while one was open for 1% -> 1% of each run, Pallas kernels for 13% -> 12%
where the time goes in v7:
time: 169 us; the launch traced here: 168 us
  starting transfers between devices  59.1 us (35%)
  waiting for transfers between devices  44.3 us (26%)
  Pallas kernels  34 us (20%)
  blocking collectives  26.1 us (15%)
  local copies, waits for them, and re-layouts  3.69 us (2%)
    all_to_all x5, starting transfers between devices, exchange(): return lax.all_to_all(pieces, axis, 0, 0)  37.1 us
    all_to_all x5, waiting for transfers between devices, exchange(): return lax.all_to_all(pieces, axis, 0, 0)  30.9 us
    all_to_all x1, blocking collectives, exchange(): return lax.all_to_all(pieces, axis, 0, 0)  26.1 us
    ppermute x6, starting transfers between devices, fan(): sent.append(lax.ppermute(block, 'row', pairs))  22 us
    ppermute x6, waiting for transfers between devices, fan(): sent.append(lax.ppermute(block, 'row', pairs))  13.3 us
    pallas_call x1, Pallas kernels, body(): pl.pallas_call(lambda *refs: invert_kernel(rows, cols, *refs), out_shape=...  12.5 us
    pallas_call x1, Pallas kernels, body(): pl.pallas_call(lambda *refs: factor_kernel(share, step, *refs), out_shape...  6.83 us
    pallas_call x1, Pallas kernels, body(): pl.pallas_call(lambda *refs: product_kernel(col_blocks, fold, slim, *refs...  4.38 us
  transfers between devices with their start and end apart: 11, of which 7 were waited for; matrix products, arithmetic and copies ran while one was open for 1% of the time, Pallas kernels for 12%

profile of v7, /device:TPU:1, one launch (start us, length us, event | category | flops | bytes accessed | tf_op | source)
XLA Modules:
  0.0 167.8 jit_solution(10169515405369921623)
XLA Ops:
  0.1 1.6 copy-done
  1.7 2.0 %prepare.1 = f32[32,40,128]{2,1,0:T(8,128)} custom-call(s32[2]{0:T(128)S(1)} %pad_add_fusion.refs_0_, f32[4096,128]{1,0:T(8,128)S(1)} %bitcast.12), custom_call_target="tpu_custom_call" | custom-call | flops 201326592 | bytes 3000000 | tf_op jit(solution)/shard_map/prepare/pallas_call | solution.py:320
  3.7 10.4 %all-to-all-start = ((f32[32,40,128]{2,1,0:T(8,128)}), f32[32,40,128]{2,1,0:T(8,128)S(1)}, u32[]{:S(2)}, u32[]{:S(2)}) async-start(f32[32,40,128]{2,1,0:T(8,128)} %prepare.1), calls=%async_computation | async-start | bytes 1310720 | tf_op jit(solution)/shard_map/all_to_all | solution.py:291
  14.1 0.7 top.1
  14.8 12.3 %all-to-all-done = f32[32,40,128]{2,1,0:T(8,128)S(1)} async-done(((f32[32,40,128]{2,1,0:T(8,128)}), f32[32,40,128]{2,1,0:T(8,128)S(1)}, u32[]{:S(2)}, u32[]{:S(2)}) %all-to-all-start) | async-done | bytes 655392 | tf_op jit(solution)/shard_map/all_to_all | solution.py:291
  27.2 10.5 %collective-permute-start.2 = (f32[512,128]{1,0:T(8,128)S(1)}, f32[512,128]{1,0:T(8,128)S(1)}, u32[]{:S(2)}, u32[]{:S(2)}) collective-permute-start(f32[512,128]{1,0:T(8,128)S(1)} %top.1), channel_id=1, source_target_pairs={{0,384},{1,385},{2,386},{3,387},{4,388},{5,389},{6,390},{7,391},{8... | collective-permute-start | bytes 786440 | tf_op jit(solution)/shard_map/ppermute | solution.py:347
  37.7 3.7 %collective-permute-start.1 = (f32[512,128]{1,0:T(8,128)S(1)}, f32[512,128]{1,0:T(8,128)S(1)}, u32[]{:S(2)}, u32[]{:S(2)}) collective-permute-start(f32[512,128]{1,0:T(8,128)S(1)} %top.1), channel_id=1, source_target_pairs={{0,256},{1,257},{2,258},{3,259},{4,260},{5,261},{6,262},{7,263},{8... | collective-permute-start | bytes 786440 | tf_op jit(solution)/shard_map/ppermute | solution.py:347
  41.3 2.0 %collective-permute-start = (f32[512,128]{1,0:T(8,128)S(1)}, f32[512,128]{1,0:T(8,128)}, u32[]{:S(2)}, u32[]{:S(2)}) collective-permute-start(f32[512,128]{1,0:T(8,128)S(1)} %top.1), channel_id=1, source_target_pairs={{0,128},{1,129},{2,130},{3,131},{4,132},{5,133},{6,134},{7,135},{8... | collective-permute-start | bytes 786440 | tf_op jit(solution)/shard_map/ppermute | solution.py:347
  43.4 0.6 broadcast_in_dim.8
  44.0 3.5 %all-to-all-start.1 = ((f32[16,8,128]{2,1,0:T(8,128)}), f32[16,8,128]{2,1,0:T(8,128)S(1)}, u32[]{:S(2)}, u32[]{:S(2)}) async-start(f32[16,8,128]{2,1,0:T(8,128)} %broadcast_in_dim.8), calls=%async_computation.1 | async-start | bytes 131072 | tf_op jit(solution)/shard_map/all_to_all | solution.py:291
  47.5 0.7 slice_bitcast_fusion.1.share_ref
  48.2 10.6 %all-to-all-done.1.got_ref = f32[16,8,128]{2,1,0:T(8,128)S(1)} async-done(((f32[16,8,128]{2,1,0:T(8,128)}), f32[16,8,128]{2,1,0:T(8,128)S(1)}, u32[]{:S(2)}, u32[]{:S(2)}) %all-to-all-start.1) | async-done | bytes 65568 | tf_op jit(solution)/shard_map/all_to_all | solution.py:291
  58.8 0.9 join.1
  59.7 6.3 %all-to-all-start.2 = ((f32[32,40,128]{2,1,0:T(8,128)}), f32[32,40,128]{2,1,0:T(8,128)S(1)}, u32[]{:S(2)}, u32[]{:S(2)}) async-start(f32[32,40,128]{2,1,0:T(8,128)} %join.1), calls=%async_computation.2 | async-start | bytes 1310720 | tf_op jit(solution)/shard_map/all_to_all | solution.py:291
  66.2 2.5 %collective-permute-start.5 = (f32[512,128]{1,0:T(8,128)S(1)}, f32[512,128]{1,0:T(8,128)S(1)}, u32[]{:S(2)}, u32[]{:S(2)}) collective-permute-start(f32[512,128]{1,0:T(8,128)S(1)} %select_select_fusion.1), channel_id=1, source_target_pairs={{0,96},{128,224},{256,352},{384,480},{1,97},{129,225},{257,353},{3... | collective-permute-start | bytes 786440 | tf_op jit(solution)/shard_map/ppermute | solution.py:347
  68.8 1.3 collective-permute-start.4
  70.1 2.0 %collective-permute-start.3 = (f32[512,128]{1,0:T(8,128)S(1)}, f32[512,128]{1,0:T(8,128)}, u32[]{:S(2)}, u32[]{:S(2)}) collective-permute-start(f32[512,128]{1,0:T(8,128)S(1)} %select_select_fusion.1), channel_id=1, source_target_pairs={{0,32},{128,160},{256,288},{384,416},{1,33},{129,161},{257,289},{3... | collective-permute-start | bytes 786440 | tf_op jit(solution)/shard_map/ppermute | solution.py:347
  72.1 2.1 %collective-permute-done.5 = f32[512,128]{1,0:T(8,128)S(1)} collective-permute-done((f32[512,128]{1,0:T(8,128)S(1)}, f32[512,128]{1,0:T(8,128)S(1)}, u32[]{:S(2)}, u32[]{:S(2)}) %collective-permute-start.5) | collective-permute-done | bytes 262176 | tf_op jit(solution)/shard_map/ppermute | solution.py:347
  74.2 5.6 %collective-permute-done.4 = f32[512,128]{1,0:T(8,128)S(1)} collective-permute-done((f32[512,128]{1,0:T(8,128)S(1)}, f32[512,128]{1,0:T(8,128)S(1)}, u32[]{:S(2)}, u32[]{:S(2)}) %collective-permute-start.4) | collective-permute-done | bytes 262176 | tf_op jit(solution)/shard_map/ppermute | solution.py:347
  79.8 5.6 %collective-permute-done.3 = f32[512,128]{1,0:T(8,128)} collective-permute-done((f32[512,128]{1,0:T(8,128)S(1)}, f32[512,128]{1,0:T(8,128)}, u32[]{:S(2)}, u32[]{:S(2)}) %collective-permute-start.3) | collective-permute-done | bytes 262176 | tf_op jit(solution)/shard_map/ppermute | solution.py:347
  85.5 4.4 %product.1 = (f32[32,40,128]{2,1,0:T(8,128)}, f32[1536,128]{1,0:T(8,128)}) custom-call(s32[2]{0:T(128)S(1)} %pad_add_fusion.refs_0_, f32[32,40,128]{2,1,0:T(8,128)S(1)} %all-to-all-done.2.refs_1_.refs_0_, f32[512,128]{1,0:T(8,128)S(1)} %select_select_fusion.refs_2_, f32[4096,128]{1,0:T(8,128)S(1)} %bitcast.14), custom_call_target="tpu_custom_call" | custom-call | flops 805306368 | bytes 4000000 | tf_op jit(solution)/shard_map/product/pallas_call | solution.py:367
  89.9 8.1 %all-to-all-start.3 = ((f32[32,40,128]{2,1,0:T(8,128)}), f32[32,40,128]{2,1,0:T(8,128)S(1)}, u32[]{:S(2)}, u32[]{:S(2)}) async-start(f32[32,40,128]{2,1,0:T(8,128)} %get-tuple-element.29), calls=%async_computation.3 | async-start | bytes 1310720 | tf_op jit(solution)/shard_map/all_to_all | solution.py:291
  98.0 0.7 slice_bitcast_fusion.refs_2_
  98.7 6.8 %factor.1.refs_3_.refs_1_ = f32[384,128]{1,0:T(8,128)} custom-call(f32[32,40,128]{2,1,0:T(8,128)S(1)} %all-to-all-done.2.refs_1_.refs_0_), custom_call_target="tpu_custom_call" | custom-call | flops 4000000000 | bytes 2000000 | tf_op jit(solution)/shard_map/factor/pallas_call | solution.py:383
  105.6 5.3 %all-to-all-done.3.refs_1_ = f32[32,40,128]{2,1,0:T(8,128)S(1)} async-done(((f32[32,40,128]{2,1,0:T(8,128)}), f32[32,40,128]{2,1,0:T(8,128)S(1)}, u32[]{:S(2)}, u32[]{:S(2)}) %all-to-all-start.3) | async-done | bytes 655392 | tf_op jit(solution)/shard_map/all_to_all | solution.py:291
  110.9 2.4 %spread.1 = f32[16,40,128]{2,1,0:T(8,128)} custom-call(s32[2]{0:T(128)S(1)} %pad_add_fusion.refs_0_, f32[32,40,128]{2,1,0:T(8,128)S(1)} %all-to-all-done.3.refs_1_, f32[40,128]{1,0:T(8,128)S(1)} %slice_bitcast_fusion.refs_2_, f32[384,128]{1,0:T(8,128)} %factor.1.refs_3_.refs_1_), custom_call_target="tpu_custom_call" | custom-call | flops 10000000 | bytes 1000000 | tf_op jit(solution)/shard_map/spread/pallas_call | solution.py:399
  113.4 8.7 %all-to-all-start.4 = ((f32[16,40,128]{2,1,0:T(8,128)}), f32[16,40,128]{2,1,0:T(8,128)S(1)}, u32[]{:S(2)}, u32[]{:S(2)}) async-start(f32[16,40,128]{2,1,0:T(8,128)} %spread.1), calls=%async_computation.4 | async-start | bytes 655360 | tf_op jit(solution)/shard_map/all_to_all | solution.py:291
  122.1 12.5 %invert.1.refs_1_ = f32[1920,128]{1,0:T(8,128)S(1)} custom-call(s32[2]{0:T(128)S(1)} %pad_add_fusion.refs_0_, f32[384,128]{1,0:T(8,128)} %factor.1.refs_3_.refs_1_, f32[1536,128]{1,0:T(8,128)} %get-tuple-element.30.refs_2_), custom_call_target="tpu_custom_call" | custom-call | flops 4000000000 | bytes 1000000 | tf_op jit(solution)/shard_map/invert/pallas_call | solution.py:410
  134.6 2.6 %all-to-all-done.4.refs_1_ = f32[16,40,128]{2,1,0:T(8,128)S(1)} async-done(((f32[16,40,128]{2,1,0:T(8,128)}), f32[16,40,128]{2,1,0:T(8,128)S(1)}, u32[]{:S(2)}, u32[]{:S(2)}) %all-to-all-start.4) | async-done | bytes 327712 | tf_op jit(solution)/shard_map/all_to_all | solution.py:291
  137.3 0.6 relay.1
  137.9 26.1 %all_to_all.30.refs_0_ = f32[32,56,128]{2,1,0:T(8,128)S(1)} all-to-all(f32[32,56,128]{2,1,0:T(8,128)S(1)} %relay.1), channel_id=1, replica_groups=mesh['row'=16,'col'=32] {'col'}, dimensions={0} | all-to-all | bytes 1835008 | tf_op jit(solution)/shard_map/all_to_all | solution.py:291
  164.0 3.6 %update.1 = f32[4096,128]{1,0:T(8,128)} custom-call(f32[32,56,128]{2,1,0:T(8,128)S(1)} %all_to_all.30.refs_0_, f32[1920,128]{1,0:T(8,128)S(1)} %invert.1.refs_1_, f32[4096,128]{1,0:T(8,128)S(1)} %bitcast.15), custom_call_target="tpu_custom_call" | custom-call | flops 1610612736 | bytes 6000000 | tf_op jit(solution)/shard_map/update/pallas_call | solution.py:427
  (17 shorter events, 0.3 us)
Async XLA Ops:
  0.1 1.6 copy-start
  1.7 12.5 %copy-start.1 = (f32[8,1,128,4,1,128]{5,4,3,2,1,0:T(1,128)S(1)}, f32[8,1,128,4,1,128]{5,4,3,2,1,0:T(1,128)}, u32[]{:S(2)}) copy-start(f32[8,1,128,4,1,128]{5,4,3,2,1,0:T(1,128)} %param.1) | copy-start | bytes 6291460
  3.7 23.5 %all-to-all-start = ((f32[32,40,128]{2,1,0:T(8,128)}), f32[32,40,128]{2,1,0:T(8,128)S(1)}, u32[]{:S(2)}, u32[]{:S(2)}) async-start(f32[32,40,128]{2,1,0:T(8,128)} %prepare.1), calls=%async_computation | async-start | bytes 1310720 | tf_op jit(solution)/shard_map/all_to_all | solution.py:291
  27.2 16.8 %copy-start.2 = (f32[32,40,128]{2,1,0:T(8,128)}, f32[32,40,128]{2,1,0:T(8,128)S(1)}, u32[]{:S(2)}) copy-start(f32[32,40,128]{2,1,0:T(8,128)S(1)} %all-to-all-done) | copy-start | bytes 1966084
  27.2 31.7 %collective-permute-start.2 = (f32[512,128]{1,0:T(8,128)S(1)}, f32[512,128]{1,0:T(8,128)S(1)}, u32[]{:S(2)}, u32[]{:S(2)}) collective-permute-start(f32[512,128]{1,0:T(8,128)S(1)} %top.1), channel_id=1, source_target_pairs={{0,384},{1,385},{2,386},{3,387},{4,388},{5,389},{6,390},{7,391},{8... | collective-permute-start | bytes 786440 | tf_op jit(solution)/shard_map/ppermute | solution.py:347
  37.7 21.2 %collective-permute-start.1 = (f32[512,128]{1,0:T(8,128)S(1)}, f32[512,128]{1,0:T(8,128)S(1)}, u32[]{:S(2)}, u32[]{:S(2)}) collective-permute-start(f32[512,128]{1,0:T(8,128)S(1)} %top.1), channel_id=1, source_target_pairs={{0,256},{1,257},{2,258},{3,259},{4,260},{5,261},{6,262},{7,263},{8... | collective-permute-start | bytes 786440 | tf_op jit(solution)/shard_map/ppermute | solution.py:347
  41.3 17.5 %collective-permute-start = (f32[512,128]{1,0:T(8,128)S(1)}, f32[512,128]{1,0:T(8,128)}, u32[]{:S(2)}, u32[]{:S(2)}) collective-permute-start(f32[512,128]{1,0:T(8,128)S(1)} %top.1), channel_id=1, source_target_pairs={{0,128},{1,129},{2,130},{3,131},{4,132},{5,133},{6,134},{7,135},{8... | collective-permute-start | bytes 786440 | tf_op jit(solution)/shard_map/ppermute | solution.py:347
  44.0 14.8 %all-to-all-start.1 = ((f32[16,8,128]{2,1,0:T(8,128)}), f32[16,8,128]{2,1,0:T(8,128)S(1)}, u32[]{:S(2)}, u32[]{:S(2)}) async-start(f32[16,8,128]{2,1,0:T(8,128)} %broadcast_in_dim.8), calls=%async_computation.1 | async-start | bytes 131072 | tf_op jit(solution)/shard_map/all_to_all | solution.py:291
  58.8 7.3 %copy-start.3 = (f32[512,128]{1,0:T(8,128)}, f32[512,128]{1,0:T(8,128)S(1)}, u32[]{:S(2)}) copy-start(f32[512,128]{1,0:T(8,128)S(1)} %collective-permute-done.1) | copy-start | bytes 786436
  59.7 25.7 %all-to-all-start.2 = ((f32[32,40,128]{2,1,0:T(8,128)}), f32[32,40,128]{2,1,0:T(8,128)S(1)}, u32[]{:S(2)}, u32[]{:S(2)}) async-start(f32[32,40,128]{2,1,0:T(8,128)} %join.1), calls=%async_computation.2 | async-start | bytes 1310720 | tf_op jit(solution)/shard_map/all_to_all | solution.py:291
  66.2 8.0 %collective-permute-start.5 = (f32[512,128]{1,0:T(8,128)S(1)}, f32[512,128]{1,0:T(8,128)S(1)}, u32[]{:S(2)}, u32[]{:S(2)}) collective-permute-start(f32[512,128]{1,0:T(8,128)S(1)} %select_select_fusion.1), channel_id=1, source_target_pairs={{0,96},{128,224},{256,352},{384,480},{1,97},{129,225},{257,353},{3... | collective-permute-start | bytes 786440 | tf_op jit(solution)/shard_map/ppermute | solution.py:347
  68.8 11.1 %collective-permute-start.4 = (f32[512,128]{1,0:T(8,128)S(1)}, f32[512,128]{1,0:T(8,128)S(1)}, u32[]{:S(2)}, u32[]{:S(2)}) collective-permute-start(f32[512,128]{1,0:T(8,128)S(1)} %select_select_fusion.1), channel_id=1, source_target_pairs={{0,64},{128,192},{256,320},{384,448},{1,65},{129,193},{257,321},{3... | collective-permute-start | bytes 786440 | tf_op jit(solution)/shard_map/ppermute | solution.py:347
  70.1 15.4 %collective-permute-start.3 = (f32[512,128]{1,0:T(8,128)S(1)}, f32[512,128]{1,0:T(8,128)}, u32[]{:S(2)}, u32[]{:S(2)}) collective-permute-start(f32[512,128]{1,0:T(8,128)S(1)} %select_select_fusion.1), channel_id=1, source_target_pairs={{0,32},{128,160},{256,288},{384,416},{1,33},{129,161},{257,289},{3... | collective-permute-start | bytes 786440 | tf_op jit(solution)/shard_map/ppermute | solution.py:347
  79.8 5.6 %copy-start.4 = (f32[512,128]{1,0:T(8,128)}, f32[512,128]{1,0:T(8,128)S(1)}, u32[]{:S(2)}) copy-start(f32[512,128]{1,0:T(8,128)S(1)} %collective-permute-done.4) | copy-start | bytes 786436
  89.9 21.0 %all-to-all-start.3 = ((f32[32,40,128]{2,1,0:T(8,128)}), f32[32,40,128]{2,1,0:T(8,128)S(1)}, u32[]{:S(2)}, u32[]{:S(2)}) async-start(f32[32,40,128]{2,1,0:T(8,128)} %get-tuple-element.29), calls=%async_computation.3 | async-start | bytes 1310720 | tf_op jit(solution)/shard_map/all_to_all | solution.py:291
  113.4 23.9 %all-to-all-start.4 = ((f32[16,40,128]{2,1,0:T(8,128)}), f32[16,40,128]{2,1,0:T(8,128)S(1)}, u32[]{:S(2)}, u32[]{:S(2)}) async-start(f32[16,40,128]{2,1,0:T(8,128)} %spread.1), calls=%async_computation.4 | async-start | bytes 655360 | tf_op jit(solution)/shard_map/all_to_all | solution.py:291

commit v8 on v5

--- a/solution.py
+++ b/solution.py
@@ -92,13 +92,6 @@
         rows = right[i] - ratio * pltpu.roll(right[i], 1, 0)
         out.append(rows * lax.rsqrt(diag - ratio * below))
     return out
-
-
-def fetch(copies):
-    for copy in copies:
-        copy.start()
-    for copy in copies:
-        copy.wait()
 
 
 def invert_kernel(rows, cols, ids_ref, state_hbm, panel_hbm, pack_ref, state_ref, panel_ref, sems):
@@ -140,11 +133,13 @@
     pack_ref[4 * NB + cols :, :] = y[NB:rows]
 
 
-def prepare_kernel(col_blocks, fold, slim, ids_ref, a_ref, send_ref):
-    rows = a_ref.shape[0] // col_blocks
-    col_count = send_ref.shape[0]
+def prepare_kernel(fold, slim, ids_ref, a_hbm, send_ref, panel_ref, sem):
+    rows, col_count = a_hbm.shape[0], send_ref.shape[0]
     share, step, per = fold * slim, NB // col_count, NB // slim
-    panel = a_ref[pl.ds(0, rows, col_blocks), :]
+    get_panel = pltpu.make_async_copy(a_hbm.at[:, 0, :], panel_ref, sem)
+    get_panel.start()
+    get_panel.wait()
+    panel = panel_ref[...]
     first = jnp.where((ids_ref[0] == 0) & (ids_ref[1] == 0), 0.0, panel[:NB])
     panel = jnp.concatenate([first, panel[NB:]], 0)
     gram = mult(panel, panel, 0, 0)
@@ -214,18 +209,16 @@
     for i in range(count):
         here = jnp.where(lane_id == sub_id + SUB * i, 1.0, 0.0)
         state_ref[NB + SUB * i : NB + SUB * i + SUB, :] = here * signs[SUB * i : SUB * i + SUB]
-    fetch([pltpu.make_async_copy(state_ref, state_hbm, sem)])
-
-
-def spread_kernel(share, step, ids_ref, got_hbm, own_hbm, state_hbm, send_ref, got_ref, own_ref, state_ref, sems):
-    fetch(
-        [
-            pltpu.make_async_copy(got_hbm, got_ref, sems.at[0]),
-            pltpu.make_async_copy(own_hbm, own_ref, sems.at[1]),
-            pltpu.make_async_copy(state_hbm.at[: 2 * NB, :], state_ref, sems.at[2]),
-        ]
-    )
+    put_state = pltpu.make_async_copy(state_ref, state_hbm, sem)
+    put_state.start()
+    put_state.wait()
+
+
+def spread_kernel(share, step, ids_ref, got_ref, own_ref, state_hbm, send_ref, state_ref, sem):
+    get_state = pltpu.make_async_copy(state_hbm.at[: 2 * NB, :], state_ref, sem)
+    get_state.start()
     total = jnp.sum(got_ref[...], 0)
+    get_state.wait()
     own = own_ref[...]
     line = jnp.sum(state_ref[NB:, :], axis=0, keepdims=True)
     turned = mult(total, state_ref[:NB, :], 1, 1)
@@ -265,16 +258,16 @@
         low_ref[:, at * NB : (at + 1) * NB] = low
     right_high, right_low = high_ref[...], low_ref[...]
     copies = []
-    for m in range(a_ref.shape[0] // cols):
-        k, f = divmod(m, fold)
-        z = got_ref[k * per : (k + 1) * per, f * slim : (f + 1) * slim, :].reshape(NB, NB)
-        high, low = halves(jnp.concatenate([y_ref[m * NB : (m + 1) * NB, :], z], 1))
+    for k in range(a_ref.shape[0] // (fold * cols)):
+        z = [got_ref[k * per : (k + 1) * per, f * slim : (f + 1) * slim, :].reshape(NB, NB) for f in range(fold)]
+        y = y_ref[k * fold * NB : (k + 1) * fold * NB, :]
+        high, low = halves(jnp.concatenate([y, jnp.concatenate(z, 0)], 1))
         change = mult_half(low, right_high) + mult_half(high, right_low) + mult_half(high, right_high)
         for n in range(col_blocks):
-            here = pl.ds(m * NB * col_blocks + n, NB, col_blocks)
+            here = pl.ds(k * fold * cols + n, fold * NB, col_blocks)
             new_ref[here, :] = a_ref[here, :] - change[:, n * NB : (n + 1) * NB]
-        there = pl.ds(m * NB * col_blocks, NB * col_blocks)
-        copy = pltpu.make_async_copy(new_ref.at[there, :], out_ref.at[there, :], sems.at[m])
+        there = pl.ds(k * fold * cols, fold * cols)
+        copy = pltpu.make_async_copy(new_ref.at[there, :], out_ref.at[there, :], sems.at[k])
         copy.start()
         copies.append(copy)
     for copy in copies:
@@ -297,6 +290,9 @@
     share = fold * slim
     pad = 2 * step
 
+    def hbm(*dims):
+        return pltpu.HBM(dims, jnp.float32)
+
     def relay(got):
         return pl.pallas_call(
             lambda *refs: relay_kernel(fold, slim, *refs),
@@ -309,14 +305,15 @@
         )(ids, got)
 
     send = pl.pallas_call(
-        lambda *refs: prepare_kernel(col_blocks, fold, slim, *refs),
+        lambda *refs: prepare_kernel(fold, slim, *refs),
         out_shape=shape(col_count, share + pad, NB),
-        in_specs=[SMEM, VMEM],
+        in_specs=[SMEM, HBM],
         out_specs=VMEM,
+        scratch_shapes=[pltpu.VMEM((rows, NB), jnp.float32), pltpu.SemaphoreType.DMA],
         compiler_params=PARAMS,
         name="prepare",
         cost_estimate=cost(2 * rows * NB * NB * 6, 3_000_000),
-    )(ids, lines)
+    )(ids, pltpu.with_memory_space_constraint(kernel.reshape(rows, col_blocks, NB), pltpu.HBM))
     got = exchange(send, "col")
     own = got[1]
     got = jnp.broadcast_to(got[0][None], (row_count,) + got.shape[1:])
@@ -324,7 +321,7 @@
 
     send, panel = pl.pallas_call(
         lambda *refs: product_kernel(col_blocks, fold, slim, *refs),
-        out_shape=(shape(col_count, share + pad, NB), shape(rows + cols, NB)),
+        out_shape=(hbm(col_count, share + pad, NB), hbm(rows + cols, NB)),
         in_specs=[SMEM, VMEM, VMEM],
         out_specs=(HBM, HBM),
         scratch_shapes=[
@@ -340,7 +337,7 @@
     summed = exchange(send, "col")
     state = pl.pallas_call(
         lambda *refs: factor_kernel(share + slim, step, *refs),
-        out_shape=shape(3 * NB, NB),
+        out_shape=hbm(3 * NB, NB),
         in_specs=[VMEM],
         out_specs=HBM,
         scratch_shapes=[pltpu.VMEM((3 * NB, NB), jnp.float32)]
@@ -351,17 +348,15 @@
         cost_estimate=cost(4_000_000_000, 2_000_000),
     )(got)
 
+    state = pltpu.with_memory_space_constraint(state, pltpu.HBM)
+    panel = pltpu.with_memory_space_constraint(panel, pltpu.HBM)
+
     send = pl.pallas_call(
         lambda *refs: spread_kernel(share, step, *refs),
         out_shape=shape(row_count, share + pad, NB),
-        in_specs=[SMEM, HBM, HBM, HBM],
+        in_specs=[SMEM, VMEM, VMEM, HBM],
         out_specs=VMEM,
-        scratch_shapes=[
-            pltpu.VMEM((col_count, share + pad, NB), jnp.float32),
-            pltpu.VMEM((share + pad, NB), jnp.float32),
-            pltpu.VMEM((2 * NB, NB), jnp.float32),
-            pltpu.SemaphoreType.DMA((3,)),
-        ],
+        scratch_shapes=[pltpu.VMEM((2 * NB, NB), jnp.float32), pltpu.SemaphoreType.DMA],
         compiler_params=PARAMS,
         name="spread",
         cost_estimate=cost(10_000_000, 1_000_000),
@@ -395,7 +390,7 @@
             pltpu.VMEM((NB, NB), jnp.float32),
             pltpu.VMEM((NB, NB), jnp.float32),
             pltpu.VMEM((rows * col_blocks, NB), jnp.float32),
-            pltpu.SemaphoreType.DMA((row_blocks,)),
+            pltpu.SemaphoreType.DMA((row_blocks // fold,)),
         ],
         compiler_params=PARAMS,
         name="update",

time: 160 us -> 157 us (0.981)
  local copies, waits for them, and re-layouts: 5.41 us -> 0.03 us
  Pallas kernels: 31.8 us -> 33.8 us
    unnamed x14 -> x2, local copies, waits for them, and re-layouts: 5.38 us -> 0.01 us
where the time goes in v8:
time: 157 us
  blocking collectives  103 us (66%)
  Pallas kernels  33.8 us (22%)
  starting transfers between devices  10.2 us (6%)
  waiting for transfers between devices  8.86 us (6%)
    all_to_all x4, blocking collectives, exchange(): return lax.all_to_all(pieces, axis, 0, 0)  103 us
    pallas_call x1, Pallas kernels, body(): pl.pallas_call(lambda *refs: invert_kernel(rows, cols, *refs), out_shape=...  12.5 us
    all_to_all x2, starting transfers between devices, exchange(): return lax.all_to_all(pieces, axis, 0, 0)  10.2 us
    all_to_all x2, waiting for transfers between devices, exchange(): return lax.all_to_all(pieces, axis, 0, 0)  8.86 us
    pallas_call x1, Pallas kernels, body(): pl.pallas_call(lambda *refs: factor_kernel(share + slim, step, *refs), ou...  6.84 us
    pallas_call x1, Pallas kernels, body(): pl.pallas_call(lambda *refs: product_kernel(col_blocks, fold, slim, *refs...  4.37 us
    pallas_call x1, Pallas kernels, body(): pl.pallas_call(lambda *refs: update_kernel(col_blocks, fold, slim, *refs)...  3.64 us
  transfers between devices with their start and end apart: 2, of which 2 were waited for; matrix products, arithmetic and copies ran while one was open for 0% of the time, Pallas kernels for 12%

profile of v8, /device:TPU:1, one launch (start us, length us, event | category | flops | bytes accessed | tf_op | source)
XLA Modules:
  0.0 156.7 jit_solution(8429636776329905422)
XLA Ops:
  0.0 0.1 pad_add_fusion.refs_0_
  0.1 2.2 %prepare.1 = f32[32,40,128]{2,1,0:T(8,128)S(1)} custom-call(s32[2]{0:T(128)S(1)} %pad_add_fusion.refs_0_, f32[1024,4,128]{2,1,0:T(4,128)} %bitcast.11), custom_call_target="tpu_custom_call" | custom-call | flops 201326592 | bytes 3000000 | tf_op jit(solution)/shard_map/prepare/pallas_call | solution.py:307
  2.3 22.5 %all_to_all.30 = f32[32,40,128]{2,1,0:T(8,128)S(1)} all-to-all(f32[32,40,128]{2,1,0:T(8,128)S(1)} %prepare.1), channel_id=1, replica_groups=mesh['row'=16,'col'=32] {'col'}, dimensions={0} | all-to-all | bytes 1310720 | tf_op jit(solution)/shard_map/all_to_all | solution.py:278
  24.9 0.0 copy-start
  24.9 28.8 %all_to_all.31.refs_1_ = f32[16,40,128]{2,1,0:T(8,128)S(1)} all-to-all(f32[16,40,128]{2,1,0:T(8,128)S(1)} %broadcast_in_dim.8), channel_id=1, replica_groups=mesh['row'=16,'col'=32] {'row'}, dimensions={0} | all-to-all | bytes 655360 | tf_op jit(solution)/shard_map/all_to_all | solution.py:278
  53.7 0.6 relay.2
  54.3 26.1 %all_to_all.32.refs_1_.refs_0_ = f32[32,56,128]{2,1,0:T(8,128)S(1)} all-to-all(f32[32,56,128]{2,1,0:T(8,128)S(1)} %relay.2), channel_id=1, replica_groups=mesh['row'=16,'col'=32] {'col'}, dimensions={0} | all-to-all | bytes 1835008 | tf_op jit(solution)/shard_map/all_to_all | solution.py:278
  80.4 0.0 copy-done
  80.4 4.4 %product.1 = (f32[32,40,128]{2,1,0:T(8,128)}, f32[1536,128]{1,0:T(8,128)}) custom-call(s32[2]{0:T(128)S(1)} %pad_add_fusion.refs_0_, f32[32,56,128]{2,1,0:T(8,128)S(1)} %all_to_all.32.refs_1_.refs_0_, f32[4096,128]{1,0:T(8,128)S(1)} %bitcast.12), custom_call_target="tpu_custom_call" | custom-call | flops 805306368 | bytes 4000000 | tf_op jit(solution)/shard_map/product/pallas_call | solution.py:322
  84.7 4.6 %all-to-all-start.3 = ((f32[32,40,128]{2,1,0:T(8,128)}), f32[32,40,128]{2,1,0:T(8,128)}, u32[]{:S(2)}, u32[]{:S(2)}) async-start(f32[32,40,128]{2,1,0:T(8,128)} %get-tuple-element.9), calls=%async_computation.3 | async-start | bytes 1310720 | tf_op jit(solution)/shard_map/all_to_all | solution.py:278
  89.4 6.8 %factor.1.refs_3_.refs_1_ = f32[384,128]{1,0:T(8,128)} custom-call(f32[32,56,128]{2,1,0:T(8,128)S(1)} %all_to_all.32.refs_1_.refs_0_), custom_call_target="tpu_custom_call" | custom-call | flops 4000000000 | bytes 2000000 | tf_op jit(solution)/shard_map/factor/pallas_call | solution.py:338
  96.2 6.2 %all-to-all-done.3.refs_1_ = f32[32,40,128]{2,1,0:T(8,128)} async-done(((f32[32,40,128]{2,1,0:T(8,128)}), f32[32,40,128]{2,1,0:T(8,128)}, u32[]{:S(2)}, u32[]{:S(2)}) %all-to-all-start.3) | async-done | bytes 655392 | tf_op jit(solution)/shard_map/all_to_all | solution.py:278
  102.5 3.0 %spread.1 = f32[16,40,128]{2,1,0:T(8,128)} custom-call(s32[2]{0:T(128)S(1)} %pad_add_fusion.refs_0_, f32[32,40,128]{2,1,0:T(8,128)} %all-to-all-done.3.refs_1_, f32[40,128]{1,0:T(8,128)S(1)} %get-tuple-element.13.refs_2_, f32[384,128]{1,0:T(8,128)} %factor.1.refs_3_.refs_1_), custom_call_target="tpu_custom_call" | custom-call | flops 10000000 | bytes 1000000 | tf_op jit(solution)/shard_map/spread/pallas_call | solution.py:354
  105.4 5.6 %all-to-all-start.4 = ((f32[16,40,128]{2,1,0:T(8,128)}), f32[16,40,128]{2,1,0:T(8,128)S(1)}, u32[]{:S(2)}, u32[]{:S(2)}) async-start(f32[16,40,128]{2,1,0:T(8,128)} %spread.1), calls=%async_computation.4 | async-start | bytes 655360 | tf_op jit(solution)/shard_map/all_to_all | solution.py:278
  111.1 12.5 %invert.1.refs_1_ = f32[1920,128]{1,0:T(8,128)S(1)} custom-call(s32[2]{0:T(128)S(1)} %pad_add_fusion.refs_0_, f32[384,128]{1,0:T(8,128)} %factor.1.refs_3_.refs_1_, f32[1536,128]{1,0:T(8,128)} %get-tuple-element.10.refs_2_), custom_call_target="tpu_custom_call" | custom-call | flops 4000000000 | bytes 1000000 | tf_op jit(solution)/shard_map/invert/pallas_call | solution.py:365
  123.6 2.6 %all-to-all-done.4.refs_1_ = f32[16,40,128]{2,1,0:T(8,128)S(1)} async-done(((f32[16,40,128]{2,1,0:T(8,128)}), f32[16,40,128]{2,1,0:T(8,128)S(1)}, u32[]{:S(2)}, u32[]{:S(2)}) %all-to-all-start.4) | async-done | bytes 327712 | tf_op jit(solution)/shard_map/all_to_all | solution.py:278
  126.2 0.6 relay.3
  126.8 26.0 %all_to_all.33.refs_0_ = f32[32,56,128]{2,1,0:T(8,128)S(1)} all-to-all(f32[32,56,128]{2,1,0:T(8,128)S(1)} %relay.3), channel_id=1, replica_groups=mesh['row'=16,'col'=32] {'col'}, dimensions={0} | all-to-all | bytes 1835008 | tf_op jit(solution)/shard_map/all_to_all | solution.py:278
  152.9 3.6 %update.1 = f32[4096,128]{1,0:T(8,128)} custom-call(f32[32,56,128]{2,1,0:T(8,128)S(1)} %all_to_all.33.refs_0_, f32[1920,128]{1,0:T(8,128)S(1)} %invert.1.refs_1_, f32[4096,128]{1,0:T(8,128)S(1)} %bitcast.13), custom_call_target="tpu_custom_call" | custom-call | flops 1610612736 | bytes 6000000 | tf_op jit(solution)/shard_map/update/pallas_call | solution.py:382
  (2 shorter events, 0.0 us)
Async XLA Ops:
  24.9 55.5 %copy-start = (f32[8,1,128,4,1,128]{5,4,3,2,1,0:T(1,128)S(1)}, f32[8,1,128,4,1,128]{5,4,3,2,1,0:T(1,128)}, u32[]{:S(2)}) copy-start(f32[8,1,128,4,1,128]{5,4,3,2,1,0:T(1,128)} %param.1) | copy-start | bytes 6291460
  84.7 17.7 %all-to-all-start.3 = ((f32[32,40,128]{2,1,0:T(8,128)}), f32[32,40,128]{2,1,0:T(8,128)}, u32[]{:S(2)}, u32[]{:S(2)}) async-start(f32[32,40,128]{2,1,0:T(8,128)} %get-tuple-element.9), calls=%async_computation.3 | async-start | bytes 1310720 | tf_op jit(solution)/shard_map/all_to_all | solution.py:278
  105.4 20.8 %all-to-all-start.4 = ((f32[16,40,128]{2,1,0:T(8,128)}), f32[16,40,128]{2,1,0:T(8,128)S(1)}, u32[]{:S(2)}, u32[]{:S(2)}) async-start(f32[16,40,128]{2,1,0:T(8,128)} %spread.1), calls=%async_computation.4 | async-start | bytes 655360 | tf_op jit(solution)/shard_map/all_to_all | solution.py:278

commit v9 on v8

--- a/solution.py
+++ b/solution.py
@@ -163,37 +163,59 @@
         send_ref[f * row_count : (f + 1) * row_count, share : share + slim, :] = got_ref[:, f * slim : (f + 1) * slim, :]
 
 
-def product_kernel(col_blocks, fold, slim, ids_ref, got_ref, a_ref, send_hbm, panel_hbm, send_ref, panel_ref, hold_ref, sems):
+def thirds(value):
+    one = value.astype(jnp.bfloat16)
+    rest = value - one.astype(jnp.float32)
+    two = rest.astype(jnp.bfloat16)
+    return one, two, (rest - two.astype(jnp.float32)).astype(jnp.bfloat16)
+
+
+def mult_packed(left, right):
+    one, two, three = thirds(left)
+    first, second, third = thirds(right)
+    pair = jnp.concatenate([first, second], 1)
+    width = right.shape[1]
+
+    def dot(x, y):
+        return lax.dot_general(x, y, (((1,), (0,)), ((), ())), preferred_element_type=jnp.float32)
+
+    high, low = dot(one, pair), dot(two, pair)
+    tail = dot(one, third) + dot(three, first)
+    return ((low[:, width:] + tail) + (high[:, width:] + low[:, :width])) + high[:, :width]
+
+
+def product_kernel(col_blocks, fold, slim, ids_ref, got_ref, a_ref, send_hbm, send_ref, hold_ref, sems):
     col_count = got_ref.shape[0]
     rows, cols = a_ref.shape[0] // col_blocks, col_blocks * NB
     share, step, per = fold * slim, NB // col_count, NB // slim
-    panel_ref[rows:, :] = got_ref[:, share : share + slim, :].reshape(cols, NB)
-    for m in range(rows // NB):
-        k, f = divmod(m, fold)
-        panel_ref[m * NB : (m + 1) * NB, :] = got_ref[k * per : (k + 1) * per, f * slim : (f + 1) * slim, :].reshape(NB, NB)
-    put_panel = pltpu.make_async_copy(panel_ref, panel_hbm, sems.at[0])
-    put_panel.start()
-    part = jnp.zeros((rows, NB), jnp.float32)
-    for k in range(col_blocks):
-        part = part + mult(a_ref[pl.ds(k, rows, col_blocks), :], panel_ref[rows + k * NB : rows + (k + 1) * NB, :])
+    block = jnp.concatenate([a_ref[pl.ds(k, rows, col_blocks), :] for k in range(col_blocks)], 1)
+    part = mult_packed(block, got_ref[:, share : share + slim, :].reshape(cols, NB))
+    panel = []
     for m in range(rows // NB):
         k, f = divmod(m, fold)
         send_ref[k * per : (k + 1) * per, f * slim : (f + 1) * slim, :] = part[m * NB : (m + 1) * NB].reshape(per, slim, NB)
-    put_share = pltpu.make_async_copy(send_ref.at[:, :share, :], send_hbm.at[:, :share, :], sems.at[1])
+        panel.append(got_ref[k * per : (k + 1) * per, f * slim : (f + 1) * slim, :].reshape(NB, NB))
+    put_share = pltpu.make_async_copy(send_ref.at[:, :share, :], send_hbm.at[:, :share, :], sems.at[0])
     put_share.start()
-    hold_ref[...] = mult(panel_ref[:rows, :], part, 0, 0)
+    hold_ref[...] = mult(jnp.concatenate(panel, 0), part, 0, 0)
     lead = jnp.where(ids_ref[0] == 1, part[:NB], 0.0)
     for c in range(col_count):
         send_ref[c, share : share + step, :] = hold_ref[c * step : (c + 1) * step, :]
         send_ref[c, share + step : share + 2 * step, :] = lead[c * step : (c + 1) * step]
-    put_piece = pltpu.make_async_copy(send_ref.at[:, share:, :], send_hbm.at[:, share:, :], sems.at[2])
+    put_piece = pltpu.make_async_copy(send_ref.at[:, share:, :], send_hbm.at[:, share:, :], sems.at[1])
     put_piece.start()
-    put_panel.wait()
     put_share.wait()
     put_piece.wait()
 
 
-def factor_kernel(share, step, got_ref, state_hbm, state_ref, hold_ref, lead_ref, sem):
+def factor_kernel(rows, fold, slim, step, got_ref, state_hbm, panel_hbm, state_ref, panel_ref, hold_ref, lead_ref, sems):
+    share, per = (fold + 1) * slim, NB // slim
+    for m in range(rows // NB):
+        k, f = divmod(m, fold)
+        panel_ref[m * NB : (m + 1) * NB, :] = got_ref[k * per : (k + 1) * per, f * slim : (f + 1) * slim, :].reshape(NB, NB)
+    panel_ref[rows:, :] = got_ref[:, fold * slim : share, :].reshape(panel_ref.shape[0] - rows, NB)
+    put_panel = pltpu.make_async_copy(panel_ref, panel_hbm, sems.at[1])
+    put_panel.start()
     count = NB // SUB
     sub_id, lane_id = lane_ids()
     for c in range(got_ref.shape[0]):
@@ -209,14 +231,18 @@
     for i in range(count):
         here = jnp.where(lane_id == sub_id + SUB * i, 1.0, 0.0)
         state_ref[NB + SUB * i : NB + SUB * i + SUB, :] = here * signs[SUB * i : SUB * i + SUB]
-    put_state = pltpu.make_async_copy(state_ref, state_hbm, sem)
+    put_state = pltpu.make_async_copy(state_ref, state_hbm, sems.at[0])
     put_state.start()
     put_state.wait()
-
-
-def spread_kernel(share, step, ids_ref, got_ref, own_ref, state_hbm, send_ref, state_ref, sem):
-    get_state = pltpu.make_async_copy(state_hbm.at[: 2 * NB, :], state_ref, sem)
+    put_panel.wait()
+
+
+def spread_kernel(share, step, ids_ref, got_hbm, own_ref, state_hbm, send_ref, got_ref, state_ref, sems):
+    get_got = pltpu.make_async_copy(got_hbm, got_ref, sems.at[0])
+    get_state = pltpu.make_async_copy(state_hbm.at[: 2 * NB, :], state_ref, sems.at[1])
+    get_got.start()
     get_state.start()
+    get_got.wait()
     total = jnp.sum(got_ref[...], 0)
     get_state.wait()
     own = own_ref[...]
@@ -233,8 +259,15 @@
     return high, (value - high.astype(jnp.float32)).astype(jnp.bfloat16)
 
 
-def mult_half(left, right):
-    return lax.dot_general(left, right, (((1,), (1,)), ((), ())), preferred_element_type=jnp.float32)
+def mult_half(left, right, right_dim=1):
+    return lax.dot_general(left, right, (((1,), (right_dim,)), ((), ())), preferred_element_type=jnp.float32)
+
+
+def mult_halves(left, right, right_dim):
+    high, low = halves(left)
+    right_high, right_low = halves(right)
+    small = mult_half(low, right_high, right_dim) + mult_half(high, right_low, right_dim)
+    return small + mult_half(high, right_high, right_dim)
 
 
 def update_kernel(
@@ -251,7 +284,7 @@
     cross = jnp.sum(pack_ref[2 * NB : 3 * NB, :], axis=1, keepdims=True) * lead_ref[...]
     middle = mult(mult(inverse, hold_ref[...]), inverse, 1, 1) - cross - cross.T
     z_cols = got_ref[:, share : share + slim, :].reshape(cols, NB)
-    u = mult(z_cols - mult(v, middle), coupling, 1, 1)
+    u = mult_halves(z_cols - mult_halves(v, middle, 0), coupling, 1)
     for at, part in enumerate((u, v)):
         high, low = halves(part)
         high_ref[:, at * NB : (at + 1) * NB] = high
@@ -319,44 +352,46 @@
     got = jnp.broadcast_to(got[0][None], (row_count,) + got.shape[1:])
     got = exchange(relay(exchange(got, "row")), "col")
 
-    send, panel = pl.pallas_call(
+    send = pl.pallas_call(
         lambda *refs: product_kernel(col_blocks, fold, slim, *refs),
-        out_shape=(hbm(col_count, share + pad, NB), hbm(rows + cols, NB)),
+        out_shape=hbm(col_count, share + pad, NB),
         in_specs=[SMEM, VMEM, VMEM],
-        out_specs=(HBM, HBM),
+        out_specs=HBM,
         scratch_shapes=[
             pltpu.VMEM((col_count, share + pad, NB), jnp.float32),
-            pltpu.VMEM((rows + cols, NB), jnp.float32),
             pltpu.VMEM((NB, NB), jnp.float32),
-            pltpu.SemaphoreType.DMA((3,)),
+            pltpu.SemaphoreType.DMA((2,)),
         ],
         compiler_params=PARAMS,
         name="product",
         cost_estimate=cost(2 * rows * cols * NB * 6, 4_000_000),
     )(ids, got, lines)
     summed = exchange(send, "col")
-    state = pl.pallas_call(
-        lambda *refs: factor_kernel(share + slim, step, *refs),
-        out_shape=hbm(3 * NB, NB),
+    state, panel = pl.pallas_call(
+        lambda *refs: factor_kernel(rows, fold, slim, step, *refs),
+        out_shape=(hbm(3 * NB, NB), hbm(rows + cols, NB)),
         in_specs=[VMEM],
-        out_specs=HBM,
-        scratch_shapes=[pltpu.VMEM((3 * NB, NB), jnp.float32)]
+        out_specs=(HBM, HBM),
+        scratch_shapes=[pltpu.VMEM((3 * NB, NB), jnp.float32), pltpu.VMEM((rows + cols, NB), jnp.float32)]
         + [pltpu.VMEM((NB, NB), jnp.float32)] * 2
-        + [pltpu.SemaphoreType.DMA],
+        + [pltpu.SemaphoreType.DMA((2,))],
         compiler_params=PARAMS,
         name="factor",
         cost_estimate=cost(4_000_000_000, 2_000_000),
     )(got)
-
     state = pltpu.with_memory_space_constraint(state, pltpu.HBM)
     panel = pltpu.with_memory_space_constraint(panel, pltpu.HBM)
 
     send = pl.pallas_call(
         lambda *refs: spread_kernel(share, step, *refs),
         out_shape=shape(row_count, share + pad, NB),
-        in_specs=[SMEM, VMEM, VMEM, HBM],
+        in_specs=[SMEM, HBM, VMEM, HBM],
         out_specs=VMEM,
-        scratch_shapes=[pltpu.VMEM((2 * NB, NB), jnp.float32), pltpu.SemaphoreType.DMA],
+        scratch_shapes=[
+            pltpu.VMEM((col_count, share + pad, NB), jnp.float32),
+            pltpu.VMEM((2 * NB, NB), jnp.float32),
+            pltpu.SemaphoreType.DMA((2,)),
+        ],
         compiler_params=PARAMS,
         name="spread",
         cost_estimate=cost(10_000_000, 1_000_000),

time: 157 us -> 156 us (level)
  transfers between devices with their start and end apart: 2 -> 2, of which waited for: 2 -> 2; matrix products, arithmetic and copies ran while one was open for 0% -> 0% of each run, Pallas kernels for 12% -> 13%
where the time goes in v9:
time: 156 us; the launch traced here: 155 us
  blocking collectives  103 us (66%)
  Pallas kernels  32.5 us (21%)
  starting transfers between devices  10.2 us (7%)
  waiting for transfers between devices  8.69 us (6%)
    all_to_all x4, blocking collectives, exchange(): return lax.all_to_all(pieces, axis, 0, 0)  103 us
    pallas_call x1, Pallas kernels, body(): pl.pallas_call(lambda *refs: invert_kernel(rows, cols, *refs), out_shape=...  12.5 us
    all_to_all x2, starting transfers between devices, exchange(): return lax.all_to_all(pieces, axis, 0, 0)  10.2 us
    all_to_all x2, waiting for transfers between devices, exchange(): return lax.all_to_all(pieces, axis, 0, 0)  8.69 us
    pallas_call x1, Pallas kernels, body(): pl.pallas_call(lambda *refs: factor_kernel(rows, fold, slim, step, *refs)...  7.01 us
    pallas_call x1, Pallas kernels, body(): pl.pallas_call(lambda *refs: product_kernel(col_blocks, fold, slim, *refs...  3.67 us
    pallas_call x1, Pallas kernels, body(): pl.pallas_call(lambda *refs: update_kernel(col_blocks, fold, slim, *refs)...  3.23 us
  transfers between devices with their start and end apart: 2, of which 2 were waited for; matrix products, arithmetic and copies ran while one was open for 0% of the time, Pallas kernels for 13%

profile of v9, /device:TPU:1, one launch (start us, length us, event | category | flops | bytes accessed | tf_op | source)
XLA Modules:
  0.0 155.2 jit_solution(17897398889635263718)
XLA Ops:
  0.0 0.1 pad_add_fusion.refs_0_
  0.1 2.2 %prepare.1 = f32[32,40,128]{2,1,0:T(8,128)S(1)} custom-call(s32[2]{0:T(128)S(1)} %pad_add_fusion.refs_0_, f32[1024,4,128]{2,1,0:T(4,128)} %bitcast.11), custom_call_target="tpu_custom_call" | custom-call | flops 201326592 | bytes 3000000 | tf_op jit(solution)/shard_map/prepare/pallas_call | solution.py:340
  2.3 22.5 %all_to_all.30 = f32[32,40,128]{2,1,0:T(8,128)S(1)} all-to-all(f32[32,40,128]{2,1,0:T(8,128)S(1)} %prepare.1), channel_id=1, replica_groups=mesh['row'=16,'col'=32] {'col'}, dimensions={0} | all-to-all | bytes 1310720 | tf_op jit(solution)/shard_map/all_to_all | solution.py:311
  24.9 0.0 copy-start
  24.9 28.8 %all_to_all.31.refs_1_ = f32[16,40,128]{2,1,0:T(8,128)S(1)} all-to-all(f32[16,40,128]{2,1,0:T(8,128)S(1)} %broadcast_in_dim.8), channel_id=1, replica_groups=mesh['row'=16,'col'=32] {'row'}, dimensions={0} | all-to-all | bytes 655360 | tf_op jit(solution)/shard_map/all_to_all | solution.py:311
  53.7 0.6 relay.2
  54.3 26.1 %all_to_all.32.refs_1_.refs_0_ = f32[32,56,128]{2,1,0:T(8,128)S(1)} all-to-all(f32[32,56,128]{2,1,0:T(8,128)S(1)} %relay.2), channel_id=1, replica_groups=mesh['row'=16,'col'=32] {'col'}, dimensions={0} | all-to-all | bytes 1835008 | tf_op jit(solution)/shard_map/all_to_all | solution.py:311
  80.4 0.0 copy-done
  80.4 3.7 %product.1 = f32[32,40,128]{2,1,0:T(8,128)} custom-call(s32[2]{0:T(128)S(1)} %pad_add_fusion.refs_0_, f32[32,56,128]{2,1,0:T(8,128)S(1)} %all_to_all.32.refs_1_.refs_0_, f32[4096,128]{1,0:T(8,128)S(1)} %bitcast.12), custom_call_target="tpu_custom_call" | custom-call | flops 805306368 | bytes 4000000 | tf_op jit(solution)/shard_map/product/pallas_call | solution.py:355
  84.1 4.6 %all-to-all-start.3 = ((f32[32,40,128]{2,1,0:T(8,128)}), f32[32,40,128]{2,1,0:T(8,128)}, u32[]{:S(2)}, u32[]{:S(2)}) async-start(f32[32,40,128]{2,1,0:T(8,128)} %product.1), calls=%async_computation.3 | async-start | bytes 1310720 | tf_op jit(solution)/shard_map/all_to_all | solution.py:311
  88.7 7.0 %factor.1 = (f32[384,128]{1,0:T(8,128)}, f32[1536,128]{1,0:T(8,128)}) custom-call(f32[32,56,128]{2,1,0:T(8,128)S(1)} %all_to_all.32.refs_1_.refs_0_), custom_call_target="tpu_custom_call" | custom-call | flops 4000000000 | bytes 2000000 | tf_op jit(solution)/shard_map/factor/pallas_call | solution.py:370
  95.7 6.1 %all-to-all-done.3.refs_1_ = f32[32,40,128]{2,1,0:T(8,128)} async-done(((f32[32,40,128]{2,1,0:T(8,128)}), f32[32,40,128]{2,1,0:T(8,128)}, u32[]{:S(2)}, u32[]{:S(2)}) %all-to-all-start.3) | async-done | bytes 655392 | tf_op jit(solution)/shard_map/all_to_all | solution.py:311
  101.8 2.7 %spread.1 = f32[16,40,128]{2,1,0:T(8,128)} custom-call(s32[2]{0:T(128)S(1)} %pad_add_fusion.refs_0_, f32[32,40,128]{2,1,0:T(8,128)} %all-to-all-done.3.refs_1_, f32[40,128]{1,0:T(8,128)S(1)} %get-tuple-element.13.refs_2_, f32[384,128]{1,0:T(8,128)} %get-tuple-element.9.refs_3_.refs_1_), custom_call_target="tpu_custom_call" | custom-call | flops 10000000 | bytes 1000000 | tf_op jit(solution)/shard_map/spread/pallas_call | solution.py:385
  104.4 5.6 %all-to-all-start.4 = ((f32[16,40,128]{2,1,0:T(8,128)}), f32[16,40,128]{2,1,0:T(8,128)S(1)}, u32[]{:S(2)}, u32[]{:S(2)}) async-start(f32[16,40,128]{2,1,0:T(8,128)} %spread.1), calls=%async_computation.4 | async-start | bytes 655360 | tf_op jit(solution)/shard_map/all_to_all | solution.py:311
  110.0 12.5 %invert.1.refs_1_ = f32[1920,128]{1,0:T(8,128)S(1)} custom-call(s32[2]{0:T(128)S(1)} %pad_add_fusion.refs_0_, f32[384,128]{1,0:T(8,128)} %get-tuple-element.9.refs_3_.refs_1_, f32[1536,128]{1,0:T(8,128)} %get-tuple-element.10.refs_2_), custom_call_target="tpu_custom_call" | custom-call | flops 4000000000 | bytes 1000000 | tf_op jit(solution)/shard_map/invert/pallas_call | solution.py:400
  122.6 2.6 %all-to-all-done.4.refs_1_ = f32[16,40,128]{2,1,0:T(8,128)S(1)} async-done(((f32[16,40,128]{2,1,0:T(8,128)}), f32[16,40,128]{2,1,0:T(8,128)S(1)}, u32[]{:S(2)}, u32[]{:S(2)}) %all-to-all-start.4) | async-done | bytes 327712 | tf_op jit(solution)/shard_map/all_to_all | solution.py:311
  125.2 0.6 relay.3
  125.8 26.0 %all_to_all.33.refs_0_ = f32[32,56,128]{2,1,0:T(8,128)S(1)} all-to-all(f32[32,56,128]{2,1,0:T(8,128)S(1)} %relay.3), channel_id=1, replica_groups=mesh['row'=16,'col'=32] {'col'}, dimensions={0} | all-to-all | bytes 1835008 | tf_op jit(solution)/shard_map/all_to_all | solution.py:311
  151.8 3.2 %update.1 = f32[4096,128]{1,0:T(8,128)} custom-call(f32[32,56,128]{2,1,0:T(8,128)S(1)} %all_to_all.33.refs_0_, f32[1920,128]{1,0:T(8,128)S(1)} %invert.1.refs_1_, f32[4096,128]{1,0:T(8,128)S(1)} %bitcast.13), custom_call_target="tpu_custom_call" | custom-call | flops 1610612736 | bytes 6000000 | tf_op jit(solution)/shard_map/update/pallas_call | solution.py:417
  (2 shorter events, 0.0 us)
Async XLA Ops:
  24.9 55.5 %copy-start = (f32[8,1,128,4,1,128]{5,4,3,2,1,0:T(1,128)S(1)}, f32[8,1,128,4,1,128]{5,4,3,2,1,0:T(1,128)}, u32[]{:S(2)}) copy-start(f32[8,1,128,4,1,128]{5,4,3,2,1,0:T(1,128)} %param.1) | copy-start | bytes 6291460
  84.1 17.7 %all-to-all-start.3 = ((f32[32,40,128]{2,1,0:T(8,128)}), f32[32,40,128]{2,1,0:T(8,128)}, u32[]{:S(2)}, u32[]{:S(2)}) async-start(f32[32,40,128]{2,1,0:T(8,128)} %product.1), calls=%async_computation.3 | async-start | bytes 1310720 | tf_op jit(solution)/shard_map/all_to_all | solution.py:311
  104.4 20.8 %all-to-all-start.4 = ((f32[16,40,128]{2,1,0:T(8,128)}), f32[16,40,128]{2,1,0:T(8,128)S(1)}, u32[]{:S(2)}, u32[]{:S(2)}) async-start(f32[16,40,128]{2,1,0:T(8,128)} %spread.1), calls=%async_computation.4 | async-start | bytes 655360 | tf_op jit(solution)/shard_map/all_to_all | solution.py:311

commit v10 on v9

--- a/solution.py
+++ b/solution.py
@@ -133,20 +133,29 @@
     pack_ref[4 * NB + cols :, :] = y[NB:rows]
 
 
-def prepare_kernel(fold, slim, ids_ref, a_hbm, send_ref, panel_ref, sem):
+def prepare_kernel(fold, slim, ids_ref, a_hbm, send_ref, panel_ref, sems):
     rows, col_count = a_hbm.shape[0], send_ref.shape[0]
     share, step, per = fold * slim, NB // col_count, NB // slim
-    get_panel = pltpu.make_async_copy(a_hbm.at[:, 0, :], panel_ref, sem)
-    get_panel.start()
-    get_panel.wait()
-    panel = panel_ref[...]
-    first = jnp.where((ids_ref[0] == 0) & (ids_ref[1] == 0), 0.0, panel[:NB])
-    panel = jnp.concatenate([first, panel[NB:]], 0)
-    gram = mult(panel, panel, 0, 0)
-    lead = jnp.where(ids_ref[0] == 1, first, 0.0)
-    for m in range(rows // NB):
-        k, f = divmod(m, fold)
-        send_ref[k * per : (k + 1) * per, f * slim : (f + 1) * slim, :] = panel[m * NB : (m + 1) * NB].reshape(per, slim, NB)
+    parts = sems.shape[0]
+    size = rows // parts
+    copies = [
+        pltpu.make_async_copy(a_hbm.at[pl.ds(at * size, size), 0, :], panel_ref.at[pl.ds(at * size, size), :], sems.at[at])
+        for at in range(parts)
+    ]
+    for copy in copies:
+        copy.start()
+    gram = jnp.zeros((NB, NB), jnp.float32)
+    for at, copy in enumerate(copies):
+        copy.wait()
+        if at == 0:
+            panel_ref[:NB, :] = jnp.where((ids_ref[0] == 0) & (ids_ref[1] == 0), 0.0, panel_ref[:NB, :])
+        for m in range(at * size // NB, (at + 1) * size // NB):
+            k, f = divmod(m, fold)
+            block = panel_ref[m * NB : (m + 1) * NB, :]
+            send_ref[k * per : (k + 1) * per, f * slim : (f + 1) * slim, :] = block.reshape(per, slim, NB)
+        part = panel_ref[at * size : (at + 1) * size, :]
+        gram = gram + mult(part, part, 0, 0)
+    lead = jnp.where(ids_ref[0] == 1, panel_ref[:NB, :], 0.0)
     for c in range(col_count):
         send_ref[c, share : share + step, :] = gram[c * step : (c + 1) * step]
         send_ref[c, share + step : share + 2 * step, :] = lead[c * step : (c + 1) * step]
@@ -197,7 +206,7 @@
         panel.append(got_ref[k * per : (k + 1) * per, f * slim : (f + 1) * slim, :].reshape(NB, NB))
     put_share = pltpu.make_async_copy(send_ref.at[:, :share, :], send_hbm.at[:, :share, :], sems.at[0])
     put_share.start()
-    hold_ref[...] = mult(jnp.concatenate(panel, 0), part, 0, 0)
+    hold_ref[...] = mult_packed(jnp.concatenate(panel, 0).T, part)
     lead = jnp.where(ids_ref[0] == 1, part[:NB], 0.0)
     for c in range(col_count):
         send_ref[c, share : share + step, :] = hold_ref[c * step : (c + 1) * step, :]
@@ -237,7 +246,7 @@
     put_panel.wait()
 
 
-def spread_kernel(share, step, ids_ref, got_hbm, own_ref, state_hbm, send_ref, got_ref, state_ref, sems):
+def spread_kernel(share, step, ids_ref, got_hbm, own_ref, state_hbm, send_hbm, got_ref, state_ref, out_ref, sems):
     get_got = pltpu.make_async_copy(got_hbm, got_ref, sems.at[0])
     get_state = pltpu.make_async_copy(state_hbm.at[: 2 * NB, :], state_ref, sems.at[1])
     get_got.start()
@@ -250,8 +259,12 @@
     turned = mult(total, state_ref[:NB, :], 1, 1)
     rows = turned[:share] - own[:share] * line
     lead = jnp.where(ids_ref[0] == 1, turned[share + step :] - 0.5 * own[share + step :] * line, 0.0)
-    out = jnp.concatenate([rows, total[share : share + step], lead], 0)
-    send_ref[...] = jnp.broadcast_to(out[None], send_ref.shape)
+    out_ref[...] = jnp.concatenate([rows, total[share : share + step], lead], 0)
+    copies = [pltpu.make_async_copy(out_ref, send_hbm.at[at], sems.at[2 + at]) for at in range(send_hbm.shape[0])]
+    for copy in copies:
+        copy.start()
+    for copy in copies:
+        copy.wait()
 
 
 def halves(value):
@@ -342,7 +355,7 @@
         out_shape=shape(col_count, share + pad, NB),
         in_specs=[SMEM, HBM],
         out_specs=VMEM,
-        scratch_shapes=[pltpu.VMEM((rows, NB), jnp.float32), pltpu.SemaphoreType.DMA],
+        scratch_shapes=[pltpu.VMEM((rows, NB), jnp.float32), pltpu.SemaphoreType.DMA((min(4, row_blocks),))],
         compiler_params=PARAMS,
         name="prepare",
         cost_estimate=cost(2 * rows * NB * NB * 6, 3_000_000),
@@ -384,13 +397,14 @@
 
     send = pl.pallas_call(
         lambda *refs: spread_kernel(share, step, *refs),
-        out_shape=shape(row_count, share + pad, NB),
+        out_shape=hbm(row_count, share + pad, NB),
         in_specs=[SMEM, HBM, VMEM, HBM],
-        out_specs=VMEM,
+        out_specs=HBM,
         scratch_shapes=[
             pltpu.VMEM((col_count, share + pad, NB), jnp.float32),
             pltpu.VMEM((2 * NB, NB), jnp.float32),
-            pltpu.SemaphoreType.DMA((2,)),
+            pltpu.VMEM((share + pad, NB), jnp.float32),
+            pltpu.SemaphoreType.DMA((2 + row_count,)),
         ],
         compiler_params=PARAMS,
         name="spread",

time: 156 us -> 156 us (level)
  no operation moved by 1% of the time
where the time goes in v10:
time: 156 us; the launch traced here: 155 us
  blocking collectives  103 us (66%)
  Pallas kernels  32.8 us (21%)
  starting transfers between devices  10.2 us (7%)
  waiting for transfers between devices  8.69 us (6%)
    all_to_all x4, blocking collectives, exchange(): return lax.all_to_all(pieces, axis, 0, 0)  103 us
    pallas_call x1, Pallas kernels, body(): pl.pallas_call(lambda *refs: invert_kernel(rows, cols, *refs), out_shape=...  12.5 us
    all_to_all x2, starting transfers between devices, exchange(): return lax.all_to_all(pieces, axis, 0, 0)  10.2 us
    all_to_all x2, waiting for transfers between devices, exchange(): return lax.all_to_all(pieces, axis, 0, 0)  8.69 us
    pallas_call x1, Pallas kernels, body(): pl.pallas_call(lambda *refs: factor_kernel(rows, fold, slim, step, *refs)...  7.01 us
    pallas_call x1, Pallas kernels, body(): pl.pallas_call(lambda *refs: product_kernel(col_blocks, fold, slim, *refs...  3.4 us
    pallas_call x1, Pallas kernels, body(): pl.pallas_call(lambda *refs: update_kernel(col_blocks, fold, slim, *refs)...  3.23 us
  transfers between devices with their start and end apart: 2, of which 2 were waited for; matrix products, arithmetic and copies ran while one was open for 0% of the time, Pallas kernels for 13%

profile of v10, /device:TPU:1, one launch (start us, length us, event | category | flops | bytes accessed | tf_op | source)
XLA Modules:
  0.0 155.5 jit_solution(13165667361673237292)
XLA Ops:
  0.0 0.1 pad_add_fusion.refs_0_
  0.1 2.6 %prepare.1 = f32[32,40,128]{2,1,0:T(8,128)S(1)} custom-call(s32[2]{0:T(128)S(1)} %pad_add_fusion.refs_0_, f32[1024,4,128]{2,1,0:T(4,128)} %bitcast.11), custom_call_target="tpu_custom_call" | custom-call | flops 201326592 | bytes 3000000 | tf_op jit(solution)/shard_map/prepare/pallas_call | solution.py:353
  2.7 22.5 %all_to_all.30 = f32[32,40,128]{2,1,0:T(8,128)S(1)} all-to-all(f32[32,40,128]{2,1,0:T(8,128)S(1)} %prepare.1), channel_id=1, replica_groups=mesh['row'=16,'col'=32] {'col'}, dimensions={0} | all-to-all | bytes 1310720 | tf_op jit(solution)/shard_map/all_to_all | solution.py:324
  25.2 0.0 copy-start
  25.3 28.8 %all_to_all.31.refs_1_ = f32[16,40,128]{2,1,0:T(8,128)S(1)} all-to-all(f32[16,40,128]{2,1,0:T(8,128)S(1)} %broadcast_in_dim.8), channel_id=1, replica_groups=mesh['row'=16,'col'=32] {'row'}, dimensions={0} | all-to-all | bytes 655360 | tf_op jit(solution)/shard_map/all_to_all | solution.py:324
  54.1 0.6 relay.2
  54.7 26.1 %all_to_all.32.refs_1_.refs_0_ = f32[32,56,128]{2,1,0:T(8,128)S(1)} all-to-all(f32[32,56,128]{2,1,0:T(8,128)S(1)} %relay.2), channel_id=1, replica_groups=mesh['row'=16,'col'=32] {'col'}, dimensions={0} | all-to-all | bytes 1835008 | tf_op jit(solution)/shard_map/all_to_all | solution.py:324
  80.8 0.0 copy-done
  80.8 3.4 %product.1 = f32[32,40,128]{2,1,0:T(8,128)} custom-call(s32[2]{0:T(128)S(1)} %pad_add_fusion.refs_0_, f32[32,56,128]{2,1,0:T(8,128)S(1)} %all_to_all.32.refs_1_.refs_0_, f32[4096,128]{1,0:T(8,128)S(1)} %bitcast.12), custom_call_target="tpu_custom_call" | custom-call | flops 805306368 | bytes 4000000 | tf_op jit(solution)/shard_map/product/pallas_call | solution.py:368
  84.2 4.6 %all-to-all-start.3 = ((f32[32,40,128]{2,1,0:T(8,128)}), f32[32,40,128]{2,1,0:T(8,128)}, u32[]{:S(2)}, u32[]{:S(2)}) async-start(f32[32,40,128]{2,1,0:T(8,128)} %product.1), calls=%async_computation.3 | async-start | bytes 1310720 | tf_op jit(solution)/shard_map/all_to_all | solution.py:324
  88.8 7.0 %factor.1 = (f32[384,128]{1,0:T(8,128)}, f32[1536,128]{1,0:T(8,128)}) custom-call(f32[32,56,128]{2,1,0:T(8,128)S(1)} %all_to_all.32.refs_1_.refs_0_), custom_call_target="tpu_custom_call" | custom-call | flops 4000000000 | bytes 2000000 | tf_op jit(solution)/shard_map/factor/pallas_call | solution.py:383
  95.8 6.1 %all-to-all-done.3.refs_1_ = f32[32,40,128]{2,1,0:T(8,128)} async-done(((f32[32,40,128]{2,1,0:T(8,128)}), f32[32,40,128]{2,1,0:T(8,128)}, u32[]{:S(2)}, u32[]{:S(2)}) %all-to-all-start.3) | async-done | bytes 655392 | tf_op jit(solution)/shard_map/all_to_all | solution.py:324
  101.9 2.8 %spread.1 = f32[16,40,128]{2,1,0:T(8,128)} custom-call(s32[2]{0:T(128)S(1)} %pad_add_fusion.refs_0_, f32[32,40,128]{2,1,0:T(8,128)} %all-to-all-done.3.refs_1_, f32[40,128]{1,0:T(8,128)S(1)} %get-tuple-element.13.refs_2_, f32[384,128]{1,0:T(8,128)} %get-tuple-element.9.refs_3_.refs_1_), custom_call_target="tpu_custom_call" | custom-call | flops 10000000 | bytes 1000000 | tf_op jit(solution)/shard_map/spread/pallas_call | solution.py:398
  104.7 5.6 %all-to-all-start.4 = ((f32[16,40,128]{2,1,0:T(8,128)}), f32[16,40,128]{2,1,0:T(8,128)S(1)}, u32[]{:S(2)}, u32[]{:S(2)}) async-start(f32[16,40,128]{2,1,0:T(8,128)} %spread.1), calls=%async_computation.4 | async-start | bytes 655360 | tf_op jit(solution)/shard_map/all_to_all | solution.py:324
  110.3 12.5 %invert.1.refs_1_ = f32[1920,128]{1,0:T(8,128)S(1)} custom-call(s32[2]{0:T(128)S(1)} %pad_add_fusion.refs_0_, f32[384,128]{1,0:T(8,128)} %get-tuple-element.9.refs_3_.refs_1_, f32[1536,128]{1,0:T(8,128)} %get-tuple-element.10.refs_2_), custom_call_target="tpu_custom_call" | custom-call | flops 4000000000 | bytes 1000000 | tf_op jit(solution)/shard_map/invert/pallas_call | solution.py:414
  122.8 2.6 %all-to-all-done.4.refs_1_ = f32[16,40,128]{2,1,0:T(8,128)S(1)} async-done(((f32[16,40,128]{2,1,0:T(8,128)}), f32[16,40,128]{2,1,0:T(8,128)S(1)}, u32[]{:S(2)}, u32[]{:S(2)}) %all-to-all-start.4) | async-done | bytes 327712 | tf_op jit(solution)/shard_map/all_to_all | solution.py:324
  125.5 0.6 relay.3
  126.1 26.0 %all_to_all.33.refs_0_ = f32[32,56,128]{2,1,0:T(8,128)S(1)} all-to-all(f32[32,56,128]{2,1,0:T(8,128)S(1)} %relay.3), channel_id=1, replica_groups=mesh['row'=16,'col'=32] {'col'}, dimensions={0} | all-to-all | bytes 1835008 | tf_op jit(solution)/shard_map/all_to_all | solution.py:324
  152.1 3.2 %update.1 = f32[4096,128]{1,0:T(8,128)} custom-call(f32[32,56,128]{2,1,0:T(8,128)S(1)} %all_to_all.33.refs_0_, f32[1920,128]{1,0:T(8,128)S(1)} %invert.1.refs_1_, f32[4096,128]{1,0:T(8,128)S(1)} %bitcast.13), custom_call_target="tpu_custom_call" | custom-call | flops 1610612736 | bytes 6000000 | tf_op jit(solution)/shard_map/update/pallas_call | solution.py:431
  (2 shorter events, 0.0 us)
Async XLA Ops:
  25.2 55.5 %copy-start = (f32[8,1,128,4,1,128]{5,4,3,2,1,0:T(1,128)S(1)}, f32[8,1,128,4,1,128]{5,4,3,2,1,0:T(1,128)}, u32[]{:S(2)}) copy-start(f32[8,1,128,4,1,128]{5,4,3,2,1,0:T(1,128)} %param.1) | copy-start | bytes 6291460
  84.2 17.7 %all-to-all-start.3 = ((f32[32,40,128]{2,1,0:T(8,128)}), f32[32,40,128]{2,1,0:T(8,128)}, u32[]{:S(2)}, u32[]{:S(2)}) async-start(f32[32,40,128]{2,1,0:T(8,128)} %product.1), calls=%async_computation.3 | async-start | bytes 1310720 | tf_op jit(solution)/shard_map/all_to_all | solution.py:324
  104.7 20.8 %all-to-all-start.4 = ((f32[16,40,128]{2,1,0:T(8,128)}), f32[16,40,128]{2,1,0:T(8,128)S(1)}, u32[]{:S(2)}, u32[]{:S(2)}) async-start(f32[16,40,128]{2,1,0:T(8,128)} %spread.1), calls=%async_computation.4 | async-start | bytes 655360 | tf_op jit(solution)/shard_map/all_to_all | solution.py:324

commit v11 on v9

--- a/solution.py
+++ b/solution.py
@@ -142,7 +142,7 @@
     panel = panel_ref[...]
     first = jnp.where((ids_ref[0] == 0) & (ids_ref[1] == 0), 0.0, panel[:NB])
     panel = jnp.concatenate([first, panel[NB:]], 0)
-    gram = mult(panel, panel, 0, 0)
+    gram = mult_packed(panel.T, panel)
     lead = jnp.where(ids_ref[0] == 1, first, 0.0)
     for m in range(rows // NB):
         k, f = divmod(m, fold)
@@ -197,7 +197,7 @@
         panel.append(got_ref[k * per : (k + 1) * per, f * slim : (f + 1) * slim, :].reshape(NB, NB))
     put_share = pltpu.make_async_copy(send_ref.at[:, :share, :], send_hbm.at[:, :share, :], sems.at[0])
     put_share.start()
-    hold_ref[...] = mult(jnp.concatenate(panel, 0), part, 0, 0)
+    hold_ref[...] = mult_packed(jnp.concatenate(panel, 0).T, part)
     lead = jnp.where(ids_ref[0] == 1, part[:NB], 0.0)
     for c in range(col_count):
         send_ref[c, share : share + step, :] = hold_ref[c * step : (c + 1) * step, :]

time: 156 us -> 155 us (level)
  no operation moved by 1% of the time
where the time goes in v11:
time: 155 us
  blocking collectives  103 us (66%)
  Pallas kernels  32.1 us (21%)
  starting transfers between devices  10.2 us (7%)
  waiting for transfers between devices  8.69 us (6%)
    all_to_all x4, blocking collectives, exchange(): return lax.all_to_all(pieces, axis, 0, 0)  103 us
    pallas_call x1, Pallas kernels, body(): pl.pallas_call(lambda *refs: invert_kernel(rows, cols, *refs), out_shape=...  12.5 us
    all_to_all x2, starting transfers between devices, exchange(): return lax.all_to_all(pieces, axis, 0, 0)  10.2 us
    all_to_all x2, waiting for transfers between devices, exchange(): return lax.all_to_all(pieces, axis, 0, 0)  8.69 us
    pallas_call x1, Pallas kernels, body(): pl.pallas_call(lambda *refs: factor_kernel(rows, fold, slim, step, *refs)...  7.01 us
    pallas_call x1, Pallas kernels, body(): pl.pallas_call(lambda *refs: product_kernel(col_blocks, fold, slim, *refs...  3.4 us
    pallas_call x1, Pallas kernels, body(): pl.pallas_call(lambda *refs: update_kernel(col_blocks, fold, slim, *refs)...  3.23 us
  transfers between devices with their start and end apart: 2, of which 2 were waited for; matrix products, arithmetic and copies ran while one was open for 0% of the time, Pallas kernels for 13%

profile of v11, /device:TPU:1, one launch (start us, length us, event | category | flops | bytes accessed | tf_op | source)
XLA Modules:
  0.0 154.8 jit_solution(3459990368969312184)
XLA Ops:
  0.0 0.1 pad_add_fusion.refs_0_
  0.1 2.1 %prepare.1 = f32[32,40,128]{2,1,0:T(8,128)S(1)} custom-call(s32[2]{0:T(128)S(1)} %pad_add_fusion.refs_0_, f32[1024,4,128]{2,1,0:T(4,128)} %bitcast.11), custom_call_target="tpu_custom_call" | custom-call | flops 201326592 | bytes 3000000 | tf_op jit(solution)/shard_map/prepare/pallas_call | solution.py:340
  2.2 22.5 %all_to_all.30 = f32[32,40,128]{2,1,0:T(8,128)S(1)} all-to-all(f32[32,40,128]{2,1,0:T(8,128)S(1)} %prepare.1), channel_id=1, replica_groups=mesh['row'=16,'col'=32] {'col'}, dimensions={0} | all-to-all | bytes 1310720 | tf_op jit(solution)/shard_map/all_to_all | solution.py:311
  24.7 0.0 copy-start
  24.8 28.8 %all_to_all.31.refs_1_ = f32[16,40,128]{2,1,0:T(8,128)S(1)} all-to-all(f32[16,40,128]{2,1,0:T(8,128)S(1)} %broadcast_in_dim.8), channel_id=1, replica_groups=mesh['row'=16,'col'=32] {'row'}, dimensions={0} | all-to-all | bytes 655360 | tf_op jit(solution)/shard_map/all_to_all | solution.py:311
  53.6 0.6 relay.2
  54.2 26.1 %all_to_all.32.refs_1_.refs_0_ = f32[32,56,128]{2,1,0:T(8,128)S(1)} all-to-all(f32[32,56,128]{2,1,0:T(8,128)S(1)} %relay.2), channel_id=1, replica_groups=mesh['row'=16,'col'=32] {'col'}, dimensions={0} | all-to-all | bytes 1835008 | tf_op jit(solution)/shard_map/all_to_all | solution.py:311
  80.2 0.0 copy-done
  80.2 3.4 %product.1 = f32[32,40,128]{2,1,0:T(8,128)} custom-call(s32[2]{0:T(128)S(1)} %pad_add_fusion.refs_0_, f32[32,56,128]{2,1,0:T(8,128)S(1)} %all_to_all.32.refs_1_.refs_0_, f32[4096,128]{1,0:T(8,128)S(1)} %bitcast.12), custom_call_target="tpu_custom_call" | custom-call | flops 805306368 | bytes 4000000 | tf_op jit(solution)/shard_map/product/pallas_call | solution.py:355
  83.7 4.6 %all-to-all-start.3 = ((f32[32,40,128]{2,1,0:T(8,128)}), f32[32,40,128]{2,1,0:T(8,128)}, u32[]{:S(2)}, u32[]{:S(2)}) async-start(f32[32,40,128]{2,1,0:T(8,128)} %product.1), calls=%async_computation.3 | async-start | bytes 1310720 | tf_op jit(solution)/shard_map/all_to_all | solution.py:311
  88.3 7.0 %factor.1 = (f32[384,128]{1,0:T(8,128)}, f32[1536,128]{1,0:T(8,128)}) custom-call(f32[32,56,128]{2,1,0:T(8,128)S(1)} %all_to_all.32.refs_1_.refs_0_), custom_call_target="tpu_custom_call" | custom-call | flops 4000000000 | bytes 2000000 | tf_op jit(solution)/shard_map/factor/pallas_call | solution.py:370
  95.3 6.1 %all-to-all-done.3.refs_1_ = f32[32,40,128]{2,1,0:T(8,128)} async-done(((f32[32,40,128]{2,1,0:T(8,128)}), f32[32,40,128]{2,1,0:T(8,128)}, u32[]{:S(2)}, u32[]{:S(2)}) %all-to-all-start.3) | async-done | bytes 655392 | tf_op jit(solution)/shard_map/all_to_all | solution.py:311
  101.4 2.7 %spread.1 = f32[16,40,128]{2,1,0:T(8,128)} custom-call(s32[2]{0:T(128)S(1)} %pad_add_fusion.refs_0_, f32[32,40,128]{2,1,0:T(8,128)} %all-to-all-done.3.refs_1_, f32[40,128]{1,0:T(8,128)S(1)} %get-tuple-element.13.refs_2_, f32[384,128]{1,0:T(8,128)} %get-tuple-element.9.refs_3_.refs_1_), custom_call_target="tpu_custom_call" | custom-call | flops 10000000 | bytes 1000000 | tf_op jit(solution)/shard_map/spread/pallas_call | solution.py:385
  104.0 5.6 %all-to-all-start.4 = ((f32[16,40,128]{2,1,0:T(8,128)}), f32[16,40,128]{2,1,0:T(8,128)S(1)}, u32[]{:S(2)}, u32[]{:S(2)}) async-start(f32[16,40,128]{2,1,0:T(8,128)} %spread.1), calls=%async_computation.4 | async-start | bytes 655360 | tf_op jit(solution)/shard_map/all_to_all | solution.py:311
  109.6 12.5 %invert.1.refs_1_ = f32[1920,128]{1,0:T(8,128)S(1)} custom-call(s32[2]{0:T(128)S(1)} %pad_add_fusion.refs_0_, f32[384,128]{1,0:T(8,128)} %get-tuple-element.9.refs_3_.refs_1_, f32[1536,128]{1,0:T(8,128)} %get-tuple-element.10.refs_2_), custom_call_target="tpu_custom_call" | custom-call | flops 4000000000 | bytes 1000000 | tf_op jit(solution)/shard_map/invert/pallas_call | solution.py:400
  122.2 2.6 %all-to-all-done.4.refs_1_ = f32[16,40,128]{2,1,0:T(8,128)S(1)} async-done(((f32[16,40,128]{2,1,0:T(8,128)}), f32[16,40,128]{2,1,0:T(8,128)S(1)}, u32[]{:S(2)}, u32[]{:S(2)}) %all-to-all-start.4) | async-done | bytes 327712 | tf_op jit(solution)/shard_map/all_to_all | solution.py:311
  124.8 0.6 relay.3
  125.4 26.0 %all_to_all.33.refs_0_ = f32[32,56,128]{2,1,0:T(8,128)S(1)} all-to-all(f32[32,56,128]{2,1,0:T(8,128)S(1)} %relay.3), channel_id=1, replica_groups=mesh['row'=16,'col'=32] {'col'}, dimensions={0} | all-to-all | bytes 1835008 | tf_op jit(solution)/shard_map/all_to_all | solution.py:311
  151.4 3.2 %update.1 = f32[4096,128]{1,0:T(8,128)} custom-call(f32[32,56,128]{2,1,0:T(8,128)S(1)} %all_to_all.33.refs_0_, f32[1920,128]{1,0:T(8,128)S(1)} %invert.1.refs_1_, f32[4096,128]{1,0:T(8,128)S(1)} %bitcast.13), custom_call_target="tpu_custom_call" | custom-call | flops 1610612736 | bytes 6000000 | tf_op jit(solution)/shard_map/update/pallas_call | solution.py:417
  (2 shorter events, 0.0 us)
Async XLA Ops:
  24.7 55.5 %copy-start = (f32[8,1,128,4,1,128]{5,4,3,2,1,0:T(1,128)S(1)}, f32[8,1,128,4,1,128]{5,4,3,2,1,0:T(1,128)}, u32[]{:S(2)}) copy-start(f32[8,1,128,4,1,128]{5,4,3,2,1,0:T(1,128)} %param.1) | copy-start | bytes 6291460
  83.7 17.7 %all-to-all-start.3 = ((f32[32,40,128]{2,1,0:T(8,128)}), f32[32,40,128]{2,1,0:T(8,128)}, u32[]{:S(2)}, u32[]{:S(2)}) async-start(f32[32,40,128]{2,1,0:T(8,128)} %product.1), calls=%async_computation.3 | async-start | bytes 1310720 | tf_op jit(solution)/shard_map/all_to_all | solution.py:311
  104.0 20.8 %all-to-all-start.4 = ((f32[16,40,128]{2,1,0:T(8,128)}), f32[16,40,128]{2,1,0:T(8,128)S(1)}, u32[]{:S(2)}, u32[]{:S(2)}) async-start(f32[16,40,128]{2,1,0:T(8,128)} %spread.1), calls=%async_computation.4 | async-start | bytes 655360 | tf_op jit(solution)/shard_map/all_to_all | solution.py:311

commit v12 on v11

--- a/solution.py
+++ b/solution.py
@@ -282,7 +282,7 @@
     coupling, inverse, v = pack_ref[:NB, :], pack_ref[NB : 2 * NB, :], pack_ref[3 * NB : 3 * NB + cols, :]
     y_ref = pack_ref.at[3 * NB + cols :, :]
     cross = jnp.sum(pack_ref[2 * NB : 3 * NB, :], axis=1, keepdims=True) * lead_ref[...]
-    middle = mult(mult(inverse, hold_ref[...]), inverse, 1, 1) - cross - cross.T
+    middle = mult_packed(mult_packed(inverse, hold_ref[...]), inverse.T) - cross - cross.T
     z_cols = got_ref[:, share : share + slim, :].reshape(cols, NB)
     u = mult_halves(z_cols - mult_halves(v, middle, 0), coupling, 1)
     for at, part in enumerate((u, v)):

time: 155 us -> 155 us (level)
  no operation moved by 1% of the time
where the time goes in v12:
time: 155 us; the launch traced here: 154 us
  blocking collectives  103 us (66%)
  Pallas kernels  31.8 us (21%)
  starting transfers between devices  10.2 us (7%)
  waiting for transfers between devices  8.69 us (6%)
    all_to_all x4, blocking collectives, exchange(): return lax.all_to_all(pieces, axis, 0, 0)  103 us
    pallas_call x1, Pallas kernels, body(): pl.pallas_call(lambda *refs: invert_kernel(rows, cols, *refs), out_shape=...  12.5 us
    all_to_all x2, starting transfers between devices, exchange(): return lax.all_to_all(pieces, axis, 0, 0)  10.2 us
    all_to_all x2, waiting for transfers between devices, exchange(): return lax.all_to_all(pieces, axis, 0, 0)  8.69 us
    pallas_call x1, Pallas kernels, body(): pl.pallas_call(lambda *refs: factor_kernel(rows, fold, slim, step, *refs)...  7.01 us
    pallas_call x1, Pallas kernels, body(): pl.pallas_call(lambda *refs: product_kernel(col_blocks, fold, slim, *refs...  3.4 us
  transfers between devices with their start and end apart: 2, of which 2 were waited for; matrix products, arithmetic and copies ran while one was open for 0% of the time, Pallas kernels for 13%

profile of v12, /device:TPU:1, one launch (start us, length us, event | category | flops | bytes accessed | tf_op | source)
XLA Modules:
  0.0 154.4 jit_solution(9769163762761745391)
XLA Ops:
  0.0 0.1 pad_add_fusion.refs_0_
  0.1 2.1 %prepare.1 = f32[32,40,128]{2,1,0:T(8,128)S(1)} custom-call(s32[2]{0:T(128)S(1)} %pad_add_fusion.refs_0_, f32[1024,4,128]{2,1,0:T(4,128)} %bitcast.11), custom_call_target="tpu_custom_call" | custom-call | flops 201326592 | bytes 3000000 | tf_op jit(solution)/shard_map/prepare/pallas_call | solution.py:340
  2.2 22.5 %all_to_all.30 = f32[32,40,128]{2,1,0:T(8,128)S(1)} all-to-all(f32[32,40,128]{2,1,0:T(8,128)S(1)} %prepare.1), channel_id=1, replica_groups=mesh['row'=16,'col'=32] {'col'}, dimensions={0} | all-to-all | bytes 1310720 | tf_op jit(solution)/shard_map/all_to_all | solution.py:311
  24.7 0.0 copy-start
  24.8 28.8 %all_to_all.31.refs_1_ = f32[16,40,128]{2,1,0:T(8,128)S(1)} all-to-all(f32[16,40,128]{2,1,0:T(8,128)S(1)} %broadcast_in_dim.8), channel_id=1, replica_groups=mesh['row'=16,'col'=32] {'row'}, dimensions={0} | all-to-all | bytes 655360 | tf_op jit(solution)/shard_map/all_to_all | solution.py:311
  53.6 0.6 relay.2
  54.2 26.1 %all_to_all.32.refs_1_.refs_0_ = f32[32,56,128]{2,1,0:T(8,128)S(1)} all-to-all(f32[32,56,128]{2,1,0:T(8,128)S(1)} %relay.2), channel_id=1, replica_groups=mesh['row'=16,'col'=32] {'col'}, dimensions={0} | all-to-all | bytes 1835008 | tf_op jit(solution)/shard_map/all_to_all | solution.py:311
  80.2 0.0 copy-done
  80.2 3.4 %product.1 = f32[32,40,128]{2,1,0:T(8,128)} custom-call(s32[2]{0:T(128)S(1)} %pad_add_fusion.refs_0_, f32[32,56,128]{2,1,0:T(8,128)S(1)} %all_to_all.32.refs_1_.refs_0_, f32[4096,128]{1,0:T(8,128)S(1)} %bitcast.12), custom_call_target="tpu_custom_call" | custom-call | flops 805306368 | bytes 4000000 | tf_op jit(solution)/shard_map/product/pallas_call | solution.py:355
  83.7 4.6 %all-to-all-start.3 = ((f32[32,40,128]{2,1,0:T(8,128)}), f32[32,40,128]{2,1,0:T(8,128)}, u32[]{:S(2)}, u32[]{:S(2)}) async-start(f32[32,40,128]{2,1,0:T(8,128)} %product.1), calls=%async_computation.3 | async-start | bytes 1310720 | tf_op jit(solution)/shard_map/all_to_all | solution.py:311
  88.3 7.0 %factor.1 = (f32[384,128]{1,0:T(8,128)}, f32[1536,128]{1,0:T(8,128)}) custom-call(f32[32,56,128]{2,1,0:T(8,128)S(1)} %all_to_all.32.refs_1_.refs_0_), custom_call_target="tpu_custom_call" | custom-call | flops 4000000000 | bytes 2000000 | tf_op jit(solution)/shard_map/factor/pallas_call | solution.py:370
  95.3 6.1 %all-to-all-done.3.refs_1_ = f32[32,40,128]{2,1,0:T(8,128)} async-done(((f32[32,40,128]{2,1,0:T(8,128)}), f32[32,40,128]{2,1,0:T(8,128)}, u32[]{:S(2)}, u32[]{:S(2)}) %all-to-all-start.3) | async-done | bytes 655392 | tf_op jit(solution)/shard_map/all_to_all | solution.py:311
  101.4 2.7 %spread.1 = f32[16,40,128]{2,1,0:T(8,128)} custom-call(s32[2]{0:T(128)S(1)} %pad_add_fusion.refs_0_, f32[32,40,128]{2,1,0:T(8,128)} %all-to-all-done.3.refs_1_, f32[40,128]{1,0:T(8,128)S(1)} %get-tuple-element.13.refs_2_, f32[384,128]{1,0:T(8,128)} %get-tuple-element.9.refs_3_.refs_1_), custom_call_target="tpu_custom_call" | custom-call | flops 10000000 | bytes 1000000 | tf_op jit(solution)/shard_map/spread/pallas_call | solution.py:385
  104.0 5.6 %all-to-all-start.4 = ((f32[16,40,128]{2,1,0:T(8,128)}), f32[16,40,128]{2,1,0:T(8,128)S(1)}, u32[]{:S(2)}, u32[]{:S(2)}) async-start(f32[16,40,128]{2,1,0:T(8,128)} %spread.1), calls=%async_computation.4 | async-start | bytes 655360 | tf_op jit(solution)/shard_map/all_to_all | solution.py:311
  109.6 12.5 %invert.1.refs_1_ = f32[1920,128]{1,0:T(8,128)S(1)} custom-call(s32[2]{0:T(128)S(1)} %pad_add_fusion.refs_0_, f32[384,128]{1,0:T(8,128)} %get-tuple-element.9.refs_3_.refs_1_, f32[1536,128]{1,0:T(8,128)} %get-tuple-element.10.refs_2_), custom_call_target="tpu_custom_call" | custom-call | flops 4000000000 | bytes 1000000 | tf_op jit(solution)/shard_map/invert/pallas_call | solution.py:400
  122.2 2.6 %all-to-all-done.4.refs_1_ = f32[16,40,128]{2,1,0:T(8,128)S(1)} async-done(((f32[16,40,128]{2,1,0:T(8,128)}), f32[16,40,128]{2,1,0:T(8,128)S(1)}, u32[]{:S(2)}, u32[]{:S(2)}) %all-to-all-start.4) | async-done | bytes 327712 | tf_op jit(solution)/shard_map/all_to_all | solution.py:311
  124.8 0.6 relay.3
  125.4 26.0 %all_to_all.33.refs_0_ = f32[32,56,128]{2,1,0:T(8,128)S(1)} all-to-all(f32[32,56,128]{2,1,0:T(8,128)S(1)} %relay.3), channel_id=1, replica_groups=mesh['row'=16,'col'=32] {'col'}, dimensions={0} | all-to-all | bytes 1835008 | tf_op jit(solution)/shard_map/all_to_all | solution.py:311
  151.4 2.9 %update.1 = f32[4096,128]{1,0:T(8,128)} custom-call(f32[32,56,128]{2,1,0:T(8,128)S(1)} %all_to_all.33.refs_0_, f32[1920,128]{1,0:T(8,128)S(1)} %invert.1.refs_1_, f32[4096,128]{1,0:T(8,128)S(1)} %bitcast.13), custom_call_target="tpu_custom_call" | custom-call | flops 1610612736 | bytes 6000000 | tf_op jit(solution)/shard_map/update/pallas_call | solution.py:417
  (2 shorter events, 0.0 us)
Async XLA Ops:
  24.7 55.5 %copy-start = (f32[8,1,128,4,1,128]{5,4,3,2,1,0:T(1,128)S(1)}, f32[8,1,128,4,1,128]{5,4,3,2,1,0:T(1,128)}, u32[]{:S(2)}) copy-start(f32[8,1,128,4,1,128]{5,4,3,2,1,0:T(1,128)} %param.1) | copy-start | bytes 6291460
  83.7 17.7 %all-to-all-start.3 = ((f32[32,40,128]{2,1,0:T(8,128)}), f32[32,40,128]{2,1,0:T(8,128)}, u32[]{:S(2)}, u32[]{:S(2)}) async-start(f32[32,40,128]{2,1,0:T(8,128)} %product.1), calls=%async_computation.3 | async-start | bytes 1310720 | tf_op jit(solution)/shard_map/all_to_all | solution.py:311
  104.0 20.8 %all-to-all-start.4 = ((f32[16,40,128]{2,1,0:T(8,128)}), f32[16,40,128]{2,1,0:T(8,128)S(1)}, u32[]{:S(2)}, u32[]{:S(2)}) async-start(f32[16,40,128]{2,1,0:T(8,128)} %spread.1), calls=%async_computation.4 | async-start | bytes 655360 | tf_op jit(solution)/shard_map/all_to_all | solution.py:311
